TPU v7x, 256 devices: a whole 4x4x8 slice. The times are simulated.
256 devices in a mesh: prow: 64 (over z, y, core), pcol: 4 (over x).
Axes of the slice: x: 4, y: 4, z: 8, core: 2. Of those that a mesh axis runs over, the one named last changes fastest.
Arguments:
- matrix: bfloat16 [32768, 20480], P('prow', 'pcol')
- pivots: int32 [2, 256], replicated, may hold values from 0 to 32767, as said below
Outputs:
- factored: bfloat16 [32768, 20480], P('prow', 'pcol')
Inputs may be any that keep to these rules, and one draw needn't show every extreme that they name: `pivots`: each list holds 256 distinct row indices; no index appears in two lists. The rows k * 2 * 256 to (k + 1) * 2 * 256 - 1 hold at most 8 entries of one list, and some such k holds exactly 8 in every list. The pivot rows of each panel give its diagonal block a diagonal large enough, relative to its other entries, that the Newton-Schulz steps converge.
All inputs are finite; a program needn't handle non-finite values.
Results may differ from a plain program's by a relative error of at most 0.001.
Values may be sent and summed in bfloat16 or wider, within the bound.
No kernel may reach another device: no remote copies, remote signals or barrier semaphores. Data moves between devices by JAX's collectives and lax.ppermute only.
A program may use at most 64 MiB of HBM per device.

v0:
```python
import jax
import jax.numpy as jnp
from jax import lax
from jax.sharding import PartitionSpec as P

NB = 256
PANELS = 2
NEWTON = 3


def broadcast(array, axis, root):
    mine = lax.axis_index(axis) == root
    return lax.psum(jnp.where(mine, array, jnp.zeros_like(array)), axis)


def inverse(block):
    guess = jnp.diag(1.0 / jnp.diagonal(block))
    twice = 2.0 * jnp.eye(block.shape[0], dtype=jnp.float32)
    for step in range(NEWTON):
        inner = twice - jnp.dot(block, guess, precision=lax.Precision.HIGHEST)
        guess = jnp.dot(guess, inner, precision=lax.Precision.HIGHEST)
    return guess


def left_factor(block, current, active, panel):
    inv = inverse(block.astype(jnp.float32))
    left = jnp.dot(current[:, :NB].astype(jnp.float32), inv, precision=lax.Precision.HIGHEST)
    left = jnp.where(active[:, None], left, 0.0).astype(jnp.bfloat16)
    return broadcast(left, "pcol", panel)


def on_device(matrix, pivots):
    rows_dev, width = matrix.shape
    groups = lax.axis_size("prow")
    columns = lax.axis_size("pcol")
    cap = 2 * NB // groups
    myself = lax.axis_index("prow")
    column = lax.axis_index("pcol")
    first = myself * rows_dev
    own_rows = first + jnp.arange(rows_dev, dtype=jnp.int32)
    block_ids = jnp.arange(width, dtype=jnp.int32) // NB
    logical = block_ids * columns + column
    slot_ids = jnp.arange(cap, dtype=jnp.int32)
    order = jnp.arange(NB, dtype=jnp.int32)
    current = matrix
    for panel in range(PANELS):
        chosen = pivots[panel]
        earlier = pivots[: panel + 1].reshape(-1)
        active = jnp.logical_not(jnp.any(own_rows[:, None] == earlier[None, :], axis=1))
        later = logical > panel
        owner = chosen // rows_dev
        before = (owner[:, None] == owner[None, :]) & (order[None, :] < order[:, None])
        rank = jnp.sum(before.astype(jnp.int32), axis=1)
        target = owner * cap + rank
        match = (owner[None, :] == myself) & (rank[None, :] == slot_ids[:, None])
        local_rows = jnp.sum(jnp.where(match, chosen[None, :] - first, 0), axis=1)
        filled = jnp.any(match, axis=1)
        packed = jnp.where(
            filled[:, None], jnp.take(current, local_rows, axis=0), jnp.zeros((), jnp.bfloat16)
        )
        gathered = lax.all_gather(packed, "prow", axis=0, tiled=True)
        upper = jnp.take(gathered, target, axis=0)
        left = left_factor(upper[:, :NB], current, active, panel)
        product = jnp.dot(left, upper, preferred_element_type=jnp.float32)
        fresh = (current.astype(jnp.float32) - product).astype(jnp.bfloat16)
        current = jnp.where(active[:, None] & later[None, :], fresh, current)
        placed = jnp.where(active[:, None] & (column == panel), left, current[:, :NB])
        current = current.at[:, :NB].set(placed)
    return current


def solution(mesh):
    return jax.shard_map(
        on_device,
        mesh=mesh,
        in_specs=(P("prow", "pcol"), P()),
        out_specs=P("prow", "pcol"),
        check_vma=False,
    )
```

profile of v0, /device:TPU:1, one launch (start us, length us, event | category | flops | bytes accessed | tf_op | source)
XLA Modules:
  0.0 353.2 jit_solution(8359108372499193858)
XLA Ops:
  6.5 0.8 compare_reduce_fusion.2
  7.3 0.8 fusion.45
  8.9 3.8 %gather_fusion.2 = bf16[8,5120]{1,0:T(8,128)(2,1)S(1)} fusion(bf16[512,5120]{1,0:T(8,128)(2,1)} %param.10, s32[1024]{0:T(1024)S(1)} %pad_clamp_fusion.3), kind=kCustom, calls=%fused_computation.clone | custom fusion | bytes 163872 | tf_op jit(solution)/shard_map/jit(_take)/gather | solution.py:59
  12.7 0.7 select_select_fusion.3
  13.8 83.9 %all-gather.3.cloned.1.call-done = bf16[512,5120]{1,0:T(8,128)(2,1)} async-done(((bf16[8,5120]{1,0:T(8,128)(2,1)}), bf16[512,5120]{1,0:T(8,128)(2,1)}) %all-gather.3.cloned.1.call-update) | async-done | bytes 5242896 | tf_op jit(solution)/shard_map/all_gather | solution.py:61
  97.8 7.8 %gather_fusion.3 = bf16[256,5120]{1,0:T(8,128)(2,1)S(1)} fusion(bf16[512,5120]{1,0:T(8,128)(2,1)} %all-gather.3.cloned.1.call-done, s32[1024]{0:T(1024)S(1)} %pad_clamp_fusion.2), kind=kCustom, calls=%fused_computation.1.clone | custom fusion | bytes 5243904 | tf_op jit(solution)/shard_map/jit(_take)/gather | solution.py:62
  106.0 1.5 copy-done.1
  107.5 2.3 gather_fusion
  109.9 1.3 convolution_subtract_fusion.5
  111.5 1.2 convolution_subtract_fusion.4
  113.9 2.3 fusion.4
  116.5 7.9 %copy.17 = bf16[512,5120]{0,1:T(8,128)(2,1)} copy(bf16[512,5120]{1,0:T(8,128)(2,1)} %param.10) | data formatting | bytes 10485760 | tf_op args[0]
  124.4 0.6 compare_reduce_fusion.4
  125.2 32.4 %all-reduce.3.cloned.1.call-done = bf16[512,256]{0,1:T(8,128)(2,1)} async-done(((bf16[512,256]{0,1:T(8,128)(2,1)}), bf16[512,256]{0,1:T(8,128)(2,1)}) %all-reduce.3.cloned.1.call-update) | async-done | bytes 262160 | tf_op jit(solution)/shard_map/psum | solution.py:13
  157.5 7.8 %and_select_fusion = bf16[512,5120]{0,1:T(8,128)(2,1)S(1)} fusion(bf16[512,5120]{0,1:T(8,128)(2,1)} %copy.17, bf16[512,256]{0,1:T(8,128)(2,1)} %all-reduce.3.cloned.1.call-done, bf16[256,5120]{1,0:T(8,128)(2,1)S(1)} %copy-done.2, pred[512]{0:T(512)(128)(4,1)S(1)} %get-tuple-element.48, pred[5120]{0:T(1024)(128)(4,1)S(1)} %fusion.34), kind=kOutput, calls=%fused_computation.8 | convolution fusion | flops 1355284480 | bytes 13374976 | tf_op jit(solution)/shard_map/dot_general | solution.py:64
  165.3 2.4 copy.29
  167.7 1.5 copy-done
  169.2 2.3 fusion.29
  171.5 7.9 %copy.20 = bf16[512,5120]{1,0:T(8,128)(2,1)} copy(bf16[512,5120]{0,1:T(8,128)(2,1)} %fusion.29) | data formatting | bytes 10485760 | tf_op jit(solution)/shard_map/scatter | solution.py:68
  179.4 3.8 %gather_fusion.4 = bf16[8,5120]{1,0:T(8,128)(2,1)S(1)} fusion(bf16[512,5120]{1,0:T(8,128)(2,1)} %copy.20, s32[1024]{0:T(1024)S(1)} %pad_clamp_fusion.1), kind=kCustom, calls=%fused_computation.2.clone | custom fusion | bytes 163872 | tf_op jit(solution)/shard_map/jit(_take)/gather | solution.py:59
  183.2 0.7 select_select_fusion.2
  184.3 82.8 %all-gather.5.cloned.1.call-done = bf16[512,5120]{1,0:T(8,128)(2,1)} async-done(((bf16[8,5120]{1,0:T(8,128)(2,1)}), bf16[512,5120]{1,0:T(8,128)(2,1)}) %all-gather.5.cloned.1.call-update) | async-done | bytes 5242896 | tf_op jit(solution)/shard_map/all_gather | solution.py:61
  267.1 7.8 %gather_fusion.5 = bf16[256,5120]{1,0:T(8,128)(2,1)S(1)} fusion(bf16[512,5120]{1,0:T(8,128)(2,1)} %all-gather.5.cloned.1.call-done, s32[1024]{0:T(1024)S(1)} %pad_clamp_fusion), kind=kCustom, calls=%fused_computation.3.clone | custom fusion | bytes 5243904 | tf_op jit(solution)/shard_map/jit(_take)/gather | solution.py:62
  275.3 1.5 copy-done.3
  276.8 2.3 gather_fusion.1
  279.2 1.3 convolution_subtract_fusion.2
  280.9 1.2 convolution_subtract_fusion.1
  283.2 2.7 fusion.2
  285.9 41.3 %all-reduce.5.cloned.1.call-done = bf16[512,256]{0,1:T(8,128)(2,1)} async-done(((bf16[512,256]{0,1:T(8,128)(2,1)}), bf16[512,256]{0,1:T(8,128)(2,1)}) %all-reduce.5.cloned.1.call-update) | async-done | bytes 262160 | tf_op jit(solution)/shard_map/psum | solution.py:13
  327.2 9.3 %and_select_fusion.1 = bf16[512,5120]{0,1:T(8,128)(2,1)} fusion(bf16[512,5120]{0,1:T(8,128)(2,1)} %fusion.29, bf16[512,256]{0,1:T(8,128)(2,1)} %all-reduce.5.cloned.1.call-done, bf16[256,5120]{1,0:T(8,128)(2,1)S(1)} %copy-done.4, pred[512]{0:T(512)(128)(4,1)S(1)} %get-tuple-element.46, pred[5120]{0:T(1024)(128)(4,1)S(1)} %fusion.35), kind=kOutput, calls=%fused_computation.9 | convolution fusion | flops 1355284480 | bytes 13374976 | tf_op jit(solution)/shard_map/dot_general | solution.py:64
  336.5 2.3 fusion.11
  338.8 7.9 %copy.23 = bf16[512,5120]{1,0:T(8,128)(2,1)} copy(bf16[512,5120]{0,1:T(8,128)(2,1)} %fusion.11) | data formatting | bytes 10485760 | tf_op jit(solution)/shard_map/scatter | solution.py:68
  (61 shorter events, 5.5 us)
Async XLA Ops:
  6.5 91.3 %all-gather.3.cloned.1.call-start = ((), (), s32[]{:S(2)}) async-start(), calls=%async_computation | async-start | bytes 5324800 | tf_op jit(solution)/shard_map/all_gather | solution.py:61
  13.5 144.0 %all-reduce.3.cloned.1.call-start = ((), (), s32[]{:S(2)}) async-start(), calls=%async_computation.1 | async-start | bytes 524288 | tf_op jit(solution)/shard_map/psum | solution.py:13
  106.0 1.5 copy-start.1
  107.5 5.7 %copy-start.2 = (bf16[256,5120]{1,0:T(8,128)(2,1)S(1)}, bf16[256,5120]{1,0:T(8,128)(2,1)}, u32[]{:S(2)}) copy-start(bf16[256,5120]{1,0:T(8,128)(2,1)} %copy-done.1) | copy-start | bytes 7864324
  116.2 150.9 %all-gather.5.cloned.1.call-start = ((), (), s32[]{:S(2)}) async-start(), calls=%async_computation.2 | async-start | bytes 5324800 | tf_op jit(solution)/shard_map/all_gather | solution.py:61
  165.3 3.9 %copy-start = (bf16[512,5120]{0,1:T(8,128)(2,1)}, bf16[512,5120]{0,1:T(8,128)(2,1)S(1)}, u32[]{:S(2)}) copy-start(bf16[512,5120]{0,1:T(8,128)(2,1)S(1)} %and_select_fusion) | copy-start | bytes 15728644
  165.3 3.9 %copy-start.5 = (bf16[512,256]{0,1:T(8,128)(2,1)S(1)}, bf16[512,256]{0,1:T(8,128)(2,1)}, u32[]{:S(2)}) copy-start(bf16[512,256]{0,1:T(8,128)(2,1)} %all-reduce.3.cloned.1.call-done) | copy-start | bytes 786436
  171.5 12.5 %copy-start.7 = (s32[2,256]{1,0:T(2,128)S(1)}, s32[2,256]{1,0:T(2,128)}, u32[]{:S(2)}) copy-start(s32[2,256]{1,0:T(2,128)} %param.11) | copy-start | bytes 6148
  183.9 143.2 %all-reduce.5.cloned.1.call-start = ((), (), s32[]{:S(2)}) async-start(), calls=%async_computation.3 | async-start | bytes 524288 | tf_op jit(solution)/shard_map/psum | solution.py:13
  275.3 1.5 copy-start.3
  276.8 5.7 %copy-start.4 = (bf16[256,5120]{1,0:T(8,128)(2,1)S(1)}, bf16[256,5120]{1,0:T(8,128)(2,1)}, u32[]{:S(2)}) copy-start(bf16[256,5120]{1,0:T(8,128)(2,1)} %copy-done.3) | copy-start | bytes 7864324
  327.2 9.3 %copy-start.6 = (bf16[512,256]{0,1:T(8,128)(2,1)S(1)}, bf16[512,256]{0,1:T(8,128)(2,1)}, u32[]{:S(2)}) copy-start(bf16[512,256]{0,1:T(8,128)(2,1)} %all-reduce.5.cloned.1.call-done) | copy-start | bytes 786436
Sparse Core Ops, SparseCore 0:
  13.6 84.1 all-gather.2
  116.3 41.1 all-reduce.2
  184.1 83.0 all-gather.4
  286.0 41.1 all-reduce.4
where the time goes:
time: 355 us; the launch traced here: 353 us
  waiting for transfers between devices  240 us (68%)
  local copies, waits for them, and re-layouts  58.6 us (17%)
  matrix products  29.9 us (8%)
  between operations  13.5 us (4%)
  other arithmetic  10.4 us (3%)
    all_gather x2, waiting for transfers between devices, on_device(): gathered = lax.all_gather(packed, 'prow', axis=0, tiled=True)  167 us
    psum x2, waiting for transfers between devices, broadcast(): return lax.psum(jnp.where(mine, array, jnp.zeros_like(array)), axis)  73.6 us
    dot_general x2, matrix products, on_device(): product = jnp.dot(left, upper, preferred_element_type=jnp.float32)  17.1 us
    scatter x2, local copies, waits for them, and re-layouts, on_device(): current = current.at[:, :NB].set(placed)  15.8 us
    gather x2, local copies, waits for them, and re-layouts, on_device(): upper = jnp.take(gathered, target, axis=0)  15.7 us
    unnamed x19, local copies, waits for them, and re-layouts  14.8 us
    gather x2, local copies, waits for them, and re-layouts, on_device(): jnp.take(current, local_rows, axis=0)  7.67 us
  transfers between devices with their start and end apart: 4, of which 4 were waited for; matrix products, arithmetic and copies ran while one was open for 3% of the time, Pallas kernels for 0%

commit v1 on v0

v1 whole, which is shorter than its diff:
```python
import functools
import jax
import jax.numpy as jnp
from jax import lax
from jax.experimental import pallas as pl
from jax.experimental.pallas import tpu as pltpu
from jax.sharding import PartitionSpec as P

NB = 256
NEWTON = 3
ZN, YN = 8, 4
CAP = 8
SLOTS = 2 * CAP
CHIP = 2 * SLOTS
WZ = 2560
F32 = jnp.float32
BF16 = jnp.bfloat16
VMEM = pl.BlockSpec(memory_space=pltpu.VMEM)
SMEM = pl.BlockSpec(memory_space=pltpu.SMEM)
ANY = pl.BlockSpec(memory_space=pl.ANY)
HBM = pl.BlockSpec(memory_space=pltpu.HBM)
PARAMS = pltpu.CompilerParams(vmem_limit_bytes=16 * 2**20)


def moves(dz, dy):
    pairs = []
    for z in range(ZN):
        for y in range(YN):
            for core in range(2):
                sign = 1 - 2 * core
                there = ((z + sign * dz) % ZN) * YN + (y + sign * dy) % YN
                pairs.append(((z * YN + y) * 2 + core, there * 2 + core))
    return pairs


ALONG_Z = moves(1, 0)
ALONG_Y = moves(0, 1)
TWICE_Y = moves(0, 2)
PAIR = [(i, i ^ 1) for i in range(2 * ZN * YN)]


NEAR = [(0, 1), (1, 0)]
FAR = [(0, 3), (1, 2)]
SKIP = [(0, 2), (1, 3)]
ACROSS = [(2, 3), (3, 2)]


def over(array, pairs):
    return lax.ppermute(array, "pcol", pairs)


def send(array, pairs):
    return lax.ppermute(array, "prow", pairs)


def after(array, *others):
    return lax.optimization_barrier((array, *others))[0]


def both(*arrays):
    return lax.optimization_barrier(arrays)


def iota(shape, dim):
    return lax.broadcasted_iota(jnp.int32, shape, dim)


def to_column(row):
    n = row.shape[1]
    eye = iota((n, n), 0) == iota((n, n), 1)
    return jnp.sum(jnp.where(eye, row, 0.0), axis=1, keepdims=True)


def slot_column(piv_row, rows_dev):
    n = piv_row.shape[1]
    owner_row = lax.div(piv_row, jnp.int32(rows_dev)).astype(F32)
    owner_col = to_column(owner_row)
    before = iota((n, n), 1) < iota((n, n), 0)
    rank = jnp.sum(jnp.where(before & (owner_row == owner_col), 1.0, 0.0), axis=1, keepdims=True)
    return owner_col * CAP + rank


def chip_slots(me, order):
    n = ZN * YN * SLOTS
    pos = iota((1, n), 1)
    block = pos // SLOTS
    chip = me // 2
    z, y = chip // YN, chip % YN
    sign = 2 * (me % 2) - 1
    if order == "z first":
        zz = (z - block % ZN) & (ZN - 1)
        yy = (y + sign * (block // ZN)) & (YN - 1)
    else:
        yy = (y - block % YN) & (YN - 1)
        zz = (z + sign * (block // YN)) & (ZN - 1)
    return ((zz * YN + yy) * SLOTS + pos % SLOTS).astype(F32)


def is_pivot(piv_row, me, rows_dev):
    local = piv_row - me * rows_dev
    hit = iota((rows_dev, piv_row.shape[1]), 0) == local
    return jnp.max(jnp.where(hit, 1.0, 0.0), axis=1, keepdims=True) > 0.5


def list_rows(blocks, which):
    parts = []
    for block in blocks:
        rows, width = block.shape
        chips = rows // CHIP
        parts.append(block.reshape(chips, 2, SLOTS, width)[:, which].reshape(chips * SLOTS, width))
    return jnp.concatenate(parts, axis=0) if len(parts) > 1 else parts[0]


def dot(a, b):
    return jnp.dot(a, b, preferred_element_type=F32)


def dot_high(a, b):
    return jnp.dot(a, b, precision=lax.Precision.HIGHEST, preferred_element_type=F32)


def pieces(b):
    high = b.astype(BF16)
    rest = b - high.astype(F32)
    middle = rest.astype(BF16)
    return high, middle, (rest - middle.astype(F32)).astype(BF16)


def dot_exact(a, parts):
    high, middle, low = parts
    return dot(a, high) + (dot(a, middle) + dot(a, low))


def pick_kernel(chunk, ids, piv_ref, a_hbm, out_ref, a_ref, sems):
    me = ids[0]
    chunks, rows_dev, _ = a_ref.shape

    def fetch(k):
        return pltpu.make_async_copy(
            a_hbm.at[:, pl.ds(k * chunk, chunk)], a_ref.at[k], sems.at[k]
        )

    for k in range(chunks):
        fetch(k).start()
    hots = []
    for which in range(2):
        piv_row = piv_ref[which : which + 1, :]
        n = piv_row.shape[1]
        owner_row = lax.div(piv_row, jnp.int32(rows_dev)).astype(F32)
        owner_col = to_column(owner_row)
        before = iota((n, n), 0) < iota((n, n), 1)
        rank = jnp.sum(jnp.where(before & (owner_row == owner_col), 1.0, 0.0), axis=0, keepdims=True)
        slot = rank + ((me % 2) * CAP).astype(F32)
        mine = owner_row == me.astype(F32)
        place = mine & (iota((SLOTS, n), 0).astype(F32) == slot)
        local = to_column((piv_row - me * rows_dev).astype(F32))
        row = local == iota((n, rows_dev), 1).astype(F32)
        hot = dot(jnp.where(place, 1.0, 0.0).astype(BF16), jnp.where(row, 1.0, 0.0).astype(BF16))
        hots.append(hot)
    hot = jnp.concatenate(hots, axis=0).astype(BF16)
    for k in range(chunks):
        fetch(k).wait()
        out_ref[:, k * chunk : (k + 1) * chunk] = dot(hot, a_ref[k]).astype(BF16)


def pick(ids, pivots, matrix):
    rows_dev, width = matrix.shape
    chunk = 1024
    chunks = width // chunk
    return pl.pallas_call(
        functools.partial(pick_kernel, chunk),
        in_specs=[SMEM, VMEM, HBM],
        out_specs=VMEM,
        out_shape=jax.ShapeDtypeStruct((CHIP, width), BF16),
        scratch_shapes=[
            pltpu.VMEM((chunks, rows_dev, chunk), BF16),
            pltpu.SemaphoreType.DMA((chunks,)),
        ],
        compiler_params=PARAMS,
        cost_estimate=pl.CostEstimate(
            flops=2 * CHIP * rows_dev * width, bytes_accessed=4 * rows_dev * width, transcendentals=0
        ),
        name="pick",
    )(ids, pivots, pltpu.with_memory_space_constraint(matrix, pltpu.HBM))


def maps_kernel(rows_dev, ids, piv_ref, *out_refs):
    me = ids[0]
    for which in range(2):
        slots = slot_column(piv_ref[which : which + 1, :], rows_dev)
        rows = slice(which * NB, (which + 1) * NB)
        for order, out in zip(("z first", "y first"), out_refs):
            out[rows, :] = jnp.where(slots == chip_slots(me, order), 1.0, 0.0).astype(BF16)


def maps(ids, pivots, rows_dev):
    shape = jax.ShapeDtypeStruct((2 * NB, ZN * YN * SLOTS), BF16)
    return pl.pallas_call(
        functools.partial(maps_kernel, rows_dev),
        in_specs=[SMEM, VMEM],
        out_specs=[VMEM] * 2,
        out_shape=[shape] * 2,
        cost_estimate=pl.CostEstimate(flops=2**30, bytes_accessed=2**22, transcendentals=0),
        name="maps",
    )(ids, pivots)


def inverse(block):
    n = block.shape[0]
    wide = block.astype(F32)
    eye = iota((n, n), 0) == iota((n, n), 1)
    diagonal_row = jnp.sum(jnp.where(eye, wide, 0.0), axis=0, keepdims=True)
    diagonal_col = jnp.sum(jnp.where(eye, wide, 0.0), axis=1, keepdims=True)
    twice = jnp.where(eye, 2.0, 0.0)
    guess = (1.0 / diagonal_col) * (twice - wide * (1.0 / diagonal_row))
    for step in range(NEWTON - 1):
        inner = twice - dot_exact(block, pieces(guess))
        guess = dot_high(guess, inner)
    return guess


def factor_kernel(ids, piv_ref, s0_ref, s1_ref, pan0_ref, pan1_ref, l0_ref, l1_ref, lp_ref, fin_ref):
    me, col = ids[0], ids[1]
    rows_dev = pan0_ref.shape[0]
    upper01 = s1_ref[:NB, :]
    inv0 = pieces(inverse(s0_ref[:NB, :]))
    lower = dot_exact(s0_ref[NB:, :], inv0).astype(BF16)
    lp_ref[...] = lower
    block1 = (s1_ref[NB:, :].astype(F32) - dot(lower, upper01)).astype(BF16)
    inv1 = pieces(inverse(block1))
    live0 = jnp.logical_not(is_pivot(piv_ref[0:1, :], me, rows_dev))
    live1 = live0 & jnp.logical_not(is_pivot(piv_ref[1:2, :], me, rows_dev))
    pan0 = pan0_ref[...]
    left0 = jnp.where(live0, dot_exact(pan0, inv0), 0.0).astype(BF16)
    l0_ref[...] = left0
    pan1 = (pan1_ref[...].astype(F32) - dot(left0, upper01)).astype(BF16)
    left1 = jnp.where(live1, dot_exact(pan1, inv1), 0.0).astype(BF16)
    l1_ref[...] = left1
    fin0 = jnp.where(live0, left0.astype(F32), pan0.astype(F32))
    fin1 = jnp.where(live1, left1.astype(F32), pan1.astype(F32))
    fin_ref[...] = jnp.where(col == 0, fin0, fin1).astype(BF16)


def factor(ids, pivots, uppers, pan0, pan1):
    rows_dev = pan0.shape[0]
    left = jax.ShapeDtypeStruct((rows_dev, NB), BF16)
    return pl.pallas_call(
        factor_kernel,
        in_specs=[SMEM] + [VMEM] * 5,
        out_specs=[VMEM] * 4,
        out_shape=[left, left, jax.ShapeDtypeStruct((NB, NB), BF16), left],
        compiler_params=PARAMS,
        cost_estimate=pl.CostEstimate(
            flops=2 * 3 * 64 * NB**3, bytes_accessed=4 * 2**20, transcendentals=0
        ),
        name="factor",
    )(ids, pivots, *uppers, pan0, pan1)


def step_of(width):
    if width < 512:
        return width
    return 640 if width % 1280 == 0 else 512


def select_kernel(spans, hot_ref, *refs):
    blocks, (u0_ref, u1_ref) = refs[:-2], refs[-2:]
    width = u0_ref.shape[1]
    step = step_of(width)
    for at in range(0, width, step):
        cols = slice(at, at + step)
        parts = [block[:, cols] for block in blocks]
        for which, out in ((0, u0_ref), (1, u1_ref)):
            rows = slice(which * NB, (which + 1) * NB)
            hot = jnp.concatenate([hot_ref[rows, a:b] for a, b in spans], axis=1)
            out[:, cols] = dot(hot, list_rows(parts, which)).astype(BF16)


def select(hot, blocks, spans):
    width = blocks[0].shape[1]
    shape = jax.ShapeDtypeStruct((NB, width), BF16)
    slots = sum(b - a for a, b in spans)
    return pl.pallas_call(
        functools.partial(select_kernel, spans),
        in_specs=[VMEM] * (1 + len(blocks)),
        out_specs=[VMEM, VMEM],
        out_shape=[shape, shape],
        compiler_params=PARAMS,
        cost_estimate=pl.CostEstimate(
            flops=2 * 2 * NB * slots * width, bytes_accessed=2**20, transcendentals=0
        ),
        name="select",
    )(hot, *blocks)


def update_kernel(
    start, span, ids, hot_ref, u0_ref, u1_ref, mine_ref, other_ref, l0_ref, l1_ref, lp_ref, fin_ref,
    a_hbm, _, out_hbm, a_ref, out_ref, in_sems, out_sems,
):
    me, col = ids[0], ids[1]
    width = u0_ref.shape[1]
    half = width // 2
    step = step_of(width)
    steps = width // step

    def fetch(k):
        cols = pl.ds(start + k * step, step)
        return pltpu.make_async_copy(a_hbm.at[:, cols], a_ref.at[k], in_sems.at[k])

    def put(k):
        cols = pl.ds(start + k * step, step)
        return pltpu.make_async_copy(out_ref.at[k], out_hbm.at[:, cols], out_sems.at[k])

    for k in range(steps):
        fetch(k).start()
    for k in range(steps):
        at = k * step
        side = at // half
        cols = slice(at, at + step)
        near = slice(at - side * half, at - side * half + step)
        last = jnp.where(me % 2 == side, mine_ref[:, near], other_ref[:, near])
        u0 = u0_ref[:, cols].astype(F32) + dot(hot_ref[:NB, span], list_rows([last], 0))
        u0 = u0.astype(BF16)
        u1 = u1_ref[:, cols].astype(F32) + dot(hot_ref[NB:, span], list_rows([last], 1))
        u1 = (u1 - dot(lp_ref[...], u0)).astype(BF16)
        fetch(k).wait()
        a = (a_ref[k].astype(F32) - dot(l0_ref[...], u0)).astype(BF16)
        out_ref[k] = (a.astype(F32) - dot(l1_ref[...], u1)).astype(BF16)
        if start + at == 0:

            @pl.when(col < 2)
            def _():
                out_ref[k, :, :NB] = fin_ref[...]

        put(k).start()
    for k in range(steps):
        put(k).wait()


def update(ids, hot, span, uppers, mine, other, lefts, lower, fin, matrix, out, start):
    rows_dev, columns = matrix.shape
    width = uppers[0].shape[1]
    step = step_of(width)
    steps = width // step
    aliases = {}
    if out is None:
        out = jnp.zeros((16, 128), BF16)
    else:
        aliases = {11: 0}
    return pl.pallas_call(
        functools.partial(update_kernel, start, slice(*span)),
        in_specs=[SMEM] + [VMEM] * 9 + [ANY, ANY],
        out_specs=ANY,
        out_shape=jax.ShapeDtypeStruct((rows_dev, columns), BF16),
        scratch_shapes=[
            pltpu.VMEM((steps, rows_dev, step), BF16),
            pltpu.VMEM((steps, rows_dev, step), BF16),
            pltpu.SemaphoreType.DMA((steps,)),
            pltpu.SemaphoreType.DMA((steps,)),
        ],
        input_output_aliases=aliases,
        compiler_params=PARAMS,
        cost_estimate=pl.CostEstimate(
            flops=2 * width * NB * (2 * 128 + NB + 2 * rows_dev),
            bytes_accessed=4 * width * rows_dev,
            transcendentals=0,
        ),
        name="update",
    )(ids, hot, *uppers, mine, other, *lefts, lower, fin, matrix, out)


def on_device(matrix, pivots):
    rows_dev, width = matrix.shape
    me = lax.axis_index("prow")
    col = lax.axis_index("pcol")
    ids = jnp.stack([me, col]).astype(jnp.int32)
    even = me % 2 == 0

    def panels(array, near, far, across):
        zero = jnp.where(col == 0, array, jnp.where(col == 1, near, jnp.where(col == 3, far, across)))
        one = jnp.where(col == 1, array, jnp.where(col == 0, near, jnp.where(col == 2, far, across)))
        return zero, one

    def half(array):
        width = array.shape[1] // 2
        return jnp.where(even, array[:, :width], array[:, width:])

    packed = pick(ids, pivots, matrix)
    packed = packed + send(packed, PAIR)
    zb, yb = packed[:, :WZ], packed[:, WZ:]
    n = CHIP

    hot_z, hot_y = maps(ids, pivots, rows_dev)
    t1, r1, hot_z, hot_y = both(send(zb, ALONG_Z), send(yb, ALONG_Y), hot_z, hot_y)

    t2, r2, q1 = both(send(t1, ALONG_Z), send(r1, ALONG_Y), send(r1, PAIR))
    yf = jnp.concatenate([yb, jnp.where(even, r1, q1), r2, jnp.where(even, q1, r1)], axis=0)

    y1 = send(yf, ALONG_Z)
    t3 = send(t2, ALONG_Z)
    own = jnp.concatenate([t1, t2, t3], axis=0)
    t4, oth, y1 = both(send(t3, ALONG_Z), send(own, PAIR), y1)

    def z_blocks(cols):
        own_cols, oth_cols = own[:, cols], oth[:, cols]
        down, up = jnp.where(even, own_cols, oth_cols), jnp.where(even, oth_cols, own_cols)
        order = [zb[:, cols], down, t4[:, cols], up[2 * n :], up[n : 2 * n], up[:n]]
        return jnp.concatenate(order, axis=0)

    v0 = z_blocks(slice(0, NB))
    zf = z_blocks(slice(0, WZ))
    v1, v2 = both(send(v0, ALONG_Y), send(v0, TWICE_Y))
    z1 = send(after(zf, v1), ALONG_Y)
    w1 = send(v1, PAIR)
    k = ZN * SLOTS
    entries = select(hot_z, [v0, v1, v2, w1], [(i * k, (i + 1) * k) for i in range(4)])
    panel = after(matrix[:, :NB], v1)
    near, far = over(panel, NEAR), over(panel, FAR)
    y2, o1, near, far, *entries = both(
        send(y1, ALONG_Z), send(y1, PAIR), near, far, *entries
    )

    part = jnp.where(even, entries[0], entries[1])
    part = panels(part, over(part, NEAR), over(part, FAR), over(part, SKIP))
    part = jnp.concatenate(part, axis=1)
    across = over(far, ACROSS)
    y3, z1, o2, part, across = both(send(y2, ALONG_Z), z1, send(y2, PAIR), part, across)
    pan0, pan1 = panels(panel, near, far, across)

    rest = send(part, PAIR)
    uppers = jnp.concatenate([jnp.where(even, part, rest), jnp.where(even, rest, part)], axis=0)
    uppers = [uppers[:, :NB], uppers[:, NB:]]
    left0, left1, lower, fin = factor(ids, pivots, uppers, pan0, pan1)
    p1, o3 = send(z1, PAIR), send(y3, PAIR)
    uz = select(hot_z, [zf, z1, p1], [(0, k), (k, 2 * k), (3 * k, 4 * k)])
    n = YN * SLOTS
    spans = [(i * n, (i + 1) * n) for i in (0, 1, 2, 3, 5, 6, 7)]
    uy = select(hot_y, [yf, y1, y2, y3, o3, o2, o1], spans)
    z2, y4, left0, *us = both(
        send(half(z1), ALONG_Y), send(half(y3), ALONG_Z), left0, *uz, *uy
    )
    uz, uy = us[:2], us[2:]

    lefts = (left0, left1)
    p2, o4 = send(z2, PAIR), send(y4, PAIR)
    out = update(ids, hot_z, (2 * k, 3 * k), uz, z2, p2, lefts, lower, fin, matrix, None, 0)
    return update(ids, hot_y, (4 * n, 5 * n), uy, y4, o4, lefts, lower, fin, matrix, out, WZ)


def solution(mesh):
    return jax.shard_map(
        on_device,
        mesh=mesh,
        in_specs=(P("prow", "pcol"), P()),
        out_specs=P("prow", "pcol"),
        check_vma=False,
    )
```

time: 355 us -> 116 us (0.33)
  the two profiles are of different devices: /device:TPU:1 before, /device:TPU:7 now
where the time goes in v1:
time: 116 us
  starting transfers between devices  44.4 us (38%)
  waiting for transfers between devices  37 us (32%)
  Pallas kernels  27.5 us (24%)
  local copies, waits for them, and re-layouts  4.56 us (4%)
  other arithmetic  1.76 us (2%)
    ppermute x25, starting transfers between devices, send(): return lax.ppermute(array, 'prow', pairs)  36.2 us
    ppermute x6, waiting for transfers between devices, over(): return lax.ppermute(array, 'pcol', pairs)  22.1 us
    ppermute x25, waiting for transfers between devices, send(): return lax.ppermute(array, 'prow', pairs)  14.9 us
    pallas_call x2, Pallas kernels, update(): pl.pallas_call(functools.partial(update_kernel, start, slice(*span)), in_...  11.6 us
    ppermute x6, starting transfers between devices, over(): return lax.ppermute(array, 'pcol', pairs)  8.14 us
    pallas_call x1, Pallas kernels, factor(): pl.pallas_call(factor_kernel, in_specs=[SMEM] + [VMEM] * 5, out_specs=[VM...  5.26 us
    pallas_call x3, Pallas kernels, select(): pl.pallas_call(functools.partial(select_kernel, spans), in_specs=[VMEM] *...  5.18 us
    unnamed x48, local copies, waits for them, and re-layouts  3.56 us
  transfers between devices with their start and end apart: 31, of which 11 were waited for; matrix products, arithmetic and copies ran while one was open for 2% of the time, Pallas kernels for 16%

profile of v1, /device:TPU:7, one launch (start us, length us, event | category | flops | bytes accessed | tf_op | source)
XLA Modules:
  0.0 115.9 jit_solution(8278805473212610990)
XLA Ops:
  0.8 3.4 %pick.1 = bf16[32,5120]{1,0:T(8,128)(2,1)S(1)} custom-call(s32[2]{0:T(128)S(1)} %pad_add_fusion.ids, s32[2,256]{1,0:T(2,128)S(1)} %copy-done.10, bf16[512,5120]{1,0:T(8,128)(2,1)} %a_hbm.5), custom_call_target="tpu_custom_call" | custom-call | flops 167772160 | bytes 10485760 | tf_op jit(solution)/shard_map/pick/pallas_call | solution.py:170
  4.9 1.3 %collective-permute-done = bf16[32,5120]{1,0:T(8,128)(2,1)S(1)} collective-permute-done((bf16[32,5120]{1,0:T(8,128)(2,1)S(1)}, bf16[32,5120]{1,0:T(8,128)(2,1)S(1)}, u32[]{:S(2)}, u32[]{:S(2)}) %collective-permute-start) | collective-permute-done | bytes 327712 | tf_op jit(solution)/shard_map/ppermute | solution.py:53
  6.3 5.7 %collective-permute-start.1 = (bf16[32,2560]{1,0:T(8,128)(2,1)S(1)}, bf16[32,2560]{1,0:T(8,128)(2,1)S(1)}, u32[]{:S(2)}, u32[]{:S(2)}) collective-permute-start(bf16[32,2560]{1,0:T(8,128)(2,1)S(1)} %get-tuple-element.107), channel_id=1, source_target_pairs={{0,32},{4,228},{8,40},{12,236},{16,48},{20,244},{24,56},{28,252},{... | collective-permute-start | bytes 491528 | tf_op jit(solution)/shard_map/ppermute | solution.py:53
  12.0 2.7 %collective-permute-start.2 = (bf16[32,2560]{1,0:T(8,128)(2,1)S(1)}, bf16[32,2560]{1,0:T(8,128)(2,1)S(1)}, u32[]{:S(2)}, u32[]{:S(2)}) collective-permute-start(bf16[32,2560]{1,0:T(8,128)(2,1)S(1)} %get-tuple-element.106), channel_id=1, source_target_pairs={{0,8},{4,28},{8,16},{12,4},{16,24},{20,12},{24,0},{28,20},{32,40},... | collective-permute-start | bytes 491528 | tf_op jit(solution)/shard_map/ppermute | solution.py:53
  14.7 2.0 %maps.1 = (bf16[512,512]{1,0:T(8,128)(2,1)}, bf16[512,512]{1,0:T(8,128)(2,1)}) custom-call(s32[2]{0:T(128)} %copy-done.8, s32[2,256]{1,0:T(2,128)} %piv_ref.5), custom_call_target="tpu_custom_call" | custom-call | flops 1073741824 | bytes 4194304 | tf_op jit(solution)/shard_map/maps/pallas_call | solution.py:198
  17.0 3.1 %collective-permute-start.4 = (bf16[32,2560]{1,0:T(8,128)(2,1)S(1)}, bf16[32,2560]{1,0:T(8,128)(2,1)S(1)}, u32[]{:S(2)}, u32[]{:S(2)}) collective-permute-start(bf16[32,2560]{1,0:T(8,128)(2,1)S(1)} %collective-permute-done.2), channel_id=1, source_target_pairs={{0,8},{4,28},{8,16},{12,4},{16,24},{20,12},{24,0},{28,20},{32,40},... | collective-permute-start | bytes 491528 | tf_op jit(solution)/shard_map/ppermute | solution.py:53
  20.8 3.5 %collective-permute-done.3 = bf16[32,2560]{1,0:T(8,128)(2,1)S(1)} collective-permute-done((bf16[32,2560]{1,0:T(8,128)(2,1)S(1)}, bf16[32,2560]{1,0:T(8,128)(2,1)S(1)}, u32[]{:S(2)}, u32[]{:S(2)}) %collective-permute-start.3) | collective-permute-done | bytes 163872 | tf_op jit(solution)/shard_map/ppermute | solution.py:53
  24.4 1.8 %collective-permute-start.6 = (bf16[32,2560]{1,0:T(8,128)(2,1)S(1)}, bf16[32,2560]{1,0:T(8,128)(2,1)S(1)}, u32[]{:S(2)}, u32[]{:S(2)}) collective-permute-start(bf16[32,2560]{1,0:T(8,128)(2,1)S(1)} %collective-permute-done.3), channel_id=1, source_target_pairs={{0,32},{4,228},{8,40},{12,236},{16,48},{20,244},{24,56},{28,252},{... | collective-permute-start | bytes 491528 | tf_op jit(solution)/shard_map/ppermute | solution.py:53
  26.8 1.7 %collective-permute-done.6 = bf16[32,2560]{1,0:T(8,128)(2,1)S(1)} collective-permute-done((bf16[32,2560]{1,0:T(8,128)(2,1)S(1)}, bf16[32,2560]{1,0:T(8,128)(2,1)S(1)}, u32[]{:S(2)}, u32[]{:S(2)}) %collective-permute-start.6) | collective-permute-done | bytes 163872 | tf_op jit(solution)/shard_map/ppermute | solution.py:53
  28.6 2.8 %collective-permute-start.8 = (bf16[96,2560]{1,0:T(8,128)(2,1)S(1)}, bf16[96,2560]{1,0:T(8,128)(2,1)S(1)}, u32[]{:S(2)}, u32[]{:S(2)}) collective-permute-start(bf16[96,2560]{1,0:T(8,128)(2,1)S(1)} %constant_dynamic-update-slice_fusion), channel_id=1, source_target_pairs={{0,4},{4,0},{8,12},{12,8},{16,20},{20,16},{24,28},{28,24},{32,36},... | collective-permute-start | bytes 1474568 | tf_op jit(solution)/shard_map/ppermute | solution.py:53
  31.8 6.1 %collective-permute-done.7 = bf16[32,2560]{1,0:T(8,128)(2,1)S(1)} collective-permute-done((bf16[32,2560]{1,0:T(8,128)(2,1)S(1)}, bf16[32,2560]{1,0:T(8,128)(2,1)S(1)}, u32[]{:S(2)}, u32[]{:S(2)}) %collective-permute-start.7) | collective-permute-done | bytes 163872 | tf_op jit(solution)/shard_map/ppermute | solution.py:53
  38.0 1.9 %collective-permute-start.13 = (bf16[256,256]{1,0:T(8,128)(2,1)S(1)}, bf16[256,256]{1,0:T(8,128)(2,1)S(1)}, u32[]{:S(2)}, u32[]{:S(2)}) collective-permute-start(bf16[256,256]{1,0:T(8,128)(2,1)S(1)} %constant_dynamic-update-slice_fusion.3.refs_0_), channel_id=1, source_target_pairs={{0,16},{4,20},{8,24},{12,28},{16,0},{20,4},{24,8},{28,12},{32,48},... | collective-permute-start | bytes 393224 | tf_op jit(solution)/shard_map/ppermute | solution.py:53
  40.1 4.3 %collective-permute-start.11 = (bf16[128,2560]{1,0:T(8,128)(2,1)S(1)}, bf16[128,2560]{1,0:T(8,128)(2,1)S(1)}, u32[]{:S(2)}, u32[]{:S(2)}) collective-permute-start(bf16[128,2560]{1,0:T(8,128)(2,1)S(1)} %collective-permute-done.9.refs_1_), channel_id=1, source_target_pairs={{0,4},{4,0},{8,12},{12,8},{16,20},{20,16},{24,28},{28,24},{32,36},... | collective-permute-start | bytes 1966088 | tf_op jit(solution)/shard_map/ppermute | solution.py:53
  45.9 3.0 %collective-permute-start.18 = (bf16[256,2560]{1,0:T(8,128)(2,1)}, bf16[256,2560]{1,0:T(8,128)(2,1)S(1)}, u32[]{:S(2)}, u32[]{:S(2)}) collective-permute-start(bf16[256,2560]{1,0:T(8,128)(2,1)} %copy-done.2), channel_id=1, source_target_pairs={{0,8},{4,28},{8,16},{12,4},{16,24},{20,12},{24,0},{28,20},{32,40},... | collective-permute-start | bytes 3932168 | tf_op jit(solution)/shard_map/ppermute | solution.py:53
  48.8 1.9 %collective-permute-start.16 = (bf16[256,256]{1,0:T(8,128)(2,1)S(1)}, bf16[256,256]{1,0:T(8,128)(2,1)S(1)}, u32[]{:S(2)}, u32[]{:S(2)}) collective-permute-start(bf16[256,256]{1,0:T(8,128)(2,1)S(1)} %collective-permute-done.12.refs_1_), channel_id=1, source_target_pairs={{0,4},{4,0},{8,12},{12,8},{16,20},{20,16},{24,28},{28,24},{32,36},... | collective-permute-start | bytes 393224 | tf_op jit(solution)/shard_map/ppermute | solution.py:53
  51.7 1.3 %collective-permute-start.15 = (bf16[512,256]{1,0:T(8,128)(2,1)S(1)}, bf16[512,256]{1,0:T(8,128)(2,1)S(1)}, u32[]{:S(2)}, u32[]{:S(2)}) collective-permute-start(bf16[512,256]{1,0:T(8,128)(2,1)S(1)} %slice.60), channel_id=1, source_target_pairs={{0,3},{1,2},{4,7},{5,6},{8,11},{9,10},{12,15},{13,14},{16,19},{17,... | collective-permute-start | bytes 786440 | tf_op jit(solution)/shard_map/ppermute | solution.py:49
  54.0 8.7 %collective-permute-done.15 = bf16[512,256]{1,0:T(8,128)(2,1)S(1)} collective-permute-done((bf16[512,256]{1,0:T(8,128)(2,1)S(1)}, bf16[512,256]{1,0:T(8,128)(2,1)S(1)}, u32[]{:S(2)}, u32[]{:S(2)}) %collective-permute-start.15) | collective-permute-done | bytes 262176 | tf_op jit(solution)/shard_map/ppermute | solution.py:49
  64.6 1.3 %collective-permute-start.22 = (bf16[256,256]{1,0:T(8,128)(2,1)S(1)}, bf16[256,256]{1,0:T(8,128)(2,1)S(1)}, u32[]{:S(2)}, u32[]{:S(2)}) collective-permute-start(bf16[256,256]{1,0:T(8,128)(2,1)S(1)} %broadcast_select_fusion.5), channel_id=1, source_target_pairs={{0,2},{1,3},{4,6},{5,7},{8,10},{9,11},{12,14},{13,15},{16,18},{17,... | collective-permute-start | bytes 393224 | tf_op jit(solution)/shard_map/ppermute | solution.py:49
  65.9 1.3 %collective-permute-start.21 = (bf16[256,256]{1,0:T(8,128)(2,1)S(1)}, bf16[256,256]{1,0:T(8,128)(2,1)}, u32[]{:S(2)}, u32[]{:S(2)}) collective-permute-start(bf16[256,256]{1,0:T(8,128)(2,1)S(1)} %broadcast_select_fusion.5), channel_id=1, source_target_pairs={{0,3},{1,2},{4,7},{5,6},{8,11},{9,10},{12,15},{13,14},{16,19},{17,... | collective-permute-start | bytes 393224 | tf_op jit(solution)/shard_map/ppermute | solution.py:49
  67.2 6.0 %collective-permute-done.22 = bf16[256,256]{1,0:T(8,128)(2,1)S(1)} collective-permute-done((bf16[256,256]{1,0:T(8,128)(2,1)S(1)}, bf16[256,256]{1,0:T(8,128)(2,1)S(1)}, u32[]{:S(2)}, u32[]{:S(2)}) %collective-permute-start.22) | collective-permute-done | bytes 131104 | tf_op jit(solution)/shard_map/ppermute | solution.py:49
  73.9 1.3 %collective-permute-start.20 = (bf16[256,256]{1,0:T(8,128)(2,1)S(1)}, bf16[256,256]{1,0:T(8,128)(2,1)}, u32[]{:S(2)}, u32[]{:S(2)}) collective-permute-start(bf16[256,256]{1,0:T(8,128)(2,1)S(1)} %broadcast_select_fusion.5), channel_id=1, source_target_pairs={{0,1},{1,0},{4,5},{5,4},{8,9},{9,8},{12,13},{13,12},{16,17},{17,16... | collective-permute-start | bytes 393224 | tf_op jit(solution)/shard_map/ppermute | solution.py:49
  75.2 1.2 %collective-permute-done.21 = bf16[256,256]{1,0:T(8,128)(2,1)} collective-permute-done((bf16[256,256]{1,0:T(8,128)(2,1)S(1)}, bf16[256,256]{1,0:T(8,128)(2,1)}, u32[]{:S(2)}, u32[]{:S(2)}) %collective-permute-start.21) | collective-permute-done | bytes 131104 | tf_op jit(solution)/shard_map/ppermute | solution.py:49
  76.4 2.3 %collective-permute-start.23 = (bf16[512,256]{1,0:T(8,128)(2,1)}, bf16[512,256]{1,0:T(8,128)(2,1)S(1)}, u32[]{:S(2)}, u32[]{:S(2)}) collective-permute-start(bf16[512,256]{1,0:T(8,128)(2,1)} %copy-done.12), channel_id=1, source_target_pairs={{2,3},{3,2},{6,7},{7,6},{10,11},{11,10},{14,15},{15,14},{18,19},{1... | collective-permute-start | bytes 786440 | tf_op jit(solution)/shard_map/ppermute | solution.py:49
  79.8 6.2 %collective-permute-done.23 = bf16[512,256]{1,0:T(8,128)(2,1)S(1)} collective-permute-done((bf16[512,256]{1,0:T(8,128)(2,1)}, bf16[512,256]{1,0:T(8,128)(2,1)S(1)}, u32[]{:S(2)}, u32[]{:S(2)}) %collective-permute-start.23) | collective-permute-done | bytes 262176 | tf_op jit(solution)/shard_map/ppermute | solution.py:49
  86.1 1.3 %collective-permute-start.28 = (bf16[128,2560]{1,0:T(8,128)(2,1)S(1)}, bf16[128,2560]{1,0:T(8,128)(2,1)S(1)}, u32[]{:S(2)}, u32[]{:S(2)}) collective-permute-start(bf16[128,2560]{1,0:T(8,128)(2,1)S(1)} %collective-permute-done.17.refs_3_), channel_id=1, source_target_pairs={{0,4},{4,0},{8,12},{12,8},{16,20},{20,16},{24,28},{28,24},{32,36},... | collective-permute-start | bytes 1966088 | tf_op jit(solution)/shard_map/ppermute | solution.py:53
  88.1 2.8 %collective-permute-start.24 = (bf16[256,1280]{1,0:T(8,128)(2,1)S(1)}, bf16[256,1280]{1,0:T(8,128)(2,1)S(1)}, u32[]{:S(2)}, u32[]{:S(2)}) collective-permute-start(bf16[256,1280]{1,0:T(8,128)(2,1)S(1)} %slice_select_fusion), channel_id=1, source_target_pairs={{0,8},{4,28},{8,16},{12,4},{16,24},{20,12},{24,0},{28,20},{32,40},... | collective-permute-start | bytes 1966088 | tf_op jit(solution)/shard_map/ppermute | solution.py:53
  91.6 5.3 %factor.1 = (bf16[512,256]{1,0:T(8,128)(2,1)S(1)}, bf16[512,256]{1,0:T(8,128)(2,1)S(1)}, bf16[256,256]{1,0:T(8,128)(2,1)S(1)}, bf16[512,256]{1,0:T(8,128)(2,1)S(1)}) custom-call(s32[2]{0:T(128)S(1)} %copy-done.9, s32[2,256]{1,0:T(2,128)S(1)} %copy-done.11, bf16[512,256]{1,0:T(8,128)(2,1)S(1)} %get-tuple-element.100.s0_ref, ...), custom_call_target="tpu_custom_call" | custom-call | flops 6442450944 | bytes 4194304 | tf_op jit(solution)/shard_map/factor/pallas_call | solution.py:247
  96.9 3.2 %select.7 = (bf16[256,2560]{1,0:T(8,128)(2,1)S(1)}, bf16[256,2560]{1,0:T(8,128)(2,1)S(1)}) custom-call(bf16[512,512]{1,0:T(8,128)(2,1)S(1)} %copy-done.1, bf16[128,2560]{1,0:T(8,128)(2,1)S(1)} %pad_maximum_fusion.refs_0_, bf16[128,2560]{1,0:T(8,128)(2,1)S(1)} %copy-done.5, bf16[128,2560]{1,0:T(8,128)(2,1)} %collective-permute-done.10.refs_2_, ...), custom_call_target="tpu_custom_call" | custom-call | flops 1174405120 | bytes 1048576 | tf_op jit(solution)/shard_map/select/pallas_call | solution.py:283
  100.2 1.7 %select.6 = (bf16[256,2560]{1,0:T(8,128)(2,1)S(1)}, bf16[256,2560]{1,0:T(8,128)(2,1)S(1)}) custom-call(bf16[512,512]{1,0:T(8,128)(2,1)S(1)} %copy-done, bf16[256,2560]{1,0:T(8,128)(2,1)S(1)} %copy-done.3, bf16[256,2560]{1,0:T(8,128)(2,1)S(1)} %collective-permute-done.18.refs_1_, bf16[256,2560]{1,0:T(8,128)(2,1)S(1)} %collective-permute-done.27.refs_2_), custom_call_target="tpu_custom_call" | custom-call | flops 1006632960 | bytes 1048576 | tf_op jit(solution)/shard_map/select/pallas_call | solution.py:283
  102.5 1.6 %collective-permute-done.30.other_ref = bf16[256,1280]{1,0:T(8,128)(2,1)S(1)} collective-permute-done((bf16[256,1280]{1,0:T(8,128)(2,1)S(1)}, bf16[256,1280]{1,0:T(8,128)(2,1)S(1)}, u32[]{:S(2)}, u32[]{:S(2)}) %collective-permute-start.30) | collective-permute-done | bytes 655392 | tf_op jit(solution)/shard_map/ppermute | solution.py:53
  104.1 6.0 %update.2._ = bf16[512,5120]{1,0:T(8,128)(2,1)} custom-call(s32[2]{0:T(128)S(1)} %copy-done.9, bf16[512,512]{1,0:T(8,128)(2,1)S(1)} %copy-done, bf16[256,2560]{1,0:T(8,128)(2,1)S(1)} %get-tuple-element.90.u0_ref, bf16[256,2560]{1,0:T(8,128)(2,1)S(1)} %get-tuple-element.91.u1_ref, bf16[256,1280]{1,0:T(8,128)(2,1)S(1)} %collective-permute-done.24.mine_ref, ...), custom_call_target="tpu_custom_call" | custom-call | flops 2013265920 | bytes 5242880 | tf_op jit(solution)/shard_map/update/pallas_call | solution.py:350
  110.1 5.6 %update.3 = bf16[512,5120]{1,0:T(8,128)(2,1)} custom-call(s32[2]{0:T(128)S(1)} %copy-done.9, bf16[512,512]{1,0:T(8,128)(2,1)S(1)} %copy-done.1, bf16[256,2560]{1,0:T(8,128)(2,1)S(1)} %get-tuple-element.83.u0_ref, bf16[256,2560]{1,0:T(8,128)(2,1)S(1)} %get-tuple-element.84.u1_ref, ...), custom_call_target="tpu_custom_call", output_to_operand_aliasing={{}: (11, {})} | custom-call | flops 2013265920 | bytes 5242880 | tf_op jit(solution)/shard_map/update/pallas_call | solution.py:350
  (106 shorter events, 12.9 us)
Async XLA Ops:
  4.2 2.0 %collective-permute-start = (bf16[32,5120]{1,0:T(8,128)(2,1)S(1)}, bf16[32,5120]{1,0:T(8,128)(2,1)S(1)}, u32[]{:S(2)}, u32[]{:S(2)}) collective-permute-start(bf16[32,5120]{1,0:T(8,128)(2,1)S(1)} %pick.1), channel_id=1, source_target_pairs={{0,4},{4,0},{8,12},{12,8},{16,20},{20,16},{24,28},{28,24},{32,36},... | collective-permute-start | bytes 983048 | tf_op jit(solution)/shard_map/ppermute | solution.py:53
  6.3 10.4 %collective-permute-start.1 = (bf16[32,2560]{1,0:T(8,128)(2,1)S(1)}, bf16[32,2560]{1,0:T(8,128)(2,1)S(1)}, u32[]{:S(2)}, u32[]{:S(2)}) collective-permute-start(bf16[32,2560]{1,0:T(8,128)(2,1)S(1)} %get-tuple-element.107), channel_id=1, source_target_pairs={{0,32},{4,228},{8,40},{12,236},{16,48},{20,244},{24,56},{28,252},{... | collective-permute-start | bytes 491528 | tf_op jit(solution)/shard_map/ppermute | solution.py:53
  12.0 5.0 %collective-permute-start.2 = (bf16[32,2560]{1,0:T(8,128)(2,1)S(1)}, bf16[32,2560]{1,0:T(8,128)(2,1)S(1)}, u32[]{:S(2)}, u32[]{:S(2)}) collective-permute-start(bf16[32,2560]{1,0:T(8,128)(2,1)S(1)} %get-tuple-element.106), channel_id=1, source_target_pairs={{0,8},{4,28},{8,16},{12,4},{16,24},{20,12},{24,0},{28,20},{32,40},... | collective-permute-start | bytes 491528 | tf_op jit(solution)/shard_map/ppermute | solution.py:53
  17.0 7.4 %collective-permute-start.5 = (bf16[32,2560]{1,0:T(8,128)(2,1)S(1)}, bf16[32,2560]{1,0:T(8,128)(2,1)S(1)}, u32[]{:S(2)}, u32[]{:S(2)}) collective-permute-start(bf16[32,2560]{1,0:T(8,128)(2,1)S(1)} %collective-permute-done.2), channel_id=1, source_target_pairs={{0,4},{4,0},{8,12},{12,8},{16,20},{20,16},{24,28},{28,24},{32,36},... | collective-permute-start | bytes 491528 | tf_op jit(solution)/shard_map/ppermute | solution.py:53
  17.0 7.4 %collective-permute-start.4 = (bf16[32,2560]{1,0:T(8,128)(2,1)S(1)}, bf16[32,2560]{1,0:T(8,128)(2,1)S(1)}, u32[]{:S(2)}, u32[]{:S(2)}) collective-permute-start(bf16[32,2560]{1,0:T(8,128)(2,1)S(1)} %collective-permute-done.2), channel_id=1, source_target_pairs={{0,8},{4,28},{8,16},{12,4},{16,24},{20,12},{24,0},{28,20},{32,40},... | collective-permute-start | bytes 491528 | tf_op jit(solution)/shard_map/ppermute | solution.py:53
  20.1 4.3 %collective-permute-start.3 = (bf16[32,2560]{1,0:T(8,128)(2,1)S(1)}, bf16[32,2560]{1,0:T(8,128)(2,1)S(1)}, u32[]{:S(2)}, u32[]{:S(2)}) collective-permute-start(bf16[32,2560]{1,0:T(8,128)(2,1)S(1)} %collective-permute-done.1), channel_id=1, source_target_pairs={{0,32},{4,228},{8,40},{12,236},{16,48},{20,244},{24,56},{28,252},{... | collective-permute-start | bytes 491528 | tf_op jit(solution)/shard_map/ppermute | solution.py:53
  24.4 4.2 %collective-permute-start.6 = (bf16[32,2560]{1,0:T(8,128)(2,1)S(1)}, bf16[32,2560]{1,0:T(8,128)(2,1)S(1)}, u32[]{:S(2)}, u32[]{:S(2)}) collective-permute-start(bf16[32,2560]{1,0:T(8,128)(2,1)S(1)} %collective-permute-done.3), channel_id=1, source_target_pairs={{0,32},{4,228},{8,40},{12,236},{16,48},{20,244},{24,56},{28,252},{... | collective-permute-start | bytes 491528 | tf_op jit(solution)/shard_map/ppermute | solution.py:53
  26.3 11.6 %collective-permute-start.9 = (bf16[128,2560]{1,0:T(8,128)(2,1)S(1)}, bf16[128,2560]{1,0:T(8,128)(2,1)S(1)}, u32[]{:S(2)}, u32[]{:S(2)}) collective-permute-start(bf16[128,2560]{1,0:T(8,128)(2,1)S(1)} %pad_maximum_fusion.refs_0_), channel_id=1, source_target_pairs={{0,32},{4,228},{8,40},{12,236},{16,48},{20,244},{24,56},{28,252},{... | collective-permute-start | bytes 1966088 | tf_op jit(solution)/shard_map/ppermute | solution.py:53
  28.6 9.3 %collective-permute-start.8 = (bf16[96,2560]{1,0:T(8,128)(2,1)S(1)}, bf16[96,2560]{1,0:T(8,128)(2,1)S(1)}, u32[]{:S(2)}, u32[]{:S(2)}) collective-permute-start(bf16[96,2560]{1,0:T(8,128)(2,1)S(1)} %constant_dynamic-update-slice_fusion), channel_id=1, source_target_pairs={{0,4},{4,0},{8,12},{12,8},{16,20},{20,16},{24,28},{28,24},{32,36},... | collective-permute-start | bytes 1474568 | tf_op jit(solution)/shard_map/ppermute | solution.py:53
  31.4 6.5 %collective-permute-start.7 = (bf16[32,2560]{1,0:T(8,128)(2,1)S(1)}, bf16[32,2560]{1,0:T(8,128)(2,1)S(1)}, u32[]{:S(2)}, u32[]{:S(2)}) collective-permute-start(bf16[32,2560]{1,0:T(8,128)(2,1)S(1)} %collective-permute-done.6), channel_id=1, source_target_pairs={{0,32},{4,228},{8,40},{12,236},{16,48},{20,244},{24,56},{28,252},{... | collective-permute-start | bytes 491528 | tf_op jit(solution)/shard_map/ppermute | solution.py:53
  38.0 6.9 %collective-permute-start.13 = (bf16[256,256]{1,0:T(8,128)(2,1)S(1)}, bf16[256,256]{1,0:T(8,128)(2,1)S(1)}, u32[]{:S(2)}, u32[]{:S(2)}) collective-permute-start(bf16[256,256]{1,0:T(8,128)(2,1)S(1)} %constant_dynamic-update-slice_fusion.3.refs_0_), channel_id=1, source_target_pairs={{0,16},{4,20},{8,24},{12,28},{16,0},{20,4},{24,8},{28,12},{32,48},... | collective-permute-start | bytes 393224 | tf_op jit(solution)/shard_map/ppermute | solution.py:53
  39.9 6.0 %collective-permute-start.12 = (bf16[256,256]{1,0:T(8,128)(2,1)S(1)}, bf16[256,256]{1,0:T(8,128)(2,1)S(1)}, u32[]{:S(2)}, u32[]{:S(2)}) collective-permute-start(bf16[256,256]{1,0:T(8,128)(2,1)S(1)} %constant_dynamic-update-slice_fusion.3.refs_0_), channel_id=1, source_target_pairs={{0,8},{4,28},{8,16},{12,4},{16,24},{20,12},{24,0},{28,20},{32,40},... | collective-permute-start | bytes 393224 | tf_op jit(solution)/shard_map/ppermute | solution.py:53
  40.1 22.7 %collective-permute-start.11 = (bf16[128,2560]{1,0:T(8,128)(2,1)S(1)}, bf16[128,2560]{1,0:T(8,128)(2,1)S(1)}, u32[]{:S(2)}, u32[]{:S(2)}) collective-permute-start(bf16[128,2560]{1,0:T(8,128)(2,1)S(1)} %collective-permute-done.9.refs_1_), channel_id=1, source_target_pairs={{0,4},{4,0},{8,12},{12,8},{16,20},{20,16},{24,28},{28,24},{32,36},... | collective-permute-start | bytes 1966088 | tf_op jit(solution)/shard_map/ppermute | solution.py:53
  44.4 19.3 %collective-permute-start.10 = (bf16[128,2560]{1,0:T(8,128)(2,1)S(1)}, bf16[128,2560]{1,0:T(8,128)(2,1)}, u32[]{:S(2)}, u32[]{:S(2)}) collective-permute-start(bf16[128,2560]{1,0:T(8,128)(2,1)S(1)} %collective-permute-done.9.refs_1_), channel_id=1, source_target_pairs={{0,32},{4,228},{8,40},{12,236},{16,48},{20,244},{24,56},{28,252},{... | collective-permute-start | bytes 1966088 | tf_op jit(solution)/shard_map/ppermute | solution.py:53
  45.9 40.1 %collective-permute-start.18 = (bf16[256,2560]{1,0:T(8,128)(2,1)}, bf16[256,2560]{1,0:T(8,128)(2,1)S(1)}, u32[]{:S(2)}, u32[]{:S(2)}) collective-permute-start(bf16[256,2560]{1,0:T(8,128)(2,1)} %copy-done.2), channel_id=1, source_target_pairs={{0,8},{4,28},{8,16},{12,4},{16,24},{20,12},{24,0},{28,20},{32,40},... | collective-permute-start | bytes 3932168 | tf_op jit(solution)/shard_map/ppermute | solution.py:53
  48.8 4.2 %collective-permute-start.16 = (bf16[256,256]{1,0:T(8,128)(2,1)S(1)}, bf16[256,256]{1,0:T(8,128)(2,1)S(1)}, u32[]{:S(2)}, u32[]{:S(2)}) collective-permute-start(bf16[256,256]{1,0:T(8,128)(2,1)S(1)} %collective-permute-done.12.refs_1_), channel_id=1, source_target_pairs={{0,4},{4,0},{8,12},{12,8},{16,20},{20,16},{24,28},{28,24},{32,36},... | collective-permute-start | bytes 393224 | tf_op jit(solution)/shard_map/ppermute | solution.py:53
  51.7 11.0 %collective-permute-start.15 = (bf16[512,256]{1,0:T(8,128)(2,1)S(1)}, bf16[512,256]{1,0:T(8,128)(2,1)S(1)}, u32[]{:S(2)}, u32[]{:S(2)}) collective-permute-start(bf16[512,256]{1,0:T(8,128)(2,1)S(1)} %slice.60), channel_id=1, source_target_pairs={{0,3},{1,2},{4,7},{5,6},{8,11},{9,10},{12,15},{13,14},{16,19},{17,... | collective-permute-start | bytes 786440 | tf_op jit(solution)/shard_map/ppermute | solution.py:49
  53.0 9.7 %collective-permute-start.14 = (bf16[512,256]{1,0:T(8,128)(2,1)S(1)}, bf16[512,256]{1,0:T(8,128)(2,1)S(1)}, u32[]{:S(2)}, u32[]{:S(2)}) collective-permute-start(bf16[512,256]{1,0:T(8,128)(2,1)S(1)} %slice.60), channel_id=1, source_target_pairs={{0,1},{1,0},{4,5},{5,4},{8,9},{9,8},{12,13},{13,12},{16,17},{17,16... | collective-permute-start | bytes 786440 | tf_op jit(solution)/shard_map/ppermute | solution.py:49
  63.6 22.4 %collective-permute-start.19 = (bf16[128,2560]{1,0:T(8,128)(2,1)}, bf16[128,2560]{1,0:T(8,128)(2,1)}, u32[]{:S(2)}, u32[]{:S(2)}) collective-permute-start(bf16[128,2560]{1,0:T(8,128)(2,1)} %collective-permute-done.10.refs_2_), channel_id=1, source_target_pairs={{0,4},{4,0},{8,12},{12,8},{16,20},{20,16},{24,28},{28,24},{32,36},... | collective-permute-start | bytes 1966088 | tf_op jit(solution)/shard_map/ppermute | solution.py:53
  64.4 21.6 %collective-permute-start.17 = (bf16[128,2560]{1,0:T(8,128)(2,1)}, bf16[128,2560]{1,0:T(8,128)(2,1)S(1)}, u32[]{:S(2)}, u32[]{:S(2)}) collective-permute-start(bf16[128,2560]{1,0:T(8,128)(2,1)} %collective-permute-done.10.refs_2_), channel_id=1, source_target_pairs={{0,32},{4,228},{8,40},{12,236},{16,48},{20,244},{24,56},{28,252},{... | collective-permute-start | bytes 1966088 | tf_op jit(solution)/shard_map/ppermute | solution.py:53
  64.6 8.6 %collective-permute-start.22 = (bf16[256,256]{1,0:T(8,128)(2,1)S(1)}, bf16[256,256]{1,0:T(8,128)(2,1)S(1)}, u32[]{:S(2)}, u32[]{:S(2)}) collective-permute-start(bf16[256,256]{1,0:T(8,128)(2,1)S(1)} %broadcast_select_fusion.5), channel_id=1, source_target_pairs={{0,2},{1,3},{4,6},{5,7},{8,10},{9,11},{12,14},{13,15},{16,18},{17,... | collective-permute-start | bytes 393224 | tf_op jit(solution)/shard_map/ppermute | solution.py:49
  65.9 10.5 %collective-permute-start.21 = (bf16[256,256]{1,0:T(8,128)(2,1)S(1)}, bf16[256,256]{1,0:T(8,128)(2,1)}, u32[]{:S(2)}, u32[]{:S(2)}) collective-permute-start(bf16[256,256]{1,0:T(8,128)(2,1)S(1)} %broadcast_select_fusion.5), channel_id=1, source_target_pairs={{0,3},{1,2},{4,7},{5,6},{8,11},{9,10},{12,15},{13,14},{16,19},{17,... | collective-permute-start | bytes 393224 | tf_op jit(solution)/shard_map/ppermute | solution.py:49
  73.9 4.8 %collective-permute-start.20 = (bf16[256,256]{1,0:T(8,128)(2,1)S(1)}, bf16[256,256]{1,0:T(8,128)(2,1)}, u32[]{:S(2)}, u32[]{:S(2)}) collective-permute-start(bf16[256,256]{1,0:T(8,128)(2,1)S(1)} %broadcast_select_fusion.5), channel_id=1, source_target_pairs={{0,1},{1,0},{4,5},{5,4},{8,9},{9,8},{12,13},{13,12},{16,17},{17,16... | collective-permute-start | bytes 393224 | tf_op jit(solution)/shard_map/ppermute | solution.py:49
  76.4 9.6 %collective-permute-start.23 = (bf16[512,256]{1,0:T(8,128)(2,1)}, bf16[512,256]{1,0:T(8,128)(2,1)S(1)}, u32[]{:S(2)}, u32[]{:S(2)}) collective-permute-start(bf16[512,256]{1,0:T(8,128)(2,1)} %copy-done.12), channel_id=1, source_target_pairs={{2,3},{3,2},{6,7},{7,6},{10,11},{11,10},{14,15},{15,14},{18,19},{1... | collective-permute-start | bytes 786440 | tf_op jit(solution)/shard_map/ppermute | solution.py:49
  86.1 10.8 %collective-permute-start.28 = (bf16[128,2560]{1,0:T(8,128)(2,1)S(1)}, bf16[128,2560]{1,0:T(8,128)(2,1)S(1)}, u32[]{:S(2)}, u32[]{:S(2)}) collective-permute-start(bf16[128,2560]{1,0:T(8,128)(2,1)S(1)} %collective-permute-done.17.refs_3_), channel_id=1, source_target_pairs={{0,4},{4,0},{8,12},{12,8},{16,20},{20,16},{24,28},{28,24},{32,36},... | collective-permute-start | bytes 1966088 | tf_op jit(solution)/shard_map/ppermute | solution.py:53
  87.5 12.7 %collective-permute-start.27 = (bf16[256,2560]{1,0:T(8,128)(2,1)S(1)}, bf16[256,2560]{1,0:T(8,128)(2,1)S(1)}, u32[]{:S(2)}, u32[]{:S(2)}) collective-permute-start(bf16[256,2560]{1,0:T(8,128)(2,1)S(1)} %collective-permute-done.18.refs_1_), channel_id=1, source_target_pairs={{0,4},{4,0},{8,12},{12,8},{16,20},{20,16},{24,28},{28,24},{32,36},... | collective-permute-start | bytes 3932168 | tf_op jit(solution)/shard_map/ppermute | solution.py:53
  87.6 3.8 %collective-permute-start.26 = (bf16[256,512]{1,0:T(8,128)(2,1)S(1)}, bf16[256,512]{1,0:T(8,128)(2,1)S(1)}, u32[]{:S(2)}, u32[]{:S(2)}) collective-permute-start(bf16[256,512]{1,0:T(8,128)(2,1)S(1)} %pad_maximum_fusion.2), channel_id=1, source_target_pairs={{0,4},{4,0},{8,12},{12,8},{16,20},{20,16},{24,28},{28,24},{32,36},... | collective-permute-start | bytes 786440 | tf_op jit(solution)/shard_map/ppermute | solution.py:53
  88.1 13.8 %collective-permute-start.25 = (bf16[128,1280]{1,0:T(8,128)(2,1)S(1)}, bf16[128,1280]{1,0:T(8,128)(2,1)S(1)}, u32[]{:S(2)}, u32[]{:S(2)}) collective-permute-start(bf16[128,1280]{1,0:T(8,128)(2,1)S(1)} %slice_select_fusion.1), channel_id=1, source_target_pairs={{0,32},{4,228},{8,40},{12,236},{16,48},{20,244},{24,56},{28,252},{... | collective-permute-start | bytes 983048 | tf_op jit(solution)/shard_map/ppermute | solution.py:53
  88.1 13.8 %collective-permute-start.24 = (bf16[256,1280]{1,0:T(8,128)(2,1)S(1)}, bf16[256,1280]{1,0:T(8,128)(2,1)S(1)}, u32[]{:S(2)}, u32[]{:S(2)}) collective-permute-start(bf16[256,1280]{1,0:T(8,128)(2,1)S(1)} %slice_select_fusion), channel_id=1, source_target_pairs={{0,8},{4,28},{8,16},{12,4},{16,24},{20,12},{24,0},{28,20},{32,40},... | collective-permute-start | bytes 1966088 | tf_op jit(solution)/shard_map/ppermute | solution.py:53
  91.5 12.6 %slice-start = ((s8[5242880]{0:T(1024)(128)(4,1)}), s8[4194304]{0:T(1024)(128)(4,1)S(1)}, s32[]{:S(2)}) async-start(s8[5242880]{0:T(1024)(128)(4,1)} %bitcast.2), calls=%async_computation | async-start | bytes 8388608
  101.9 2.2 %collective-permute-start.30 = (bf16[256,1280]{1,0:T(8,128)(2,1)S(1)}, bf16[256,1280]{1,0:T(8,128)(2,1)S(1)}, u32[]{:S(2)}, u32[]{:S(2)}) collective-permute-start(bf16[256,1280]{1,0:T(8,128)(2,1)S(1)} %collective-permute-done.24.mine_ref), channel_id=1, source_target_pairs={{0,4},{4,0},{8,12},{12,8},{16,20},{20,16},{24,28},{28,24},{32,36},... | collective-permute-start | bytes 1966088 | tf_op jit(solution)/shard_map/ppermute | solution.py:53
  102.2 7.9 %collective-permute-start.29 = (bf16[128,1280]{1,0:T(8,128)(2,1)S(1)}, bf16[128,1280]{1,0:T(8,128)(2,1)S(1)}, u32[]{:S(2)}, u32[]{:S(2)}) collective-permute-start(bf16[128,1280]{1,0:T(8,128)(2,1)S(1)} %collective-permute-done.25.mine_ref), channel_id=1, source_target_pairs={{0,4},{4,0},{8,12},{12,8},{16,20},{20,16},{24,28},{28,24},{32,36},... | collective-permute-start | bytes 983048 | tf_op jit(solution)/shard_map/ppermute | solution.py:53
  (18 other events, 98.5 us)

commit v2 on v1

--- a/solution.py
+++ b/solution.py
@@ -12,7 +12,7 @@
 CAP = 8
 SLOTS = 2 * CAP
 CHIP = 2 * SLOTS
-WZ = 2560
+WZ = 2048
 F32 = jnp.float32
 BF16 = jnp.bfloat16
 VMEM = pl.BlockSpec(memory_space=pltpu.VMEM)
@@ -113,10 +113,6 @@
 
 def dot(a, b):
     return jnp.dot(a, b, preferred_element_type=F32)
-
-
-def dot_high(a, b):
-    return jnp.dot(a, b, precision=lax.Precision.HIGHEST, preferred_element_type=F32)
 
 
 def pieces(b):
@@ -214,8 +210,10 @@
     twice = jnp.where(eye, 2.0, 0.0)
     guess = (1.0 / diagonal_col) * (twice - wide * (1.0 / diagonal_row))
     for step in range(NEWTON - 1):
-        inner = twice - dot_exact(block, pieces(guess))
-        guess = dot_high(guess, inner)
+        parts = pieces(guess)
+        rest_high, rest_low, _ = pieces(0.5 * twice - dot_exact(block, parts))
+        change = dot(parts[0], rest_low) + dot(parts[1], rest_high)
+        guess = guess + (dot(parts[0], rest_high) + change)
     return guess
 
 
@@ -257,6 +255,33 @@
     )(ids, pivots, *uppers, pan0, pan1)
 
 
+def assemble_kernel(ids, near_ref, own_ref, other_ref, far_ref, all_ref, first_ref):
+    even = ids[0] % 2 == 0
+    n = CHIP
+    own, other = own_ref[...], other_ref[...]
+    down, up = jnp.where(even, own, other), jnp.where(even, other, own)
+    order = [near_ref[...], down, far_ref[...], up[2 * n :], up[n : 2 * n], up[:n]]
+    blocks = jnp.concatenate(order, axis=0)
+    all_ref[...] = blocks
+    first_ref[...] = blocks[:, :NB]
+
+
+def assemble(ids, near, own, other, far):
+    width = near.shape[1]
+    return pl.pallas_call(
+        assemble_kernel,
+        in_specs=[SMEM] + [VMEM] * 4,
+        out_specs=[VMEM, VMEM],
+        out_shape=[
+            jax.ShapeDtypeStruct((ZN * CHIP, width), BF16),
+            jax.ShapeDtypeStruct((ZN * CHIP, NB), BF16),
+        ],
+        compiler_params=PARAMS,
+        cost_estimate=pl.CostEstimate(flops=2**20, bytes_accessed=2**20, transcendentals=0),
+        name="assemble",
+    )(ids, near, own, other, far)
+
+
 def step_of(width):
     if width < 512:
         return width
@@ -294,79 +319,64 @@
 
 
 def update_kernel(
-    start, span, ids, hot_ref, u0_ref, u1_ref, mine_ref, other_ref, l0_ref, l1_ref, lp_ref, fin_ref,
-    a_hbm, _, out_hbm, a_ref, out_ref, in_sems, out_sems,
+    spans, ids, hotz_ref, hoty_ref, uz0, uz1, z_mine, z_other, uy0, uy1, y_mine, y_other,
+    l0_ref, l1_ref, lp_ref, fin_ref, a_ref, out_hbm, out_ref, sems,
 ):
     me, col = ids[0], ids[1]
-    width = u0_ref.shape[1]
-    half = width // 2
-    step = step_of(width)
-    steps = width // step
-
-    def fetch(k):
-        cols = pl.ds(start + k * step, step)
-        return pltpu.make_async_copy(a_hbm.at[:, cols], a_ref.at[k], in_sems.at[k])
-
-    def put(k):
-        cols = pl.ds(start + k * step, step)
-        return pltpu.make_async_copy(out_ref.at[k], out_hbm.at[:, cols], out_sems.at[k])
-
-    for k in range(steps):
-        fetch(k).start()
-    for k in range(steps):
-        at = k * step
-        side = at // half
-        cols = slice(at, at + step)
-        near = slice(at - side * half, at - side * half + step)
-        last = jnp.where(me % 2 == side, mine_ref[:, near], other_ref[:, near])
-        u0 = u0_ref[:, cols].astype(F32) + dot(hot_ref[:NB, span], list_rows([last], 0))
-        u0 = u0.astype(BF16)
-        u1 = u1_ref[:, cols].astype(F32) + dot(hot_ref[NB:, span], list_rows([last], 1))
-        u1 = (u1 - dot(lp_ref[...], u0)).astype(BF16)
-        fetch(k).wait()
-        a = (a_ref[k].astype(F32) - dot(l0_ref[...], u0)).astype(BF16)
-        out_ref[k] = (a.astype(F32) - dot(l1_ref[...], u1)).astype(BF16)
-        if start + at == 0:
-
-            @pl.when(col < 2)
-            def _():
-                out_ref[k, :, :NB] = fin_ref[...]
-
-        put(k).start()
-    for k in range(steps):
-        put(k).wait()
-
-
-def update(ids, hot, span, uppers, mine, other, lefts, lower, fin, matrix, out, start):
+    puts = []
+    start = 0
+    for span, hot_ref, u0_ref, u1_ref, mine_ref, other_ref in (
+        (spans[0], hotz_ref, uz0, uz1, z_mine, z_other),
+        (spans[1], hoty_ref, uy0, uy1, y_mine, y_other),
+    ):
+        width = u0_ref.shape[1]
+        half = width // 2
+        step = step_of(width)
+        for at in range(0, width, step):
+            side = at // half
+            cols = slice(at, at + step)
+            near = slice(at - side * half, at - side * half + step)
+            whole = slice(start + at, start + at + step)
+            last = jnp.where(me % 2 == side, mine_ref[:, near], other_ref[:, near])
+            u0 = u0_ref[:, cols].astype(F32) + dot(hot_ref[:NB, span], list_rows([last], 0))
+            u0 = u0.astype(BF16)
+            u1 = u1_ref[:, cols].astype(F32) + dot(hot_ref[NB:, span], list_rows([last], 1))
+            u1 = (u1 - dot(lp_ref[...], u0)).astype(BF16)
+            a = (a_ref[:, whole].astype(F32) - dot(l0_ref[...], u0)).astype(BF16)
+            out_ref[:, whole] = (a.astype(F32) - dot(l1_ref[...], u1)).astype(BF16)
+            if start + at == 0:
+
+                @pl.when(col < 2)
+                def _():
+                    out_ref[:, :NB] = fin_ref[...]
+
+            put = pltpu.make_async_copy(
+                out_ref.at[:, whole], out_hbm.at[:, whole], sems.at[len(puts)]
+            )
+            put.start()
+            puts.append(put)
+        start += width
+    for put in puts:
+        put.wait()
+
+
+def update(ids, hots, spans, z_parts, y_parts, lefts, lower, fin, matrix):
     rows_dev, columns = matrix.shape
-    width = uppers[0].shape[1]
-    step = step_of(width)
-    steps = width // step
-    aliases = {}
-    if out is None:
-        out = jnp.zeros((16, 128), BF16)
-    else:
-        aliases = {11: 0}
-    return pl.pallas_call(
-        functools.partial(update_kernel, start, slice(*span)),
-        in_specs=[SMEM] + [VMEM] * 9 + [ANY, ANY],
+    steps = sum(parts[0].shape[1] // step_of(parts[0].shape[1]) for parts in (z_parts, y_parts))
+    return pl.pallas_call(
+        functools.partial(update_kernel, [slice(*span) for span in spans]),
+        in_specs=[SMEM] + [VMEM] * 15,
         out_specs=ANY,
         out_shape=jax.ShapeDtypeStruct((rows_dev, columns), BF16),
-        scratch_shapes=[
-            pltpu.VMEM((steps, rows_dev, step), BF16),
-            pltpu.VMEM((steps, rows_dev, step), BF16),
-            pltpu.SemaphoreType.DMA((steps,)),
-            pltpu.SemaphoreType.DMA((steps,)),
-        ],
-        input_output_aliases=aliases,
+        scratch_shapes=[pltpu.VMEM((rows_dev, columns), BF16), pltpu.SemaphoreType.DMA((steps,))],
         compiler_params=PARAMS,
         cost_estimate=pl.CostEstimate(
-            flops=2 * width * NB * (2 * 128 + NB + 2 * rows_dev),
-            bytes_accessed=4 * width * rows_dev,
+            flops=2 * columns * NB * (2 * 128 + NB + 2 * rows_dev),
+            bytes_accessed=4 * columns * rows_dev,
             transcendentals=0,
         ),
         name="update",
-    )(ids, hot, *uppers, mine, other, *lefts, lower, fin, matrix, out)
+    )(ids, *hots, *z_parts, *y_parts, *lefts, lower, fin, matrix)
 
 
 def on_device(matrix, pivots):
@@ -393,39 +403,32 @@
     hot_z, hot_y = maps(ids, pivots, rows_dev)
     t1, r1, hot_z, hot_y = both(send(zb, ALONG_Z), send(yb, ALONG_Y), hot_z, hot_y)
 
+    panel = after(matrix[:, :NB], t1)
+    near, far = over(panel, NEAR), over(panel, FAR)
     t2, r2, q1 = both(send(t1, ALONG_Z), send(r1, ALONG_Y), send(r1, PAIR))
     yf = jnp.concatenate([yb, jnp.where(even, r1, q1), r2, jnp.where(even, q1, r1)], axis=0)
 
     y1 = send(yf, ALONG_Z)
-    t3 = send(t2, ALONG_Z)
+    t3, near, far = both(send(t2, ALONG_Z), near, far)
     own = jnp.concatenate([t1, t2, t3], axis=0)
     t4, oth, y1 = both(send(t3, ALONG_Z), send(own, PAIR), y1)
 
-    def z_blocks(cols):
-        own_cols, oth_cols = own[:, cols], oth[:, cols]
-        down, up = jnp.where(even, own_cols, oth_cols), jnp.where(even, oth_cols, own_cols)
-        order = [zb[:, cols], down, t4[:, cols], up[2 * n :], up[n : 2 * n], up[:n]]
-        return jnp.concatenate(order, axis=0)
-
-    v0 = z_blocks(slice(0, NB))
-    zf = z_blocks(slice(0, WZ))
-    v1, v2 = both(send(v0, ALONG_Y), send(v0, TWICE_Y))
+    zf, v0 = assemble(ids, zb, own, oth, t4)
+    across = over(far, ACROSS)
+    v1, v2, across = both(send(v0, ALONG_Y), send(half(v0), TWICE_Y), across)
     z1 = send(after(zf, v1), ALONG_Y)
-    w1 = send(v1, PAIR)
+    w = send(jnp.concatenate([v1, v2], axis=1), PAIR)
+    w1, w2 = w[:, :NB], w[:, NB:]
+    opposite = jnp.concatenate([jnp.where(even, v2, w2), jnp.where(even, w2, v2)], axis=1)
     k = ZN * SLOTS
-    entries = select(hot_z, [v0, v1, v2, w1], [(i * k, (i + 1) * k) for i in range(4)])
-    panel = after(matrix[:, :NB], v1)
-    near, far = over(panel, NEAR), over(panel, FAR)
-    y2, o1, near, far, *entries = both(
-        send(y1, ALONG_Z), send(y1, PAIR), near, far, *entries
-    )
+    entries = select(hot_z, [v0, v1, opposite, w1], [(i * k, (i + 1) * k) for i in range(4)])
+    y2, o1, *entries = both(send(y1, ALONG_Z), send(y1, PAIR), *entries)
+    pan0, pan1 = panels(panel, near, far, across)
 
     part = jnp.where(even, entries[0], entries[1])
     part = panels(part, over(part, NEAR), over(part, FAR), over(part, SKIP))
     part = jnp.concatenate(part, axis=1)
-    across = over(far, ACROSS)
-    y3, z1, o2, part, across = both(send(y2, ALONG_Z), z1, send(y2, PAIR), part, across)
-    pan0, pan1 = panels(panel, near, far, across)
+    y3, z1, o2, part = both(send(y2, ALONG_Z), z1, send(y2, PAIR), part)
 
     rest = send(part, PAIR)
     uppers = jnp.concatenate([jnp.where(even, part, rest), jnp.where(even, rest, part)], axis=0)
@@ -439,12 +442,12 @@
     z2, y4, left0, *us = both(
         send(half(z1), ALONG_Y), send(half(y3), ALONG_Z), left0, *uz, *uy
     )
-    uz, uy = us[:2], us[2:]
-
-    lefts = (left0, left1)
     p2, o4 = send(z2, PAIR), send(y4, PAIR)
-    out = update(ids, hot_z, (2 * k, 3 * k), uz, z2, p2, lefts, lower, fin, matrix, None, 0)
-    return update(ids, hot_y, (4 * n, 5 * n), uy, y4, o4, lefts, lower, fin, matrix, out, WZ)
+    spans = ((2 * k, 3 * k), (4 * n, 5 * n))
+    z_parts, y_parts = (*us[:2], z2, p2), (*us[2:], y4, o4)
+    return update(
+        ids, (hot_z, hot_y), spans, z_parts, y_parts, (left0, left1), lower, fin, matrix
+    )
 
 
 def solution(mesh):

time: 116 us -> 98.2 us (0.85)
  the two profiles are of different devices: /device:TPU:7 before, /device:TPU:1 now
where the time goes in v2:
time: 98.2 us; the launch traced here: 97.8 us
  starting transfers between devices  45.6 us (46%)
  Pallas kernels  25.1 us (26%)
  waiting for transfers between devices  21.1 us (21%)
  other arithmetic  2.67 us (3%)
  local copies, waits for them, and re-layouts  2.66 us (3%)
    ppermute x25, starting transfers between devices, send(): return lax.ppermute(array, 'prow', pairs)  31.1 us
    ppermute x6, starting transfers between devices, over(): return lax.ppermute(array, 'pcol', pairs)  14.5 us
    ppermute x25, waiting for transfers between devices, send(): return lax.ppermute(array, 'prow', pairs)  11.5 us
    ppermute x6, waiting for transfers between devices, over(): return lax.ppermute(array, 'pcol', pairs)  9.7 us
    pallas_call x1, Pallas kernels, update(): pl.pallas_call(functools.partial(update_kernel, [slice(*span) for span in...  7.57 us
    pallas_call x3, Pallas kernels, select(): pl.pallas_call(functools.partial(select_kernel, spans), in_specs=[VMEM] *...  6 us
    pallas_call x1, Pallas kernels, factor(): pl.pallas_call(factor_kernel, in_specs=[SMEM] + [VMEM] * 5, out_specs=[VM...  4.46 us
    pallas_call x1, Pallas kernels, pick(): pl.pallas_call(functools.partial(pick_kernel, chunk), in_specs=[SMEM, VME...  3.4 us
  transfers between devices with their start and end apart: 31, of which 8 were waited for; matrix products, arithmetic and copies ran while one was open for 4% of the time, Pallas kernels for 14%

profile of v2, /device:TPU:1, one launch (start us, length us, event | category | flops | bytes accessed | tf_op | source)
XLA Modules:
  0.0 97.8 jit_solution(14062670775797101349)
XLA Ops:
  0.8 3.4 %pick.1 = bf16[32,5120]{1,0:T(8,128)(2,1)S(1)} custom-call(s32[2]{0:T(128)S(1)} %pad_add_fusion.ids, s32[2,256]{1,0:T(2,128)S(1)} %copy-done.8, bf16[512,5120]{1,0:T(8,128)(2,1)} %a_ref.1), custom_call_target="tpu_custom_call" | custom-call | flops 167772160 | bytes 10485760 | tf_op jit(solution)/shard_map/pick/pallas_call | solution.py:166
  4.2 3.3 %collective-permute-start = (bf16[32,5120]{1,0:T(8,128)(2,1)S(1)}, bf16[32,5120]{1,0:T(8,128)(2,1)S(1)}, u32[]{:S(2)}, u32[]{:S(2)}) collective-permute-start(bf16[32,5120]{1,0:T(8,128)(2,1)S(1)} %pick.1), channel_id=1, source_target_pairs={{0,4},{4,0},{8,12},{12,8},{16,20},{20,16},{24,28},{28,24},{32,36},... | collective-permute-start | bytes 983048 | tf_op jit(solution)/shard_map/ppermute | solution.py:53
  7.5 1.3 %collective-permute-done = bf16[32,5120]{1,0:T(8,128)(2,1)S(1)} collective-permute-done((bf16[32,5120]{1,0:T(8,128)(2,1)S(1)}, bf16[32,5120]{1,0:T(8,128)(2,1)S(1)}, u32[]{:S(2)}, u32[]{:S(2)}) %collective-permute-start) | collective-permute-done | bytes 327712 | tf_op jit(solution)/shard_map/ppermute | solution.py:53
  8.9 1.1 %collective-permute-start.2 = (bf16[32,3072]{1,0:T(8,128)(2,1)S(1)}, bf16[32,3072]{1,0:T(8,128)(2,1)S(1)}, u32[]{:S(2)}, u32[]{:S(2)}) collective-permute-start(bf16[32,3072]{1,0:T(8,128)(2,1)S(1)} %slice.53), channel_id=1, source_target_pairs={{0,8},{4,28},{8,16},{12,4},{16,24},{20,12},{24,0},{28,20},{32,40},... | collective-permute-start | bytes 589832 | tf_op jit(solution)/shard_map/ppermute | solution.py:53
  10.0 5.7 %collective-permute-start.1 = (bf16[32,2048]{1,0:T(8,128)(2,1)S(1)}, bf16[32,2048]{1,0:T(8,128)(2,1)S(1)}, u32[]{:S(2)}, u32[]{:S(2)}) collective-permute-start(bf16[32,2048]{1,0:T(8,128)(2,1)S(1)} %slice.52.near_ref), channel_id=1, source_target_pairs={{0,32},{4,228},{8,40},{12,236},{16,48},{20,244},{24,56},{28,252},{... | collective-permute-start | bytes 393224 | tf_op jit(solution)/shard_map/ppermute | solution.py:53
  15.6 1.0 slice.41
  16.6 2.0 %maps.1 = (bf16[512,512]{1,0:T(8,128)(2,1)}, bf16[512,512]{1,0:T(8,128)(2,1)}) custom-call(s32[2]{0:T(128)} %copy-done.6, s32[2,256]{1,0:T(2,128)} %piv_ref.5), custom_call_target="tpu_custom_call" | custom-call | flops 1073741824 | bytes 4194304 | tf_op jit(solution)/shard_map/maps/pallas_call | solution.py:194
  19.4 2.1 %collective-permute-start.3 = (bf16[32,2048]{1,0:T(8,128)(2,1)S(1)}, bf16[32,2048]{1,0:T(8,128)(2,1)S(1)}, u32[]{:S(2)}, u32[]{:S(2)}) collective-permute-start(bf16[32,2048]{1,0:T(8,128)(2,1)S(1)} %collective-permute-done.1), channel_id=1, source_target_pairs={{0,32},{4,228},{8,40},{12,236},{16,48},{20,244},{24,56},{28,252},{... | collective-permute-start | bytes 393224 | tf_op jit(solution)/shard_map/ppermute | solution.py:53
  21.6 4.4 %collective-permute-start.8 = (bf16[512,256]{1,0:T(8,128)(2,1)S(1)}, bf16[512,256]{1,0:T(8,128)(2,1)S(1)}, u32[]{:S(2)}, u32[]{:S(2)}) collective-permute-start(bf16[512,256]{1,0:T(8,128)(2,1)S(1)} %slice.41), channel_id=1, source_target_pairs={{0,3},{1,2},{4,7},{5,6},{8,11},{9,10},{12,15},{13,14},{16,19},{17,... | collective-permute-start | bytes 786440 | tf_op jit(solution)/shard_map/ppermute | solution.py:49
  26.0 1.9 %collective-permute-start.7 = (bf16[512,256]{1,0:T(8,128)(2,1)S(1)}, bf16[512,256]{1,0:T(8,128)(2,1)S(1)}, u32[]{:S(2)}, u32[]{:S(2)}) collective-permute-start(bf16[512,256]{1,0:T(8,128)(2,1)S(1)} %slice.41), channel_id=1, source_target_pairs={{0,1},{1,0},{4,5},{5,4},{8,9},{9,8},{12,13},{13,12},{16,17},{17,16... | collective-permute-start | bytes 786440 | tf_op jit(solution)/shard_map/ppermute | solution.py:49
  29.7 1.0 %collective-permute-done.8 = bf16[512,256]{1,0:T(8,128)(2,1)S(1)} collective-permute-done((bf16[512,256]{1,0:T(8,128)(2,1)S(1)}, bf16[512,256]{1,0:T(8,128)(2,1)S(1)}, u32[]{:S(2)}, u32[]{:S(2)}) %collective-permute-start.8) | collective-permute-done | bytes 262176 | tf_op jit(solution)/shard_map/ppermute | solution.py:49
  30.7 4.4 %collective-permute-done.7 = bf16[512,256]{1,0:T(8,128)(2,1)S(1)} collective-permute-done((bf16[512,256]{1,0:T(8,128)(2,1)S(1)}, bf16[512,256]{1,0:T(8,128)(2,1)S(1)}, u32[]{:S(2)}, u32[]{:S(2)}) %collective-permute-start.7) | collective-permute-done | bytes 262176 | tf_op jit(solution)/shard_map/ppermute | solution.py:49
  35.2 2.2 %collective-permute-start.9 = (bf16[32,2048]{1,0:T(8,128)(2,1)S(1)}, bf16[32,2048]{1,0:T(8,128)(2,1)S(1)}, u32[]{:S(2)}, u32[]{:S(2)}) collective-permute-start(bf16[32,2048]{1,0:T(8,128)(2,1)S(1)} %collective-permute-done.6), channel_id=1, source_target_pairs={{0,32},{4,228},{8,40},{12,236},{16,48},{20,244},{24,56},{28,252},{... | collective-permute-start | bytes 393224 | tf_op jit(solution)/shard_map/ppermute | solution.py:53
  38.1 3.9 %collective-permute-done.9.far_ref = bf16[32,2048]{1,0:T(8,128)(2,1)S(1)} collective-permute-done((bf16[32,2048]{1,0:T(8,128)(2,1)S(1)}, bf16[32,2048]{1,0:T(8,128)(2,1)S(1)}, u32[]{:S(2)}, u32[]{:S(2)}) %collective-permute-start.9) | collective-permute-done | bytes 131104 | tf_op jit(solution)/shard_map/ppermute | solution.py:53
  42.8 1.7 %collective-permute-start.12 = (bf16[128,3072]{1,0:T(8,128)(2,1)S(1)}, bf16[128,3072]{1,0:T(8,128)(2,1)}, u32[]{:S(2)}, u32[]{:S(2)}) collective-permute-start(bf16[128,3072]{1,0:T(8,128)(2,1)S(1)} %collective-permute-done.11.refs_1_), channel_id=1, source_target_pairs={{0,32},{4,228},{8,40},{12,236},{16,48},{20,244},{24,56},{28,252},{... | collective-permute-start | bytes 2359304 | tf_op jit(solution)/shard_map/ppermute | solution.py:53
  44.5 1.6 %assemble.1 = (bf16[256,2048]{1,0:T(8,128)(2,1)}, bf16[256,256]{1,0:T(8,128)(2,1)S(1)}) custom-call(s32[2]{0:T(128)S(1)} %copy-done.7, bf16[32,2048]{1,0:T(8,128)(2,1)S(1)} %slice.52.near_ref, bf16[96,2048]{1,0:T(8,128)(2,1)S(1)} %constant_dynamic-update-slice_fusion.own_ref, bf16[96,2048]{1,0:T(8,128)(2,1)S(1)} %collective-permute-done.10.other_ref, ...), custom_call_target="tpu_custom_call" | custom-call | flops 1048576 | bytes 1048576 | tf_op jit(solution)/shard_map/assemble/pallas_call | solution.py:271
  46.1 2.5 %collective-permute-start.14 = (bf16[256,256]{1,0:T(8,128)(2,1)S(1)}, bf16[256,256]{1,0:T(8,128)(2,1)S(1)}, u32[]{:S(2)}, u32[]{:S(2)}) collective-permute-start(bf16[256,256]{1,0:T(8,128)(2,1)S(1)} %get-tuple-element.66.refs_0_), channel_id=1, source_target_pairs={{0,8},{4,28},{8,16},{12,4},{16,24},{20,12},{24,0},{28,20},{32,40},... | collective-permute-start | bytes 393224 | tf_op jit(solution)/shard_map/ppermute | solution.py:53
  49.0 4.3 %collective-permute-done.15 = bf16[256,128]{1,0:T(8,128)(2,1)S(1)} collective-permute-done((bf16[256,128]{1,0:T(8,128)(2,1)S(1)}, bf16[256,128]{1,0:T(8,128)(2,1)S(1)}, u32[]{:S(2)}, u32[]{:S(2)}) %collective-permute-start.15) | collective-permute-done | bytes 65568 | tf_op jit(solution)/shard_map/ppermute | solution.py:53
  53.5 2.4 %collective-permute-start.19 = (bf16[256,2048]{1,0:T(8,128)(2,1)}, bf16[256,2048]{1,0:T(8,128)(2,1)S(1)}, u32[]{:S(2)}, u32[]{:S(2)}) collective-permute-start(bf16[256,2048]{1,0:T(8,128)(2,1)} %get-tuple-element.74.refs_0_), channel_id=1, source_target_pairs={{0,8},{4,28},{8,16},{12,4},{16,24},{20,12},{24,0},{28,20},{32,40},... | collective-permute-start | bytes 3145736 | tf_op jit(solution)/shard_map/ppermute | solution.py:53
  57.2 1.7 %collective-permute-start.18 = (bf16[128,3072]{1,0:T(8,128)(2,1)}, bf16[128,3072]{1,0:T(8,128)(2,1)S(1)}, u32[]{:S(2)}, u32[]{:S(2)}) collective-permute-start(bf16[128,3072]{1,0:T(8,128)(2,1)} %collective-permute-done.12.refs_2_), channel_id=1, source_target_pairs={{0,32},{4,228},{8,40},{12,236},{16,48},{20,244},{24,56},{28,252},{... | collective-permute-start | bytes 2359304 | tf_op jit(solution)/shard_map/ppermute | solution.py:53
  58.9 3.8 %collective-permute-start.23 = (bf16[256,256]{1,0:T(8,128)(2,1)S(1)}, bf16[256,256]{1,0:T(8,128)(2,1)}, u32[]{:S(2)}, u32[]{:S(2)}) collective-permute-start(bf16[256,256]{1,0:T(8,128)(2,1)S(1)} %broadcast_select_fusion.4), channel_id=1, source_target_pairs={{0,2},{1,3},{4,6},{5,7},{8,10},{9,11},{12,14},{13,15},{16,18},{17,... | collective-permute-start | bytes 393224 | tf_op jit(solution)/shard_map/ppermute | solution.py:49
  62.8 1.3 %collective-permute-start.22 = (bf16[256,256]{1,0:T(8,128)(2,1)S(1)}, bf16[256,256]{1,0:T(8,128)(2,1)S(1)}, u32[]{:S(2)}, u32[]{:S(2)}) collective-permute-start(bf16[256,256]{1,0:T(8,128)(2,1)S(1)} %broadcast_select_fusion.4), channel_id=1, source_target_pairs={{0,3},{1,2},{4,7},{5,6},{8,11},{9,10},{12,15},{13,14},{16,19},{17,... | collective-permute-start | bytes 393224 | tf_op jit(solution)/shard_map/ppermute | solution.py:49
  65.0 2.4 %collective-permute-start.21 = (bf16[256,256]{1,0:T(8,128)(2,1)S(1)}, bf16[256,256]{1,0:T(8,128)(2,1)S(1)}, u32[]{:S(2)}, u32[]{:S(2)}) collective-permute-start(bf16[256,256]{1,0:T(8,128)(2,1)S(1)} %broadcast_select_fusion.4), channel_id=1, source_target_pairs={{0,1},{1,0},{4,5},{5,4},{8,9},{9,8},{12,13},{13,12},{16,17},{17,16... | collective-permute-start | bytes 393224 | tf_op jit(solution)/shard_map/ppermute | solution.py:49
  67.4 1.2 %select_select_fusion = (bf16[512,256]{1,0:T(8,128)(2,1)S(1)}, bf16[512,256]{1,0:T(8,128)(2,1)S(1)}) fusion(bf16[512,256]{1,0:T(8,128)(2,1)S(1)} %slice.41, bf16[512,256]{1,0:T(8,128)(2,1)} %copy-done.11, bf16[512,256]{1,0:T(8,128)(2,1)} %copy-done.10, bf16[512,256]{1,0:T(8,128)(2,1)} %copy-done.12, pred[]{:T(512)S(6)} %eq.29, pred[]{:T(512)S(6)} %eq.14, ...), kind=kLoop, calls=%fused_computation.8 | loop fusion | flops 786432 | bytes 1572868 | tf_op jit(solution)/shard_map/jit(_where)/select_n | solution.py:391
  68.6 3.4 %collective-permute-done.21 = bf16[256,256]{1,0:T(8,128)(2,1)S(1)} collective-permute-done((bf16[256,256]{1,0:T(8,128)(2,1)S(1)}, bf16[256,256]{1,0:T(8,128)(2,1)S(1)}, u32[]{:S(2)}, u32[]{:S(2)}) %collective-permute-start.21) | collective-permute-done | bytes 131104 | tf_op jit(solution)/shard_map/ppermute | solution.py:49
  72.0 0.9 select_select_fusion.3
  74.6 2.5 %collective-permute-start.24 = (bf16[256,1024]{1,0:T(8,128)(2,1)S(1)}, bf16[256,1024]{1,0:T(8,128)(2,1)S(1)}, u32[]{:S(2)}, u32[]{:S(2)}) collective-permute-start(bf16[256,1024]{1,0:T(8,128)(2,1)S(1)} %slice_select_fusion), channel_id=1, source_target_pairs={{0,8},{4,28},{8,16},{12,4},{16,24},{20,12},{24,0},{28,20},{32,40},... | collective-permute-start | bytes 1572872 | tf_op jit(solution)/shard_map/ppermute | solution.py:53
  77.2 4.5 %factor.1 = (bf16[512,256]{1,0:T(8,128)(2,1)S(1)}, bf16[512,256]{1,0:T(8,128)(2,1)S(1)}, bf16[256,256]{1,0:T(8,128)(2,1)S(1)}, bf16[512,256]{1,0:T(8,128)(2,1)S(1)}) custom-call(s32[2]{0:T(128)S(1)} %copy-done.7, s32[2,256]{1,0:T(2,128)S(1)} %copy-done.9, bf16[512,256]{1,0:T(8,128)(2,1)S(1)} %get-tuple-element.102.s0_ref, ...), custom_call_target="tpu_custom_call" | custom-call | flops 6442450944 | bytes 4194304 | tf_op jit(solution)/shard_map/factor/pallas_call | solution.py:245
  81.7 3.2 %select.7 = (bf16[256,3072]{1,0:T(8,128)(2,1)S(1)}, bf16[256,3072]{1,0:T(8,128)(2,1)S(1)}) custom-call(bf16[512,512]{1,0:T(8,128)(2,1)S(1)} %copy-done.1, bf16[128,3072]{1,0:T(8,128)(2,1)S(1)} %pad_maximum_fusion.refs_0_, bf16[128,3072]{1,0:T(8,128)(2,1)S(1)} %copy-done.3, bf16[128,3072]{1,0:T(8,128)(2,1)} %collective-permute-done.12.refs_2_, ...), custom_call_target="tpu_custom_call" | custom-call | flops 1409286144 | bytes 1048576 | tf_op jit(solution)/shard_map/select/pallas_call | solution.py:308
  85.0 2.5 %select.6 = (bf16[256,2048]{1,0:T(8,128)(2,1)S(1)}, bf16[256,2048]{1,0:T(8,128)(2,1)S(1)}) custom-call(bf16[512,512]{1,0:T(8,128)(2,1)S(1)} %copy-done, bf16[256,2048]{1,0:T(8,128)(2,1)} %get-tuple-element.74.refs_0_, bf16[256,2048]{1,0:T(8,128)(2,1)S(1)} %collective-permute-done.19.refs_1_, bf16[256,2048]{1,0:T(8,128)(2,1)S(1)} %collective-permute-done.27.refs_2_), custom_call_target="tpu_custom_call" | custom-call | flops 805306368 | bytes 1048576 | tf_op jit(solution)/shard_map/select/pallas_call | solution.py:308
  88.1 2.0 %collective-permute-done.30.y_other = bf16[128,1536]{1,0:T(8,128)(2,1)S(1)} collective-permute-done((bf16[128,1536]{1,0:T(8,128)(2,1)S(1)}, bf16[128,1536]{1,0:T(8,128)(2,1)S(1)}, u32[]{:S(2)}, u32[]{:S(2)}) %collective-permute-start.30) | collective-permute-done | bytes 393248 | tf_op jit(solution)/shard_map/ppermute | solution.py:53
  90.1 7.6 %update.1 = bf16[512,5120]{1,0:T(8,128)(2,1)} custom-call(s32[2]{0:T(128)S(1)} %copy-done.7, bf16[512,512]{1,0:T(8,128)(2,1)S(1)} %copy-done, bf16[512,512]{1,0:T(8,128)(2,1)S(1)} %copy-done.1, bf16[256,2048]{1,0:T(8,128)(2,1)S(1)} %get-tuple-element.89.uz0, bf16[256,2048]{1,0:T(8,128)(2,1)S(1)} %get-tuple-element.90.uz1, ...), custom_call_target="tpu_custom_call" | custom-call | flops 4026531840 | bytes 10485760 | tf_op jit(solution)/shard_map/update/pallas_call | solution.py:366
  (92 shorter events, 10.0 us)
Async XLA Ops:
  4.2 4.6 %collective-permute-start = (bf16[32,5120]{1,0:T(8,128)(2,1)S(1)}, bf16[32,5120]{1,0:T(8,128)(2,1)S(1)}, u32[]{:S(2)}, u32[]{:S(2)}) collective-permute-start(bf16[32,5120]{1,0:T(8,128)(2,1)S(1)} %pick.1), channel_id=1, source_target_pairs={{0,4},{4,0},{8,12},{12,8},{16,20},{20,16},{24,28},{28,24},{32,36},... | collective-permute-start | bytes 983048 | tf_op jit(solution)/shard_map/ppermute | solution.py:53
  8.9 9.8 %collective-permute-start.2 = (bf16[32,3072]{1,0:T(8,128)(2,1)S(1)}, bf16[32,3072]{1,0:T(8,128)(2,1)S(1)}, u32[]{:S(2)}, u32[]{:S(2)}) collective-permute-start(bf16[32,3072]{1,0:T(8,128)(2,1)S(1)} %slice.53), channel_id=1, source_target_pairs={{0,8},{4,28},{8,16},{12,4},{16,24},{20,12},{24,0},{28,20},{32,40},... | collective-permute-start | bytes 589832 | tf_op jit(solution)/shard_map/ppermute | solution.py:53
  10.0 8.7 %collective-permute-start.1 = (bf16[32,2048]{1,0:T(8,128)(2,1)S(1)}, bf16[32,2048]{1,0:T(8,128)(2,1)S(1)}, u32[]{:S(2)}, u32[]{:S(2)}) collective-permute-start(bf16[32,2048]{1,0:T(8,128)(2,1)S(1)} %slice.52.near_ref), channel_id=1, source_target_pairs={{0,32},{4,228},{8,40},{12,236},{16,48},{20,244},{24,56},{28,252},{... | collective-permute-start | bytes 393224 | tf_op jit(solution)/shard_map/ppermute | solution.py:53
  18.6 9.3 %collective-permute-start.5 = (bf16[32,3072]{1,0:T(8,128)(2,1)S(1)}, bf16[32,3072]{1,0:T(8,128)(2,1)S(1)}, u32[]{:S(2)}, u32[]{:S(2)}) collective-permute-start(bf16[32,3072]{1,0:T(8,128)(2,1)S(1)} %collective-permute-done.2), channel_id=1, source_target_pairs={{0,4},{4,0},{8,12},{12,8},{16,20},{20,16},{24,28},{28,24},{32,36},... | collective-permute-start | bytes 589832 | tf_op jit(solution)/shard_map/ppermute | solution.py:53
  18.7 9.2 %collective-permute-start.4 = (bf16[32,3072]{1,0:T(8,128)(2,1)S(1)}, bf16[32,3072]{1,0:T(8,128)(2,1)S(1)}, u32[]{:S(2)}, u32[]{:S(2)}) collective-permute-start(bf16[32,3072]{1,0:T(8,128)(2,1)S(1)} %collective-permute-done.2), channel_id=1, source_target_pairs={{0,8},{4,28},{8,16},{12,4},{16,24},{20,12},{24,0},{28,20},{32,40},... | collective-permute-start | bytes 589832 | tf_op jit(solution)/shard_map/ppermute | solution.py:53
  19.4 8.5 %collective-permute-start.3 = (bf16[32,2048]{1,0:T(8,128)(2,1)S(1)}, bf16[32,2048]{1,0:T(8,128)(2,1)S(1)}, u32[]{:S(2)}, u32[]{:S(2)}) collective-permute-start(bf16[32,2048]{1,0:T(8,128)(2,1)S(1)} %collective-permute-done.1), channel_id=1, source_target_pairs={{0,32},{4,228},{8,40},{12,236},{16,48},{20,244},{24,56},{28,252},{... | collective-permute-start | bytes 393224 | tf_op jit(solution)/shard_map/ppermute | solution.py:53
  21.6 9.1 %collective-permute-start.8 = (bf16[512,256]{1,0:T(8,128)(2,1)S(1)}, bf16[512,256]{1,0:T(8,128)(2,1)S(1)}, u32[]{:S(2)}, u32[]{:S(2)}) collective-permute-start(bf16[512,256]{1,0:T(8,128)(2,1)S(1)} %slice.41), channel_id=1, source_target_pairs={{0,3},{1,2},{4,7},{5,6},{8,11},{9,10},{12,15},{13,14},{16,19},{17,... | collective-permute-start | bytes 786440 | tf_op jit(solution)/shard_map/ppermute | solution.py:49
  26.0 9.1 %collective-permute-start.7 = (bf16[512,256]{1,0:T(8,128)(2,1)S(1)}, bf16[512,256]{1,0:T(8,128)(2,1)S(1)}, u32[]{:S(2)}, u32[]{:S(2)}) collective-permute-start(bf16[512,256]{1,0:T(8,128)(2,1)S(1)} %slice.41), channel_id=1, source_target_pairs={{0,1},{1,0},{4,5},{5,4},{8,9},{9,8},{12,13},{13,12},{16,17},{17,16... | collective-permute-start | bytes 786440 | tf_op jit(solution)/shard_map/ppermute | solution.py:49
  27.9 7.1 %collective-permute-start.6 = (bf16[32,2048]{1,0:T(8,128)(2,1)S(1)}, bf16[32,2048]{1,0:T(8,128)(2,1)S(1)}, u32[]{:S(2)}, u32[]{:S(2)}) collective-permute-start(bf16[32,2048]{1,0:T(8,128)(2,1)S(1)} %collective-permute-done.3), channel_id=1, source_target_pairs={{0,32},{4,228},{8,40},{12,236},{16,48},{20,244},{24,56},{28,252},{... | collective-permute-start | bytes 393224 | tf_op jit(solution)/shard_map/ppermute | solution.py:53
  28.9 27.1 %copy-start = (bf16[512,512]{1,0:T(8,128)(2,1)S(1)}, bf16[512,512]{1,0:T(8,128)(2,1)}, u32[]{:S(2)}) copy-start(bf16[512,512]{1,0:T(8,128)(2,1)} %get-tuple-element.54.hot_ref.hotz_ref) | copy-start | bytes 1572868
  28.9 13.1 %collective-permute-start.11 = (bf16[128,3072]{1,0:T(8,128)(2,1)S(1)}, bf16[128,3072]{1,0:T(8,128)(2,1)S(1)}, u32[]{:S(2)}, u32[]{:S(2)}) collective-permute-start(bf16[128,3072]{1,0:T(8,128)(2,1)S(1)} %pad_maximum_fusion.refs_0_), channel_id=1, source_target_pairs={{0,32},{4,228},{8,40},{12,236},{16,48},{20,244},{24,56},{28,252},{... | collective-permute-start | bytes 2359304 | tf_op jit(solution)/shard_map/ppermute | solution.py:53
  35.1 6.9 %collective-permute-start.10 = (bf16[96,2048]{1,0:T(8,128)(2,1)S(1)}, bf16[96,2048]{1,0:T(8,128)(2,1)S(1)}, u32[]{:S(2)}, u32[]{:S(2)}) collective-permute-start(bf16[96,2048]{1,0:T(8,128)(2,1)S(1)} %constant_dynamic-update-slice_fusion.own_ref), channel_id=1, source_target_pairs={{0,4},{4,0},{8,12},{12,8},{16,20},{20,16},{24,28},{28,24},{32,36},... | collective-permute-start | bytes 1179656 | tf_op jit(solution)/shard_map/ppermute | solution.py:53
  35.2 6.8 %collective-permute-start.9 = (bf16[32,2048]{1,0:T(8,128)(2,1)S(1)}, bf16[32,2048]{1,0:T(8,128)(2,1)S(1)}, u32[]{:S(2)}, u32[]{:S(2)}) collective-permute-start(bf16[32,2048]{1,0:T(8,128)(2,1)S(1)} %collective-permute-done.6), channel_id=1, source_target_pairs={{0,32},{4,228},{8,40},{12,236},{16,48},{20,244},{24,56},{28,252},{... | collective-permute-start | bytes 393224 | tf_op jit(solution)/shard_map/ppermute | solution.py:53
  37.4 11.6 %collective-permute-start.16 = (bf16[512,256]{1,0:T(8,128)(2,1)S(1)}, bf16[512,256]{1,0:T(8,128)(2,1)S(1)}, u32[]{:S(2)}, u32[]{:S(2)}) collective-permute-start(bf16[512,256]{1,0:T(8,128)(2,1)S(1)} %collective-permute-done.8), channel_id=1, source_target_pairs={{2,3},{3,2},{6,7},{7,6},{10,11},{11,10},{14,15},{15,14},{18,19},{1... | collective-permute-start | bytes 786440 | tf_op jit(solution)/shard_map/ppermute | solution.py:49
  42.0 14.3 %collective-permute-start.13 = (bf16[128,3072]{1,0:T(8,128)(2,1)S(1)}, bf16[128,3072]{1,0:T(8,128)(2,1)S(1)}, u32[]{:S(2)}, u32[]{:S(2)}) collective-permute-start(bf16[128,3072]{1,0:T(8,128)(2,1)S(1)} %collective-permute-done.11.refs_1_), channel_id=1, source_target_pairs={{0,4},{4,0},{8,12},{12,8},{16,20},{20,16},{24,28},{28,24},{32,36},... | collective-permute-start | bytes 2359304 | tf_op jit(solution)/shard_map/ppermute | solution.py:53
  42.8 14.4 %collective-permute-start.12 = (bf16[128,3072]{1,0:T(8,128)(2,1)S(1)}, bf16[128,3072]{1,0:T(8,128)(2,1)}, u32[]{:S(2)}, u32[]{:S(2)}) collective-permute-start(bf16[128,3072]{1,0:T(8,128)(2,1)S(1)} %collective-permute-done.11.refs_1_), channel_id=1, source_target_pairs={{0,32},{4,228},{8,40},{12,236},{16,48},{20,244},{24,56},{28,252},{... | collective-permute-start | bytes 2359304 | tf_op jit(solution)/shard_map/ppermute | solution.py:53
  46.1 7.2 %collective-permute-start.14 = (bf16[256,256]{1,0:T(8,128)(2,1)S(1)}, bf16[256,256]{1,0:T(8,128)(2,1)S(1)}, u32[]{:S(2)}, u32[]{:S(2)}) collective-permute-start(bf16[256,256]{1,0:T(8,128)(2,1)S(1)} %get-tuple-element.66.refs_0_), channel_id=1, source_target_pairs={{0,8},{4,28},{8,16},{12,4},{16,24},{20,12},{24,0},{28,20},{32,40},... | collective-permute-start | bytes 393224 | tf_op jit(solution)/shard_map/ppermute | solution.py:53
  48.6 4.7 %collective-permute-start.15 = (bf16[256,128]{1,0:T(8,128)(2,1)S(1)}, bf16[256,128]{1,0:T(8,128)(2,1)S(1)}, u32[]{:S(2)}, u32[]{:S(2)}) collective-permute-start(bf16[256,128]{1,0:T(8,128)(2,1)S(1)} %slice_select_fusion.2), channel_id=1, source_target_pairs={{0,16},{4,20},{8,24},{12,28},{16,0},{20,4},{24,8},{28,12},{32,48},... | collective-permute-start | bytes 196616 | tf_op jit(solution)/shard_map/ppermute | solution.py:53
  53.4 2.5 %collective-permute-start.17 = (bf16[256,384]{1,0:T(8,128)(2,1)S(1)}, bf16[256,384]{1,0:T(8,128)(2,1)S(1)}, u32[]{:S(2)}, u32[]{:S(2)}) collective-permute-start(bf16[256,384]{1,0:T(8,128)(2,1)S(1)} %pad_maximum_fusion.3), channel_id=1, source_target_pairs={{0,4},{4,0},{8,12},{12,8},{16,20},{20,16},{24,28},{28,24},{32,36},... | collective-permute-start | bytes 589832 | tf_op jit(solution)/shard_map/ppermute | solution.py:53
  53.5 19.5 %collective-permute-start.19 = (bf16[256,2048]{1,0:T(8,128)(2,1)}, bf16[256,2048]{1,0:T(8,128)(2,1)S(1)}, u32[]{:S(2)}, u32[]{:S(2)}) collective-permute-start(bf16[256,2048]{1,0:T(8,128)(2,1)} %get-tuple-element.74.refs_0_), channel_id=1, source_target_pairs={{0,8},{4,28},{8,16},{12,4},{16,24},{20,12},{24,0},{28,20},{32,40},... | collective-permute-start | bytes 3145736 | tf_op jit(solution)/shard_map/ppermute | solution.py:53
  57.2 15.8 %collective-permute-start.20 = (bf16[128,3072]{1,0:T(8,128)(2,1)}, bf16[128,3072]{1,0:T(8,128)(2,1)}, u32[]{:S(2)}, u32[]{:S(2)}) collective-permute-start(bf16[128,3072]{1,0:T(8,128)(2,1)} %collective-permute-done.12.refs_2_), channel_id=1, source_target_pairs={{0,4},{4,0},{8,12},{12,8},{16,20},{20,16},{24,28},{28,24},{32,36},... | collective-permute-start | bytes 2359304 | tf_op jit(solution)/shard_map/ppermute | solution.py:53
  57.2 15.8 %collective-permute-start.18 = (bf16[128,3072]{1,0:T(8,128)(2,1)}, bf16[128,3072]{1,0:T(8,128)(2,1)S(1)}, u32[]{:S(2)}, u32[]{:S(2)}) collective-permute-start(bf16[128,3072]{1,0:T(8,128)(2,1)} %collective-permute-done.12.refs_2_), channel_id=1, source_target_pairs={{0,32},{4,228},{8,40},{12,236},{16,48},{20,244},{24,56},{28,252},{... | collective-permute-start | bytes 2359304 | tf_op jit(solution)/shard_map/ppermute | solution.py:53
  58.9 6.0 %collective-permute-start.23 = (bf16[256,256]{1,0:T(8,128)(2,1)S(1)}, bf16[256,256]{1,0:T(8,128)(2,1)}, u32[]{:S(2)}, u32[]{:S(2)}) collective-permute-start(bf16[256,256]{1,0:T(8,128)(2,1)S(1)} %broadcast_select_fusion.4), channel_id=1, source_target_pairs={{0,2},{1,3},{4,6},{5,7},{8,10},{9,11},{12,14},{13,15},{16,18},{17,... | collective-permute-start | bytes 393224 | tf_op jit(solution)/shard_map/ppermute | solution.py:49
  62.8 5.8 %collective-permute-start.22 = (bf16[256,256]{1,0:T(8,128)(2,1)S(1)}, bf16[256,256]{1,0:T(8,128)(2,1)S(1)}, u32[]{:S(2)}, u32[]{:S(2)}) collective-permute-start(bf16[256,256]{1,0:T(8,128)(2,1)S(1)} %broadcast_select_fusion.4), channel_id=1, source_target_pairs={{0,3},{1,2},{4,7},{5,6},{8,11},{9,10},{12,15},{13,14},{16,19},{17,... | collective-permute-start | bytes 393224 | tf_op jit(solution)/shard_map/ppermute | solution.py:49
  65.0 7.0 %collective-permute-start.21 = (bf16[256,256]{1,0:T(8,128)(2,1)S(1)}, bf16[256,256]{1,0:T(8,128)(2,1)S(1)}, u32[]{:S(2)}, u32[]{:S(2)}) collective-permute-start(bf16[256,256]{1,0:T(8,128)(2,1)S(1)} %broadcast_select_fusion.4), channel_id=1, source_target_pairs={{0,1},{1,0},{4,5},{5,4},{8,9},{9,8},{12,13},{13,12},{16,17},{17,16... | collective-permute-start | bytes 393224 | tf_op jit(solution)/shard_map/ppermute | solution.py:49
  73.0 4.1 %collective-permute-start.26 = (bf16[256,512]{1,0:T(8,128)(2,1)S(1)}, bf16[256,512]{1,0:T(8,128)(2,1)S(1)}, u32[]{:S(2)}, u32[]{:S(2)}) collective-permute-start(bf16[256,512]{1,0:T(8,128)(2,1)S(1)} %pad_maximum_fusion.2), channel_id=1, source_target_pairs={{0,4},{4,0},{8,12},{12,8},{16,20},{20,16},{24,28},{28,24},{32,36},... | collective-permute-start | bytes 786440 | tf_op jit(solution)/shard_map/ppermute | solution.py:53
  73.9 7.8 %collective-permute-start.28 = (bf16[128,3072]{1,0:T(8,128)(2,1)S(1)}, bf16[128,3072]{1,0:T(8,128)(2,1)S(1)}, u32[]{:S(2)}, u32[]{:S(2)}) collective-permute-start(bf16[128,3072]{1,0:T(8,128)(2,1)S(1)} %collective-permute-done.18.refs_3_), channel_id=1, source_target_pairs={{0,4},{4,0},{8,12},{12,8},{16,20},{20,16},{24,28},{28,24},{32,36},... | collective-permute-start | bytes 2359304 | tf_op jit(solution)/shard_map/ppermute | solution.py:53
  74.0 13.5 %collective-permute-start.25 = (bf16[128,1536]{1,0:T(8,128)(2,1)S(1)}, bf16[128,1536]{1,0:T(8,128)(2,1)S(1)}, u32[]{:S(2)}, u32[]{:S(2)}) collective-permute-start(bf16[128,1536]{1,0:T(8,128)(2,1)S(1)} %slice_select_fusion.1), channel_id=1, source_target_pairs={{0,32},{4,228},{8,40},{12,236},{16,48},{20,244},{24,56},{28,252},{... | collective-permute-start | bytes 1179656 | tf_op jit(solution)/shard_map/ppermute | solution.py:53
  74.3 10.6 %collective-permute-start.27 = (bf16[256,2048]{1,0:T(8,128)(2,1)S(1)}, bf16[256,2048]{1,0:T(8,128)(2,1)S(1)}, u32[]{:S(2)}, u32[]{:S(2)}) collective-permute-start(bf16[256,2048]{1,0:T(8,128)(2,1)S(1)} %collective-permute-done.19.refs_1_), channel_id=1, source_target_pairs={{0,4},{4,0},{8,12},{12,8},{16,20},{20,16},{24,28},{28,24},{32,36},... | collective-permute-start | bytes 3145736 | tf_op jit(solution)/shard_map/ppermute | solution.py:53
  74.6 12.9 %collective-permute-start.24 = (bf16[256,1024]{1,0:T(8,128)(2,1)S(1)}, bf16[256,1024]{1,0:T(8,128)(2,1)S(1)}, u32[]{:S(2)}, u32[]{:S(2)}) collective-permute-start(bf16[256,1024]{1,0:T(8,128)(2,1)S(1)} %slice_select_fusion), channel_id=1, source_target_pairs={{0,8},{4,28},{8,16},{12,4},{16,24},{20,12},{24,0},{28,20},{32,40},... | collective-permute-start | bytes 1572872 | tf_op jit(solution)/shard_map/ppermute | solution.py:53
  87.5 2.6 %collective-permute-start.29 = (bf16[256,1024]{1,0:T(8,128)(2,1)S(1)}, bf16[256,1024]{1,0:T(8,128)(2,1)S(1)}, u32[]{:S(2)}, u32[]{:S(2)}) collective-permute-start(bf16[256,1024]{1,0:T(8,128)(2,1)S(1)} %collective-permute-done.24.z_mine), channel_id=1, source_target_pairs={{0,4},{4,0},{8,12},{12,8},{16,20},{20,16},{24,28},{28,24},{32,36},... | collective-permute-start | bytes 1572872 | tf_op jit(solution)/shard_map/ppermute | solution.py:53
  87.6 2.5 %collective-permute-start.30 = (bf16[128,1536]{1,0:T(8,128)(2,1)S(1)}, bf16[128,1536]{1,0:T(8,128)(2,1)S(1)}, u32[]{:S(2)}, u32[]{:S(2)}) collective-permute-start(bf16[128,1536]{1,0:T(8,128)(2,1)S(1)} %collective-permute-done.25.y_mine), channel_id=1, source_target_pairs={{0,4},{4,0},{8,12},{12,8},{16,20},{20,16},{24,28},{28,24},{32,36},... | collective-permute-start | bytes 1179656 | tf_op jit(solution)/shard_map/ppermute | solution.py:53
  (14 other events, 130.0 us)

commit v3 on v2

--- a/solution.py
+++ b/solution.py
@@ -39,10 +39,9 @@
 PAIR = [(i, i ^ 1) for i in range(2 * ZN * YN)]
 
 
-NEAR = [(0, 1), (1, 0)]
-FAR = [(0, 3), (1, 2)]
-SKIP = [(0, 2), (1, 3)]
-ACROSS = [(2, 3), (3, 2)]
+NEAR = [(0, 1), (1, 0), (2, 3), (3, 2)]
+FAR = [(0, 3), (1, 2), (2, 1), (3, 0)]
+SKIP = [(0, 2), (1, 3), (2, 0), (3, 1)]
 
 
 def over(array, pairs):
@@ -255,15 +254,13 @@
     )(ids, pivots, *uppers, pan0, pan1)
 
 
-def assemble_kernel(ids, near_ref, own_ref, other_ref, far_ref, all_ref, first_ref):
+def assemble_kernel(ids, near_ref, own_ref, other_ref, far_ref, all_ref):
     even = ids[0] % 2 == 0
     n = CHIP
     own, other = own_ref[...], other_ref[...]
     down, up = jnp.where(even, own, other), jnp.where(even, other, own)
     order = [near_ref[...], down, far_ref[...], up[2 * n :], up[n : 2 * n], up[:n]]
-    blocks = jnp.concatenate(order, axis=0)
-    all_ref[...] = blocks
-    first_ref[...] = blocks[:, :NB]
+    all_ref[...] = jnp.concatenate(order, axis=0)
 
 
 def assemble(ids, near, own, other, far):
@@ -271,11 +268,8 @@
     return pl.pallas_call(
         assemble_kernel,
         in_specs=[SMEM] + [VMEM] * 4,
-        out_specs=[VMEM, VMEM],
-        out_shape=[
-            jax.ShapeDtypeStruct((ZN * CHIP, width), BF16),
-            jax.ShapeDtypeStruct((ZN * CHIP, NB), BF16),
-        ],
+        out_specs=VMEM,
+        out_shape=jax.ShapeDtypeStruct((ZN * CHIP, width), BF16),
         compiler_params=PARAMS,
         cost_estimate=pl.CostEstimate(flops=2**20, bytes_accessed=2**20, transcendentals=0),
         name="assemble",
@@ -413,8 +407,12 @@
     own = jnp.concatenate([t1, t2, t3], axis=0)
     t4, oth, y1 = both(send(t3, ALONG_Z), send(own, PAIR), y1)
 
-    zf, v0 = assemble(ids, zb, own, oth, t4)
-    across = over(far, ACROSS)
+    own_first, oth_first = own[:, :NB], oth[:, :NB]
+    down, up = jnp.where(even, own_first, oth_first), jnp.where(even, oth_first, own_first)
+    order = [zb[:, :NB], down, t4[:, :NB], up[2 * n :], up[n : 2 * n], up[:n]]
+    v0 = jnp.concatenate(order, axis=0)
+    zf = assemble(after(ids, v0), zb, own, oth, t4)
+    across = over(far, NEAR)
     v1, v2, across = both(send(v0, ALONG_Y), send(half(v0), TWICE_Y), across)
     z1 = send(after(zf, v1), ALONG_Y)
     w = send(jnp.concatenate([v1, v2], axis=1), PAIR)
@@ -435,16 +433,14 @@
     uppers = [uppers[:, :NB], uppers[:, NB:]]
     left0, left1, lower, fin = factor(ids, pivots, uppers, pan0, pan1)
     p1, o3 = send(z1, PAIR), send(y3, PAIR)
-    uz = select(hot_z, [zf, z1, p1], [(0, k), (k, 2 * k), (3 * k, 4 * k)])
     n = YN * SLOTS
     spans = [(i * n, (i + 1) * n) for i in (0, 1, 2, 3, 5, 6, 7)]
     uy = select(hot_y, [yf, y1, y2, y3, o3, o2, o1], spans)
-    z2, y4, left0, *us = both(
-        send(half(z1), ALONG_Y), send(half(y3), ALONG_Z), left0, *uz, *uy
-    )
+    z2, y4, left0, *uy = both(send(half(z1), ALONG_Y), send(half(y3), ALONG_Z), left0, *uy)
     p2, o4 = send(z2, PAIR), send(y4, PAIR)
+    uz = select(after(hot_z, z2), [zf, z1, p1], [(0, k), (k, 2 * k), (3 * k, 4 * k)])
     spans = ((2 * k, 3 * k), (4 * n, 5 * n))
-    z_parts, y_parts = (*us[:2], z2, p2), (*us[2:], y4, o4)
+    z_parts, y_parts = (*uz, z2, p2), (*uy, y4, o4)
     return update(
         ids, (hot_z, hot_y), spans, z_parts, y_parts, (left0, left1), lower, fin, matrix
     )

time: 98.2 us -> 95 us (0.967)
  starting transfers between devices: 45.6 us -> 42.4 us
  Pallas kernels: 25.1 us -> 22.9 us
  other arithmetic: 2.67 us -> 4.55 us
    ppermute x6, starting transfers between devices: 14.5 us -> 8.44 us  [over(): return lax.ppermute(array, 'pcol', pairs)]
    ppermute x25, starting transfers between devices: 31.1 us -> 33.9 us  [send(): return lax.ppermute(array, 'prow', pairs)]
    select_n x3, other arithmetic: 0.11 us -> 1.22 us  [half(): return jnp.where(even, array[:, :width], array[:, width:])]
    pallas_call x1, Pallas kernels: 1.62 us -> 0.62 us  [assemble(): pl.pallas_call(assemble_kernel, in_specs=[SMEM] + [VMEM] * 4, out_specs=V...]
    pallas_call x3, Pallas kernels: 6 us -> 5.01 us  [select(): pl.pallas_call(functools.partial(select_kernel, spans), in_specs=[VMEM] *...]
  transfers between devices with their start and end apart: 31 -> 31, of which waited for: 8 -> 9; matrix products, arithmetic and copies ran while one was open for 4% -> 6% of each run, Pallas kernels for 14% -> 13%
where the time goes in v3:
time: 95 us; the launch traced here: 94.7 us
  starting transfers between devices  42.4 us (45%)
  Pallas kernels  22.9 us (24%)
  waiting for transfers between devices  21.5 us (23%)
  other arithmetic  4.55 us (5%)
  local copies, waits for them, and re-layouts  2.7 us (3%)
    ppermute x25, starting transfers between devices, send(): return lax.ppermute(array, 'prow', pairs)  33.9 us
    ppermute x25, waiting for transfers between devices, send(): return lax.ppermute(array, 'prow', pairs)  12 us
    ppermute x6, waiting for transfers between devices, over(): return lax.ppermute(array, 'pcol', pairs)  9.46 us
    ppermute x6, starting transfers between devices, over(): return lax.ppermute(array, 'pcol', pairs)  8.44 us
    pallas_call x1, Pallas kernels, update(): pl.pallas_call(functools.partial(update_kernel, [slice(*span) for span in...  7.36 us
    pallas_call x3, Pallas kernels, select(): pl.pallas_call(functools.partial(select_kernel, spans), in_specs=[VMEM] *...  5.01 us
    pallas_call x1, Pallas kernels, factor(): pl.pallas_call(factor_kernel, in_specs=[SMEM] + [VMEM] * 5, out_specs=[VM...  4.46 us
    pallas_call x1, Pallas kernels, pick(): pl.pallas_call(functools.partial(pick_kernel, chunk), in_specs=[SMEM, VME...  3.4 us
  transfers between devices with their start and end apart: 31, of which 9 were waited for; matrix products, arithmetic and copies ran while one was open for 6% of the time, Pallas kernels for 13%

profile of v3, /device:TPU:1, one launch (start us, length us, event | category | flops | bytes accessed | tf_op | source)
XLA Modules:
  0.0 94.7 jit_solution(4114034929501638696)
XLA Ops:
  0.8 3.4 %pick.1 = bf16[32,5120]{1,0:T(8,128)(2,1)S(1)} custom-call(s32[2]{0:T(128)S(1)} %pad_add_fusion.ids, s32[2,256]{1,0:T(2,128)S(1)} %copy-done.8, bf16[512,5120]{1,0:T(8,128)(2,1)} %a_ref.1), custom_call_target="tpu_custom_call" | custom-call | flops 167772160 | bytes 10485760 | tf_op jit(solution)/shard_map/pick/pallas_call | solution.py:165
  4.2 3.3 %collective-permute-start = (bf16[32,5120]{1,0:T(8,128)(2,1)S(1)}, bf16[32,5120]{1,0:T(8,128)(2,1)S(1)}, u32[]{:S(2)}, u32[]{:S(2)}) collective-permute-start(bf16[32,5120]{1,0:T(8,128)(2,1)S(1)} %pick.1), channel_id=1, source_target_pairs={{0,4},{4,0},{8,12},{12,8},{16,20},{20,16},{24,28},{28,24},{32,36},... | collective-permute-start | bytes 983048 | tf_op jit(solution)/shard_map/ppermute | solution.py:52
  7.5 1.3 %collective-permute-done = bf16[32,5120]{1,0:T(8,128)(2,1)S(1)} collective-permute-done((bf16[32,5120]{1,0:T(8,128)(2,1)S(1)}, bf16[32,5120]{1,0:T(8,128)(2,1)S(1)}, u32[]{:S(2)}, u32[]{:S(2)}) %collective-permute-start) | collective-permute-done | bytes 327712 | tf_op jit(solution)/shard_map/ppermute | solution.py:52
  8.9 1.1 %collective-permute-start.2 = (bf16[32,3072]{1,0:T(8,128)(2,1)S(1)}, bf16[32,3072]{1,0:T(8,128)(2,1)S(1)}, u32[]{:S(2)}, u32[]{:S(2)}) collective-permute-start(bf16[32,3072]{1,0:T(8,128)(2,1)S(1)} %slice.82), channel_id=1, source_target_pairs={{0,8},{4,28},{8,16},{12,4},{16,24},{20,12},{24,0},{28,20},{32,40},... | collective-permute-start | bytes 589832 | tf_op jit(solution)/shard_map/ppermute | solution.py:52
  10.0 5.7 %collective-permute-start.1 = (bf16[32,2048]{1,0:T(8,128)(2,1)S(1)}, bf16[32,2048]{1,0:T(8,128)(2,1)S(1)}, u32[]{:S(2)}, u32[]{:S(2)}) collective-permute-start(bf16[32,2048]{1,0:T(8,128)(2,1)S(1)} %slice.81.near_ref), channel_id=1, source_target_pairs={{0,32},{4,228},{8,40},{12,236},{16,48},{20,244},{24,56},{28,252},{... | collective-permute-start | bytes 393224 | tf_op jit(solution)/shard_map/ppermute | solution.py:52
  16.6 2.1 %maps.1 = (bf16[512,512]{1,0:T(8,128)(2,1)}, bf16[512,512]{1,0:T(8,128)(2,1)}) custom-call(s32[2]{0:T(128)} %copy-done.6, s32[2,256]{1,0:T(2,128)} %piv_ref.5), custom_call_target="tpu_custom_call" | custom-call | flops 1073741824 | bytes 4194304 | tf_op jit(solution)/shard_map/maps/pallas_call | solution.py:193
  19.4 2.1 %collective-permute-start.3 = (bf16[32,2048]{1,0:T(8,128)(2,1)S(1)}, bf16[32,2048]{1,0:T(8,128)(2,1)S(1)}, u32[]{:S(2)}, u32[]{:S(2)}) collective-permute-start(bf16[32,2048]{1,0:T(8,128)(2,1)S(1)} %collective-permute-done.1), channel_id=1, source_target_pairs={{0,32},{4,228},{8,40},{12,236},{16,48},{20,244},{24,56},{28,252},{... | collective-permute-start | bytes 393224 | tf_op jit(solution)/shard_map/ppermute | solution.py:52
  21.6 2.5 %collective-permute-start.8 = (bf16[512,256]{1,0:T(8,128)(2,1)S(1)}, bf16[512,256]{1,0:T(8,128)(2,1)S(1)}, u32[]{:S(2)}, u32[]{:S(2)}) collective-permute-start(bf16[512,256]{1,0:T(8,128)(2,1)S(1)} %slice.63), channel_id=1, source_target_pairs={{0,3},{1,2},{2,1},{3,0},{4,7},{5,6},{6,5},{7,4},{8,11},{9,10},{10,... | collective-permute-start | bytes 786440 | tf_op jit(solution)/shard_map/ppermute | solution.py:48
  24.1 2.8 %collective-permute-start.6 = (bf16[32,2048]{1,0:T(8,128)(2,1)S(1)}, bf16[32,2048]{1,0:T(8,128)(2,1)S(1)}, u32[]{:S(2)}, u32[]{:S(2)}) collective-permute-start(bf16[32,2048]{1,0:T(8,128)(2,1)S(1)} %collective-permute-done.3), channel_id=1, source_target_pairs={{0,32},{4,228},{8,40},{12,236},{16,48},{20,244},{24,56},{28,252},{... | collective-permute-start | bytes 393224 | tf_op jit(solution)/shard_map/ppermute | solution.py:52
  27.1 2.2 %collective-permute-done.8 = bf16[512,256]{1,0:T(8,128)(2,1)S(1)} collective-permute-done((bf16[512,256]{1,0:T(8,128)(2,1)S(1)}, bf16[512,256]{1,0:T(8,128)(2,1)S(1)}, u32[]{:S(2)}, u32[]{:S(2)}) %collective-permute-start.8) | collective-permute-done | bytes 262176 | tf_op jit(solution)/shard_map/ppermute | solution.py:48
  29.3 1.8 %collective-permute-done.7 = bf16[512,256]{1,0:T(8,128)(2,1)S(1)} collective-permute-done((bf16[512,256]{1,0:T(8,128)(2,1)S(1)}, bf16[512,256]{1,0:T(8,128)(2,1)S(1)}, u32[]{:S(2)}, u32[]{:S(2)}) %collective-permute-start.7) | collective-permute-done | bytes 262176 | tf_op jit(solution)/shard_map/ppermute | solution.py:48
  31.2 1.2 %collective-permute-start.10 = (bf16[96,2048]{1,0:T(8,128)(2,1)S(1)}, bf16[96,2048]{1,0:T(8,128)(2,1)S(1)}, u32[]{:S(2)}, u32[]{:S(2)}) collective-permute-start(bf16[96,2048]{1,0:T(8,128)(2,1)S(1)} %constant_dynamic-update-slice_fusion.own_ref), channel_id=1, source_target_pairs={{0,4},{4,0},{8,12},{12,8},{16,20},{20,16},{24,28},{28,24},{32,36},... | collective-permute-start | bytes 1179656 | tf_op jit(solution)/shard_map/ppermute | solution.py:52
  32.4 1.2 %collective-permute-start.9 = (bf16[32,2048]{1,0:T(8,128)(2,1)S(1)}, bf16[32,2048]{1,0:T(8,128)(2,1)S(1)}, u32[]{:S(2)}, u32[]{:S(2)}) collective-permute-start(bf16[32,2048]{1,0:T(8,128)(2,1)S(1)} %collective-permute-done.6), channel_id=1, source_target_pairs={{0,32},{4,228},{8,40},{12,236},{16,48},{20,244},{24,56},{28,252},{... | collective-permute-start | bytes 393224 | tf_op jit(solution)/shard_map/ppermute | solution.py:52
  34.3 5.3 %collective-permute-done.9.far_ref = bf16[32,2048]{1,0:T(8,128)(2,1)S(1)} collective-permute-done((bf16[32,2048]{1,0:T(8,128)(2,1)S(1)}, bf16[32,2048]{1,0:T(8,128)(2,1)S(1)}, u32[]{:S(2)}, u32[]{:S(2)}) %collective-permute-start.9) | collective-permute-done | bytes 131104 | tf_op jit(solution)/shard_map/ppermute | solution.py:52
  39.6 2.6 %collective-permute-start.13 = (bf16[128,3072]{1,0:T(8,128)(2,1)S(1)}, bf16[128,3072]{1,0:T(8,128)(2,1)S(1)}, u32[]{:S(2)}, u32[]{:S(2)}) collective-permute-start(bf16[128,3072]{1,0:T(8,128)(2,1)S(1)} %collective-permute-done.11.refs_1_), channel_id=1, source_target_pairs={{0,4},{4,0},{8,12},{12,8},{16,20},{20,16},{24,28},{28,24},{32,36},... | collective-permute-start | bytes 2359304 | tf_op jit(solution)/shard_map/ppermute | solution.py:52
  43.0 2.4 %collective-permute-start.14 = (bf16[256,256]{1,0:T(8,128)(2,1)S(1)}, bf16[256,256]{1,0:T(8,128)(2,1)S(1)}, u32[]{:S(2)}, u32[]{:S(2)}) collective-permute-start(bf16[256,256]{1,0:T(8,128)(2,1)S(1)} %constant_dynamic-update-slice_fusion.3.refs_0_), channel_id=1, source_target_pairs={{0,8},{4,28},{8,16},{12,4},{16,24},{20,12},{24,0},{28,20},{32,40},... | collective-permute-start | bytes 393224 | tf_op jit(solution)/shard_map/ppermute | solution.py:52
  45.7 4.7 %collective-permute-done.15 = bf16[256,128]{1,0:T(8,128)(2,1)S(1)} collective-permute-done((bf16[256,128]{1,0:T(8,128)(2,1)S(1)}, bf16[256,128]{1,0:T(8,128)(2,1)S(1)}, u32[]{:S(2)}, u32[]{:S(2)}) %collective-permute-start.15) | collective-permute-done | bytes 65568 | tf_op jit(solution)/shard_map/ppermute | solution.py:52
  51.3 1.8 %collective-permute-start.19 = (bf16[256,2048]{1,0:T(8,128)(2,1)S(1)}, bf16[256,2048]{1,0:T(8,128)(2,1)S(1)}, u32[]{:S(2)}, u32[]{:S(2)}) collective-permute-start(bf16[256,2048]{1,0:T(8,128)(2,1)S(1)} %assemble.1.refs_0_), channel_id=1, source_target_pairs={{0,8},{4,28},{8,16},{12,4},{16,24},{20,12},{24,0},{28,20},{32,40},... | collective-permute-start | bytes 3145736 | tf_op jit(solution)/shard_map/ppermute | solution.py:52
  54.4 1.3 %collective-permute-start.20 = (bf16[128,3072]{1,0:T(8,128)(2,1)}, bf16[128,3072]{1,0:T(8,128)(2,1)}, u32[]{:S(2)}, u32[]{:S(2)}) collective-permute-start(bf16[128,3072]{1,0:T(8,128)(2,1)} %collective-permute-done.12.refs_2_), channel_id=1, source_target_pairs={{0,4},{4,0},{8,12},{12,8},{16,20},{20,16},{24,28},{28,24},{32,36},... | collective-permute-start | bytes 2359304 | tf_op jit(solution)/shard_map/ppermute | solution.py:52
  57.3 2.7 %collective-permute-start.23 = (bf16[256,256]{1,0:T(8,128)(2,1)}, bf16[256,256]{1,0:T(8,128)(2,1)S(1)}, u32[]{:S(2)}, u32[]{:S(2)}) collective-permute-start(bf16[256,256]{1,0:T(8,128)(2,1)} %broadcast_select_fusion.4), channel_id=1, source_target_pairs={{0,2},{1,3},{2,0},{3,1},{4,6},{5,7},{6,4},{7,5},{8,10},{9,11},{10,... | collective-permute-start | bytes 393224 | tf_op jit(solution)/shard_map/ppermute | solution.py:48
  60.9 2.9 %collective-permute-done.23 = bf16[256,256]{1,0:T(8,128)(2,1)S(1)} collective-permute-done((bf16[256,256]{1,0:T(8,128)(2,1)}, bf16[256,256]{1,0:T(8,128)(2,1)S(1)}, u32[]{:S(2)}, u32[]{:S(2)}) %collective-permute-start.23) | collective-permute-done | bytes 131104 | tf_op jit(solution)/shard_map/ppermute | solution.py:48
  63.8 1.6 %collective-permute-start.21 = (bf16[256,256]{1,0:T(8,128)(2,1)}, bf16[256,256]{1,0:T(8,128)(2,1)S(1)}, u32[]{:S(2)}, u32[]{:S(2)}) collective-permute-start(bf16[256,256]{1,0:T(8,128)(2,1)} %broadcast_select_fusion.4), channel_id=1, source_target_pairs={{0,1},{1,0},{2,3},{3,2},{4,5},{5,4},{6,7},{7,6},{8,9},{9,8},{10,11... | collective-permute-start | bytes 393224 | tf_op jit(solution)/shard_map/ppermute | solution.py:48
  65.5 1.2 %select_select_fusion = (bf16[512,256]{1,0:T(8,128)(2,1)S(1)}, bf16[512,256]{1,0:T(8,128)(2,1)S(1)}) fusion(bf16[512,256]{1,0:T(8,128)(2,1)} %copy-done.10, bf16[512,256]{1,0:T(8,128)(2,1)} %copy-done.12, bf16[512,256]{1,0:T(8,128)(2,1)} %copy-done.11, bf16[512,256]{1,0:T(8,128)(2,1)} %copy-done.13, pred[]{:T(512)S(6)} %eq.29, pred[]{:T(512)S(6)} %eq.14, ...), kind=kLoop, calls=%fused_computation.8 | loop fusion | flops 786432 | bytes 1572868 | tf_op jit(solution)/shard_map/jit(_where)/select_n | solution.py:385
  67.0 2.2 %collective-permute-done.21 = bf16[256,256]{1,0:T(8,128)(2,1)S(1)} collective-permute-done((bf16[256,256]{1,0:T(8,128)(2,1)}, bf16[256,256]{1,0:T(8,128)(2,1)S(1)}, u32[]{:S(2)}, u32[]{:S(2)}) %collective-permute-start.21) | collective-permute-done | bytes 131104 | tf_op jit(solution)/shard_map/ppermute | solution.py:48
  69.2 1.0 %select_select_fusion.3 = (bf16[256,256]{1,0:T(8,128)(2,1)S(1)}, bf16[256,256]{1,0:T(8,128)(2,1)S(1)}) fusion(bf16[256,256]{1,0:T(8,128)(2,1)} %broadcast_select_fusion.4, bf16[256,256]{1,0:T(8,128)(2,1)S(1)} %collective-permute-done.21, bf16[256,256]{1,0:T(8,128)(2,1)S(1)} %collective-permute-done.22, bf16[256,256]{1,0:T(8,128)(2,1)} %copy-done.14, ...), kind=kLoop, calls=%fused_computation.17 | loop fusion | flops 393216 | bytes 786436 | tf_op jit(solution)/shard_map/jit(_where)/select_n | solution.py:384
  71.3 1.2 %slice_select_fusion.1 = bf16[128,1536]{1,0:T(8,128)(2,1)S(1)} fusion(bf16[128,3072]{1,0:T(8,128)(2,1)} %collective-permute-done.18.refs_3_, pred[]{:T(512)S(6)} %eq.12), kind=kLoop, calls=%fused_computation.4 | loop fusion | flops 196608 | bytes 1179649 | tf_op jit(solution)/shard_map/jit(_where)/select_n | solution.py:390
  72.6 1.2 %collective-permute-start.25 = (bf16[128,1536]{1,0:T(8,128)(2,1)S(1)}, bf16[128,1536]{1,0:T(8,128)(2,1)S(1)}, u32[]{:S(2)}, u32[]{:S(2)}) collective-permute-start(bf16[128,1536]{1,0:T(8,128)(2,1)S(1)} %slice_select_fusion.1), channel_id=1, source_target_pairs={{0,32},{4,228},{8,40},{12,236},{16,48},{20,244},{24,56},{28,252},{... | collective-permute-start | bytes 1179656 | tf_op jit(solution)/shard_map/ppermute | solution.py:52
  73.9 2.5 %collective-permute-start.24 = (bf16[256,1024]{1,0:T(8,128)(2,1)S(1)}, bf16[256,1024]{1,0:T(8,128)(2,1)S(1)}, u32[]{:S(2)}, u32[]{:S(2)}) collective-permute-start(bf16[256,1024]{1,0:T(8,128)(2,1)S(1)} %slice_select_fusion), channel_id=1, source_target_pairs={{0,8},{4,28},{8,16},{12,4},{16,24},{20,12},{24,0},{28,20},{32,40},... | collective-permute-start | bytes 1572872 | tf_op jit(solution)/shard_map/ppermute | solution.py:52
  76.6 4.5 %factor.1 = (bf16[512,256]{1,0:T(8,128)(2,1)S(1)}, bf16[512,256]{1,0:T(8,128)(2,1)S(1)}, bf16[256,256]{1,0:T(8,128)(2,1)S(1)}, bf16[512,256]{1,0:T(8,128)(2,1)S(1)}) custom-call(s32[2]{0:T(128)S(1)} %copy-done.7, s32[2,256]{1,0:T(2,128)S(1)} %copy-done.9, bf16[512,256]{1,0:T(8,128)(2,1)S(1)} %get-tuple-element.100.s0_ref, ...), custom_call_target="tpu_custom_call" | custom-call | flops 6442450944 | bytes 4194304 | tf_op jit(solution)/shard_map/factor/pallas_call | solution.py:244
  81.1 3.5 %select.6 = (bf16[256,3072]{1,0:T(8,128)(2,1)S(1)}, bf16[256,3072]{1,0:T(8,128)(2,1)S(1)}) custom-call(bf16[512,512]{1,0:T(8,128)(2,1)S(1)} %copy-done.1, bf16[128,3072]{1,0:T(8,128)(2,1)S(1)} %pad_maximum_fusion.refs_0_, bf16[128,3072]{1,0:T(8,128)(2,1)S(1)} %copy-done.3, bf16[128,3072]{1,0:T(8,128)(2,1)} %collective-permute-done.12.refs_2_, ...), custom_call_target="tpu_custom_call" | custom-call | flops 1409286144 | bytes 1048576 | tf_op jit(solution)/shard_map/select/pallas_call | solution.py:302
  85.2 1.2 %select.7 = (bf16[256,2048]{1,0:T(8,128)(2,1)S(1)}, bf16[256,2048]{1,0:T(8,128)(2,1)S(1)}) custom-call(bf16[512,512]{1,0:T(8,128)(2,1)S(1)} %copy-done, bf16[256,2048]{1,0:T(8,128)(2,1)S(1)} %assemble.1.refs_0_, bf16[256,2048]{1,0:T(8,128)(2,1)S(1)} %collective-permute-done.19.refs_1_, bf16[256,2048]{1,0:T(8,128)(2,1)S(1)} %collective-permute-done.28.refs_2_), custom_call_target="tpu_custom_call" | custom-call | flops 805306368 | bytes 1048576 | tf_op jit(solution)/shard_map/select/pallas_call | solution.py:302
  87.2 7.4 %update.1 = bf16[512,5120]{1,0:T(8,128)(2,1)} custom-call(s32[2]{0:T(128)S(1)} %copy-done.7, bf16[512,512]{1,0:T(8,128)(2,1)S(1)} %copy-done, bf16[512,512]{1,0:T(8,128)(2,1)S(1)} %copy-done.1, bf16[256,2048]{1,0:T(8,128)(2,1)S(1)} %get-tuple-element.86.uz0, bf16[256,2048]{1,0:T(8,128)(2,1)S(1)} %get-tuple-element.87.uz1, ...), custom_call_target="tpu_custom_call" | custom-call | flops 4026531840 | bytes 10485760 | tf_op jit(solution)/shard_map/update/pallas_call | solution.py:360
  (102 shorter events, 12.2 us)
Async XLA Ops:
  4.2 4.6 %collective-permute-start = (bf16[32,5120]{1,0:T(8,128)(2,1)S(1)}, bf16[32,5120]{1,0:T(8,128)(2,1)S(1)}, u32[]{:S(2)}, u32[]{:S(2)}) collective-permute-start(bf16[32,5120]{1,0:T(8,128)(2,1)S(1)} %pick.1), channel_id=1, source_target_pairs={{0,4},{4,0},{8,12},{12,8},{16,20},{20,16},{24,28},{28,24},{32,36},... | collective-permute-start | bytes 983048 | tf_op jit(solution)/shard_map/ppermute | solution.py:52
  8.9 9.8 %collective-permute-start.2 = (bf16[32,3072]{1,0:T(8,128)(2,1)S(1)}, bf16[32,3072]{1,0:T(8,128)(2,1)S(1)}, u32[]{:S(2)}, u32[]{:S(2)}) collective-permute-start(bf16[32,3072]{1,0:T(8,128)(2,1)S(1)} %slice.82), channel_id=1, source_target_pairs={{0,8},{4,28},{8,16},{12,4},{16,24},{20,12},{24,0},{28,20},{32,40},... | collective-permute-start | bytes 589832 | tf_op jit(solution)/shard_map/ppermute | solution.py:52
  10.0 8.7 %collective-permute-start.1 = (bf16[32,2048]{1,0:T(8,128)(2,1)S(1)}, bf16[32,2048]{1,0:T(8,128)(2,1)S(1)}, u32[]{:S(2)}, u32[]{:S(2)}) collective-permute-start(bf16[32,2048]{1,0:T(8,128)(2,1)S(1)} %slice.81.near_ref), channel_id=1, source_target_pairs={{0,32},{4,228},{8,40},{12,236},{16,48},{20,244},{24,56},{28,252},{... | collective-permute-start | bytes 393224 | tf_op jit(solution)/shard_map/ppermute | solution.py:52
  18.7 5.4 %collective-permute-start.5 = (bf16[32,3072]{1,0:T(8,128)(2,1)S(1)}, bf16[32,3072]{1,0:T(8,128)(2,1)S(1)}, u32[]{:S(2)}, u32[]{:S(2)}) collective-permute-start(bf16[32,3072]{1,0:T(8,128)(2,1)S(1)} %collective-permute-done.2), channel_id=1, source_target_pairs={{0,4},{4,0},{8,12},{12,8},{16,20},{20,16},{24,28},{28,24},{32,36},... | collective-permute-start | bytes 589832 | tf_op jit(solution)/shard_map/ppermute | solution.py:52
  18.8 5.3 %collective-permute-start.4 = (bf16[32,3072]{1,0:T(8,128)(2,1)S(1)}, bf16[32,3072]{1,0:T(8,128)(2,1)S(1)}, u32[]{:S(2)}, u32[]{:S(2)}) collective-permute-start(bf16[32,3072]{1,0:T(8,128)(2,1)S(1)} %collective-permute-done.2), channel_id=1, source_target_pairs={{0,8},{4,28},{8,16},{12,4},{16,24},{20,12},{24,0},{28,20},{32,40},... | collective-permute-start | bytes 589832 | tf_op jit(solution)/shard_map/ppermute | solution.py:52
  19.4 4.6 %collective-permute-start.3 = (bf16[32,2048]{1,0:T(8,128)(2,1)S(1)}, bf16[32,2048]{1,0:T(8,128)(2,1)S(1)}, u32[]{:S(2)}, u32[]{:S(2)}) collective-permute-start(bf16[32,2048]{1,0:T(8,128)(2,1)S(1)} %collective-permute-done.1), channel_id=1, source_target_pairs={{0,32},{4,228},{8,40},{12,236},{16,48},{20,244},{24,56},{28,252},{... | collective-permute-start | bytes 393224 | tf_op jit(solution)/shard_map/ppermute | solution.py:52
  21.6 7.8 %collective-permute-start.8 = (bf16[512,256]{1,0:T(8,128)(2,1)S(1)}, bf16[512,256]{1,0:T(8,128)(2,1)S(1)}, u32[]{:S(2)}, u32[]{:S(2)}) collective-permute-start(bf16[512,256]{1,0:T(8,128)(2,1)S(1)} %slice.63), channel_id=1, source_target_pairs={{0,3},{1,2},{2,1},{3,0},{4,7},{5,6},{6,5},{7,4},{8,11},{9,10},{10,... | collective-permute-start | bytes 786440 | tf_op jit(solution)/shard_map/ppermute | solution.py:48
  24.0 7.1 %collective-permute-start.7 = (bf16[512,256]{1,0:T(8,128)(2,1)S(1)}, bf16[512,256]{1,0:T(8,128)(2,1)S(1)}, u32[]{:S(2)}, u32[]{:S(2)}) collective-permute-start(bf16[512,256]{1,0:T(8,128)(2,1)S(1)} %slice.63), channel_id=1, source_target_pairs={{0,1},{1,0},{2,3},{3,2},{4,5},{5,4},{6,7},{7,6},{8,9},{9,8},{10,11... | collective-permute-start | bytes 786440 | tf_op jit(solution)/shard_map/ppermute | solution.py:48
  24.1 7.1 %collective-permute-start.6 = (bf16[32,2048]{1,0:T(8,128)(2,1)S(1)}, bf16[32,2048]{1,0:T(8,128)(2,1)S(1)}, u32[]{:S(2)}, u32[]{:S(2)}) collective-permute-start(bf16[32,2048]{1,0:T(8,128)(2,1)S(1)} %collective-permute-done.3), channel_id=1, source_target_pairs={{0,32},{4,228},{8,40},{12,236},{16,48},{20,244},{24,56},{28,252},{... | collective-permute-start | bytes 393224 | tf_op jit(solution)/shard_map/ppermute | solution.py:52
  26.9 23.8 %copy-start.7 = (s32[2]{0:T(128)S(1)}, s32[2]{0:T(128)}, u32[]{:S(2)}) copy-start(s32[2]{0:T(128)} %copy-done.6) | copy-start | bytes 28
  27.0 12.6 %collective-permute-start.11 = (bf16[128,3072]{1,0:T(8,128)(2,1)S(1)}, bf16[128,3072]{1,0:T(8,128)(2,1)S(1)}, u32[]{:S(2)}, u32[]{:S(2)}) collective-permute-start(bf16[128,3072]{1,0:T(8,128)(2,1)S(1)} %pad_maximum_fusion.refs_0_), channel_id=1, source_target_pairs={{0,32},{4,228},{8,40},{12,236},{16,48},{20,244},{24,56},{28,252},{... | collective-permute-start | bytes 2359304 | tf_op jit(solution)/shard_map/ppermute | solution.py:52
  31.2 8.4 %collective-permute-start.10 = (bf16[96,2048]{1,0:T(8,128)(2,1)S(1)}, bf16[96,2048]{1,0:T(8,128)(2,1)S(1)}, u32[]{:S(2)}, u32[]{:S(2)}) collective-permute-start(bf16[96,2048]{1,0:T(8,128)(2,1)S(1)} %constant_dynamic-update-slice_fusion.own_ref), channel_id=1, source_target_pairs={{0,4},{4,0},{8,12},{12,8},{16,20},{20,16},{24,28},{28,24},{32,36},... | collective-permute-start | bytes 1179656 | tf_op jit(solution)/shard_map/ppermute | solution.py:52
  32.4 7.2 %collective-permute-start.9 = (bf16[32,2048]{1,0:T(8,128)(2,1)S(1)}, bf16[32,2048]{1,0:T(8,128)(2,1)S(1)}, u32[]{:S(2)}, u32[]{:S(2)}) collective-permute-start(bf16[32,2048]{1,0:T(8,128)(2,1)S(1)} %collective-permute-done.6), channel_id=1, source_target_pairs={{0,32},{4,228},{8,40},{12,236},{16,48},{20,244},{24,56},{28,252},{... | collective-permute-start | bytes 393224 | tf_op jit(solution)/shard_map/ppermute | solution.py:52
  33.6 12.1 %collective-permute-start.16 = (bf16[512,256]{1,0:T(8,128)(2,1)S(1)}, bf16[512,256]{1,0:T(8,128)(2,1)S(1)}, u32[]{:S(2)}, u32[]{:S(2)}) collective-permute-start(bf16[512,256]{1,0:T(8,128)(2,1)S(1)} %collective-permute-done.8), channel_id=1, source_target_pairs={{0,1},{1,0},{2,3},{3,2},{4,5},{5,4},{6,7},{7,6},{8,9},{9,8},{10,11... | collective-permute-start | bytes 786440 | tf_op jit(solution)/shard_map/ppermute | solution.py:48
  39.6 13.8 %collective-permute-start.13 = (bf16[128,3072]{1,0:T(8,128)(2,1)S(1)}, bf16[128,3072]{1,0:T(8,128)(2,1)S(1)}, u32[]{:S(2)}, u32[]{:S(2)}) collective-permute-start(bf16[128,3072]{1,0:T(8,128)(2,1)S(1)} %collective-permute-done.11.refs_1_), channel_id=1, source_target_pairs={{0,4},{4,0},{8,12},{12,8},{16,20},{20,16},{24,28},{28,24},{32,36},... | collective-permute-start | bytes 2359304 | tf_op jit(solution)/shard_map/ppermute | solution.py:52
  42.3 12.1 %collective-permute-start.12 = (bf16[128,3072]{1,0:T(8,128)(2,1)S(1)}, bf16[128,3072]{1,0:T(8,128)(2,1)}, u32[]{:S(2)}, u32[]{:S(2)}) collective-permute-start(bf16[128,3072]{1,0:T(8,128)(2,1)S(1)} %collective-permute-done.11.refs_1_), channel_id=1, source_target_pairs={{0,32},{4,228},{8,40},{12,236},{16,48},{20,244},{24,56},{28,252},{... | collective-permute-start | bytes 2359304 | tf_op jit(solution)/shard_map/ppermute | solution.py:52
  43.0 7.4 %collective-permute-start.14 = (bf16[256,256]{1,0:T(8,128)(2,1)S(1)}, bf16[256,256]{1,0:T(8,128)(2,1)S(1)}, u32[]{:S(2)}, u32[]{:S(2)}) collective-permute-start(bf16[256,256]{1,0:T(8,128)(2,1)S(1)} %constant_dynamic-update-slice_fusion.3.refs_0_), channel_id=1, source_target_pairs={{0,8},{4,28},{8,16},{12,4},{16,24},{20,12},{24,0},{28,20},{32,40},... | collective-permute-start | bytes 393224 | tf_op jit(solution)/shard_map/ppermute | solution.py:52
  45.4 5.0 %collective-permute-start.15 = (bf16[256,128]{1,0:T(8,128)(2,1)S(1)}, bf16[256,128]{1,0:T(8,128)(2,1)S(1)}, u32[]{:S(2)}, u32[]{:S(2)}) collective-permute-start(bf16[256,128]{1,0:T(8,128)(2,1)S(1)} %slice_select_fusion.2), channel_id=1, source_target_pairs={{0,16},{4,20},{8,24},{12,28},{16,0},{20,4},{24,8},{28,12},{32,48},... | collective-permute-start | bytes 196616 | tf_op jit(solution)/shard_map/ppermute | solution.py:52
  50.4 2.7 %collective-permute-start.17 = (bf16[256,384]{1,0:T(8,128)(2,1)S(1)}, bf16[256,384]{1,0:T(8,128)(2,1)S(1)}, u32[]{:S(2)}, u32[]{:S(2)}) collective-permute-start(bf16[256,384]{1,0:T(8,128)(2,1)S(1)} %pad_maximum_fusion.3), channel_id=1, source_target_pairs={{0,4},{4,0},{8,12},{12,8},{16,20},{20,16},{24,28},{28,24},{32,36},... | collective-permute-start | bytes 589832 | tf_op jit(solution)/shard_map/ppermute | solution.py:52
  51.3 18.9 %collective-permute-start.19 = (bf16[256,2048]{1,0:T(8,128)(2,1)S(1)}, bf16[256,2048]{1,0:T(8,128)(2,1)S(1)}, u32[]{:S(2)}, u32[]{:S(2)}) collective-permute-start(bf16[256,2048]{1,0:T(8,128)(2,1)S(1)} %assemble.1.refs_0_), channel_id=1, source_target_pairs={{0,8},{4,28},{8,16},{12,4},{16,24},{20,12},{24,0},{28,20},{32,40},... | collective-permute-start | bytes 3145736 | tf_op jit(solution)/shard_map/ppermute | solution.py:52
  54.4 15.9 %collective-permute-start.20 = (bf16[128,3072]{1,0:T(8,128)(2,1)}, bf16[128,3072]{1,0:T(8,128)(2,1)}, u32[]{:S(2)}, u32[]{:S(2)}) collective-permute-start(bf16[128,3072]{1,0:T(8,128)(2,1)} %collective-permute-done.12.refs_2_), channel_id=1, source_target_pairs={{0,4},{4,0},{8,12},{12,8},{16,20},{20,16},{24,28},{28,24},{32,36},... | collective-permute-start | bytes 2359304 | tf_op jit(solution)/shard_map/ppermute | solution.py:52
  55.7 14.6 %collective-permute-start.18 = (bf16[128,3072]{1,0:T(8,128)(2,1)}, bf16[128,3072]{1,0:T(8,128)(2,1)}, u32[]{:S(2)}, u32[]{:S(2)}) collective-permute-start(bf16[128,3072]{1,0:T(8,128)(2,1)} %collective-permute-done.12.refs_2_), channel_id=1, source_target_pairs={{0,32},{4,228},{8,40},{12,236},{16,48},{20,244},{24,56},{28,252},{... | collective-permute-start | bytes 2359304 | tf_op jit(solution)/shard_map/ppermute | solution.py:52
  57.3 6.5 %collective-permute-start.23 = (bf16[256,256]{1,0:T(8,128)(2,1)}, bf16[256,256]{1,0:T(8,128)(2,1)S(1)}, u32[]{:S(2)}, u32[]{:S(2)}) collective-permute-start(bf16[256,256]{1,0:T(8,128)(2,1)} %broadcast_select_fusion.4), channel_id=1, source_target_pairs={{0,2},{1,3},{2,0},{3,1},{4,6},{5,7},{6,4},{7,5},{8,10},{9,11},{10,... | collective-permute-start | bytes 393224 | tf_op jit(solution)/shard_map/ppermute | solution.py:48
  60.1 6.9 %collective-permute-start.22 = (bf16[256,256]{1,0:T(8,128)(2,1)}, bf16[256,256]{1,0:T(8,128)(2,1)S(1)}, u32[]{:S(2)}, u32[]{:S(2)}) collective-permute-start(bf16[256,256]{1,0:T(8,128)(2,1)} %broadcast_select_fusion.4), channel_id=1, source_target_pairs={{0,3},{1,2},{2,1},{3,0},{4,7},{5,6},{6,5},{7,4},{8,11},{9,10},{10,... | collective-permute-start | bytes 393224 | tf_op jit(solution)/shard_map/ppermute | solution.py:48
  63.8 5.4 %collective-permute-start.21 = (bf16[256,256]{1,0:T(8,128)(2,1)}, bf16[256,256]{1,0:T(8,128)(2,1)S(1)}, u32[]{:S(2)}, u32[]{:S(2)}) collective-permute-start(bf16[256,256]{1,0:T(8,128)(2,1)} %broadcast_select_fusion.4), channel_id=1, source_target_pairs={{0,1},{1,0},{2,3},{3,2},{4,5},{5,4},{6,7},{7,6},{8,9},{9,8},{10,11... | collective-permute-start | bytes 393224 | tf_op jit(solution)/shard_map/ppermute | solution.py:48
  70.3 6.1 %collective-permute-start.26 = (bf16[256,512]{1,0:T(8,128)(2,1)S(1)}, bf16[256,512]{1,0:T(8,128)(2,1)S(1)}, u32[]{:S(2)}, u32[]{:S(2)}) collective-permute-start(bf16[256,512]{1,0:T(8,128)(2,1)S(1)} %pad_maximum_fusion.2), channel_id=1, source_target_pairs={{0,4},{4,0},{8,12},{12,8},{16,20},{20,16},{24,28},{28,24},{32,36},... | collective-permute-start | bytes 786440 | tf_op jit(solution)/shard_map/ppermute | solution.py:52
  72.4 8.6 %collective-permute-start.27 = (bf16[128,3072]{1,0:T(8,128)(2,1)}, bf16[128,3072]{1,0:T(8,128)(2,1)S(1)}, u32[]{:S(2)}, u32[]{:S(2)}) collective-permute-start(bf16[128,3072]{1,0:T(8,128)(2,1)} %collective-permute-done.18.refs_3_), channel_id=1, source_target_pairs={{0,4},{4,0},{8,12},{12,8},{16,20},{20,16},{24,28},{28,24},{32,36},... | collective-permute-start | bytes 2359304 | tf_op jit(solution)/shard_map/ppermute | solution.py:52
  72.6 12.0 %collective-permute-start.25 = (bf16[128,1536]{1,0:T(8,128)(2,1)S(1)}, bf16[128,1536]{1,0:T(8,128)(2,1)S(1)}, u32[]{:S(2)}, u32[]{:S(2)}) collective-permute-start(bf16[128,1536]{1,0:T(8,128)(2,1)S(1)} %slice_select_fusion.1), channel_id=1, source_target_pairs={{0,32},{4,228},{8,40},{12,236},{16,48},{20,244},{24,56},{28,252},{... | collective-permute-start | bytes 1179656 | tf_op jit(solution)/shard_map/ppermute | solution.py:52
  73.8 11.4 %collective-permute-start.28 = (bf16[256,2048]{1,0:T(8,128)(2,1)S(1)}, bf16[256,2048]{1,0:T(8,128)(2,1)S(1)}, u32[]{:S(2)}, u32[]{:S(2)}) collective-permute-start(bf16[256,2048]{1,0:T(8,128)(2,1)S(1)} %collective-permute-done.19.refs_1_), channel_id=1, source_target_pairs={{0,4},{4,0},{8,12},{12,8},{16,20},{20,16},{24,28},{28,24},{32,36},... | collective-permute-start | bytes 3145736 | tf_op jit(solution)/shard_map/ppermute | solution.py:52
  73.9 10.6 %collective-permute-start.24 = (bf16[256,1024]{1,0:T(8,128)(2,1)S(1)}, bf16[256,1024]{1,0:T(8,128)(2,1)S(1)}, u32[]{:S(2)}, u32[]{:S(2)}) collective-permute-start(bf16[256,1024]{1,0:T(8,128)(2,1)S(1)} %slice_select_fusion), channel_id=1, source_target_pairs={{0,8},{4,28},{8,16},{12,4},{16,24},{20,12},{24,0},{28,20},{32,40},... | collective-permute-start | bytes 1572872 | tf_op jit(solution)/shard_map/ppermute | solution.py:52
  84.6 2.6 %collective-permute-start.29 = (bf16[256,1024]{1,0:T(8,128)(2,1)S(1)}, bf16[256,1024]{1,0:T(8,128)(2,1)S(1)}, u32[]{:S(2)}, u32[]{:S(2)}) collective-permute-start(bf16[256,1024]{1,0:T(8,128)(2,1)S(1)} %collective-permute-done.24.z_mine), channel_id=1, source_target_pairs={{0,4},{4,0},{8,12},{12,8},{16,20},{20,16},{24,28},{28,24},{32,36},... | collective-permute-start | bytes 1572872 | tf_op jit(solution)/shard_map/ppermute | solution.py:52
  85.0 2.1 %collective-permute-start.30 = (bf16[128,1536]{1,0:T(8,128)(2,1)S(1)}, bf16[128,1536]{1,0:T(8,128)(2,1)S(1)}, u32[]{:S(2)}, u32[]{:S(2)}) collective-permute-start(bf16[128,1536]{1,0:T(8,128)(2,1)S(1)} %collective-permute-done.25.y_mine), channel_id=1, source_target_pairs={{0,4},{4,0},{8,12},{12,8},{16,20},{20,16},{24,28},{28,24},{32,36},... | collective-permute-start | bytes 1179656 | tf_op jit(solution)/shard_map/ppermute | solution.py:52
  (16 other events, 110.9 us)

commit v4 on v3

--- a/solution.py
+++ b/solution.py
@@ -283,25 +283,29 @@
 
 
 def select_kernel(spans, hot_ref, *refs):
-    blocks, (u0_ref, u1_ref) = refs[:-2], refs[-2:]
-    width = u0_ref.shape[1]
+    refs, outs = refs[:-2], refs[-2:]
+    blocks, earlier = refs[: len(spans)], refs[len(spans) :]
+    width = outs[0].shape[1]
     step = step_of(width)
     for at in range(0, width, step):
         cols = slice(at, at + step)
         parts = [block[:, cols] for block in blocks]
-        for which, out in ((0, u0_ref), (1, u1_ref)):
+        for which, out in enumerate(outs):
             rows = slice(which * NB, (which + 1) * NB)
             hot = jnp.concatenate([hot_ref[rows, a:b] for a, b in spans], axis=1)
-            out[:, cols] = dot(hot, list_rows(parts, which)).astype(BF16)
-
-
-def select(hot, blocks, spans):
+            found = dot(hot, list_rows(parts, which))
+            if earlier:
+                found = found + earlier[which][:, cols].astype(F32)
+            out[:, cols] = found.astype(BF16)
+
+
+def select(hot, blocks, spans, earlier=()):
     width = blocks[0].shape[1]
     shape = jax.ShapeDtypeStruct((NB, width), BF16)
     slots = sum(b - a for a, b in spans)
     return pl.pallas_call(
         functools.partial(select_kernel, spans),
-        in_specs=[VMEM] * (1 + len(blocks)),
+        in_specs=[VMEM] * (1 + len(blocks) + len(earlier)),
         out_specs=[VMEM, VMEM],
         out_shape=[shape, shape],
         compiler_params=PARAMS,
@@ -309,7 +313,7 @@
             flops=2 * 2 * NB * slots * width, bytes_accessed=2**20, transcendentals=0
         ),
         name="select",
-    )(hot, *blocks)
+    )(hot, *blocks, *earlier)
 
 
 def update_kernel(
@@ -426,16 +430,18 @@
     part = jnp.where(even, entries[0], entries[1])
     part = panels(part, over(part, NEAR), over(part, FAR), over(part, SKIP))
     part = jnp.concatenate(part, axis=1)
-    y3, z1, o2, part = both(send(y2, ALONG_Z), z1, send(y2, PAIR), part)
+    o2 = send(y2, PAIR)
+    n = YN * SLOTS
+    spans = [(i * n, (i + 1) * n) for i in (0, 1, 2, 6, 7)]
+    uy = select(hot_y, [yf, y1, y2, o2, o1], spans)
+    y3, z1, part, *uy = both(send(y2, ALONG_Z), z1, part, *uy)
 
     rest = send(part, PAIR)
     uppers = jnp.concatenate([jnp.where(even, part, rest), jnp.where(even, rest, part)], axis=0)
     uppers = [uppers[:, :NB], uppers[:, NB:]]
     left0, left1, lower, fin = factor(ids, pivots, uppers, pan0, pan1)
     p1, o3 = send(z1, PAIR), send(y3, PAIR)
-    n = YN * SLOTS
-    spans = [(i * n, (i + 1) * n) for i in (0, 1, 2, 3, 5, 6, 7)]
-    uy = select(hot_y, [yf, y1, y2, y3, o3, o2, o1], spans)
+    uy = select(hot_y, [y3, o3], [(3 * n, 4 * n), (5 * n, 6 * n)], uy)
     z2, y4, left0, *uy = both(send(half(z1), ALONG_Y), send(half(y3), ALONG_Z), left0, *uy)
     p2, o4 = send(z2, PAIR), send(y4, PAIR)
     uz = select(after(hot_z, z2), [zf, z1, p1], [(0, k), (k, 2 * k), (3 * k, 4 * k)])

time: 95 us -> 96.1 us (1.012)
  Pallas kernels: 22.9 us -> 24.8 us
  starting transfers between devices: 42.4 us -> 43.7 us
  waiting for transfers between devices: 21.5 us -> 20.3 us
    pallas_call x3 -> x4, Pallas kernels: 5.01 us -> 6.92 us  [select(): pl.pallas_call(functools.partial(select_kernel, spans), in_specs=[VMEM] *...]
    ppermute x25, starting transfers between devices: 33.9 us -> 35.6 us  [send(): return lax.ppermute(array, 'prow', pairs)]
    ppermute x6, waiting for transfers between devices: 9.46 us -> 8.16 us  [over(): return lax.ppermute(array, 'pcol', pairs)]
  transfers between devices with their start and end apart: 31 -> 31, of which waited for: 9 -> 9; matrix products, arithmetic and copies ran while one was open for 6% -> 5% of each run, Pallas kernels for 13% -> 15%
where the time goes in v4:
time: 96.1 us; the launch traced here: 95.8 us
  starting transfers between devices  43.7 us (45%)
  Pallas kernels  24.8 us (26%)
  waiting for transfers between devices  20.3 us (21%)
  other arithmetic  3.79 us (4%)
  local copies, waits for them, and re-layouts  2.67 us (3%)
    ppermute x25, starting transfers between devices, send(): return lax.ppermute(array, 'prow', pairs)  35.6 us
    ppermute x25, waiting for transfers between devices, send(): return lax.ppermute(array, 'prow', pairs)  12.1 us
    ppermute x6, waiting for transfers between devices, over(): return lax.ppermute(array, 'pcol', pairs)  8.16 us
    ppermute x6, starting transfers between devices, over(): return lax.ppermute(array, 'pcol', pairs)  8.09 us
    pallas_call x1, Pallas kernels, update(): pl.pallas_call(functools.partial(update_kernel, [slice(*span) for span in...  7.37 us
    pallas_call x4, Pallas kernels, select(): pl.pallas_call(functools.partial(select_kernel, spans), in_specs=[VMEM] *...  6.92 us
    pallas_call x1, Pallas kernels, factor(): pl.pallas_call(factor_kernel, in_specs=[SMEM] + [VMEM] * 5, out_specs=[VM...  4.46 us
    pallas_call x1, Pallas kernels, pick(): pl.pallas_call(functools.partial(pick_kernel, chunk), in_specs=[SMEM, VME...  3.4 us
  transfers between devices with their start and end apart: 31, of which 9 were waited for; matrix products, arithmetic and copies ran while one was open for 5% of the time, Pallas kernels for 15%

profile of v4, /device:TPU:1, one launch (start us, length us, event | category | flops | bytes accessed | tf_op | source)
XLA Modules:
  0.0 95.8 jit_solution(6080485821025763318)
XLA Ops:
  0.8 3.4 %pick.1 = bf16[32,5120]{1,0:T(8,128)(2,1)S(1)} custom-call(s32[2]{0:T(128)S(1)} %pad_add_fusion.ids, s32[2,256]{1,0:T(2,128)S(1)} %copy-done.10, bf16[512,5120]{1,0:T(8,128)(2,1)} %a_ref.1), custom_call_target="tpu_custom_call" | custom-call | flops 167772160 | bytes 10485760 | tf_op jit(solution)/shard_map/pick/pallas_call | solution.py:165
  4.2 3.3 %collective-permute-start = (bf16[32,5120]{1,0:T(8,128)(2,1)S(1)}, bf16[32,5120]{1,0:T(8,128)(2,1)S(1)}, u32[]{:S(2)}, u32[]{:S(2)}) collective-permute-start(bf16[32,5120]{1,0:T(8,128)(2,1)S(1)} %pick.1), channel_id=1, source_target_pairs={{0,4},{4,0},{8,12},{12,8},{16,20},{20,16},{24,28},{28,24},{32,36},... | collective-permute-start | bytes 983048 | tf_op jit(solution)/shard_map/ppermute | solution.py:52
  7.5 1.3 %collective-permute-done = bf16[32,5120]{1,0:T(8,128)(2,1)S(1)} collective-permute-done((bf16[32,5120]{1,0:T(8,128)(2,1)S(1)}, bf16[32,5120]{1,0:T(8,128)(2,1)S(1)}, u32[]{:S(2)}, u32[]{:S(2)}) %collective-permute-start) | collective-permute-done | bytes 327712 | tf_op jit(solution)/shard_map/ppermute | solution.py:52
  10.0 5.7 %collective-permute-start.1 = (bf16[32,2048]{1,0:T(8,128)(2,1)S(1)}, bf16[32,2048]{1,0:T(8,128)(2,1)S(1)}, u32[]{:S(2)}, u32[]{:S(2)}) collective-permute-start(bf16[32,2048]{1,0:T(8,128)(2,1)S(1)} %slice.81.near_ref), channel_id=1, source_target_pairs={{0,32},{4,228},{8,40},{12,236},{16,48},{20,244},{24,56},{28,252},{... | collective-permute-start | bytes 393224 | tf_op jit(solution)/shard_map/ppermute | solution.py:52
  16.6 2.1 %maps.1 = (bf16[512,512]{1,0:T(8,128)(2,1)}, bf16[512,512]{1,0:T(8,128)(2,1)}) custom-call(s32[2]{0:T(128)} %copy-done.8, s32[2,256]{1,0:T(2,128)} %piv_ref.5), custom_call_target="tpu_custom_call" | custom-call | flops 1073741824 | bytes 4194304 | tf_op jit(solution)/shard_map/maps/pallas_call | solution.py:193
  19.4 2.1 %collective-permute-start.3 = (bf16[32,2048]{1,0:T(8,128)(2,1)S(1)}, bf16[32,2048]{1,0:T(8,128)(2,1)S(1)}, u32[]{:S(2)}, u32[]{:S(2)}) collective-permute-start(bf16[32,2048]{1,0:T(8,128)(2,1)S(1)} %collective-permute-done.1), channel_id=1, source_target_pairs={{0,32},{4,228},{8,40},{12,236},{16,48},{20,244},{24,56},{28,252},{... | collective-permute-start | bytes 393224 | tf_op jit(solution)/shard_map/ppermute | solution.py:52
  21.6 2.5 %collective-permute-start.8 = (bf16[512,256]{1,0:T(8,128)(2,1)S(1)}, bf16[512,256]{1,0:T(8,128)(2,1)S(1)}, u32[]{:S(2)}, u32[]{:S(2)}) collective-permute-start(bf16[512,256]{1,0:T(8,128)(2,1)S(1)} %slice.63), channel_id=1, source_target_pairs={{0,3},{1,2},{2,1},{3,0},{4,7},{5,6},{6,5},{7,4},{8,11},{9,10},{10,... | collective-permute-start | bytes 786440 | tf_op jit(solution)/shard_map/ppermute | solution.py:48
  24.1 2.8 %collective-permute-start.6 = (bf16[32,2048]{1,0:T(8,128)(2,1)S(1)}, bf16[32,2048]{1,0:T(8,128)(2,1)S(1)}, u32[]{:S(2)}, u32[]{:S(2)}) collective-permute-start(bf16[32,2048]{1,0:T(8,128)(2,1)S(1)} %collective-permute-done.3), channel_id=1, source_target_pairs={{0,32},{4,228},{8,40},{12,236},{16,48},{20,244},{24,56},{28,252},{... | collective-permute-start | bytes 393224 | tf_op jit(solution)/shard_map/ppermute | solution.py:52
  27.1 2.2 %collective-permute-done.8 = bf16[512,256]{1,0:T(8,128)(2,1)S(1)} collective-permute-done((bf16[512,256]{1,0:T(8,128)(2,1)S(1)}, bf16[512,256]{1,0:T(8,128)(2,1)S(1)}, u32[]{:S(2)}, u32[]{:S(2)}) %collective-permute-start.8) | collective-permute-done | bytes 262176 | tf_op jit(solution)/shard_map/ppermute | solution.py:48
  29.3 1.8 %collective-permute-done.7 = bf16[512,256]{1,0:T(8,128)(2,1)S(1)} collective-permute-done((bf16[512,256]{1,0:T(8,128)(2,1)S(1)}, bf16[512,256]{1,0:T(8,128)(2,1)S(1)}, u32[]{:S(2)}, u32[]{:S(2)}) %collective-permute-start.7) | collective-permute-done | bytes 262176 | tf_op jit(solution)/shard_map/ppermute | solution.py:48
  31.2 1.2 %collective-permute-start.10 = (bf16[96,2048]{1,0:T(8,128)(2,1)S(1)}, bf16[96,2048]{1,0:T(8,128)(2,1)S(1)}, u32[]{:S(2)}, u32[]{:S(2)}) collective-permute-start(bf16[96,2048]{1,0:T(8,128)(2,1)S(1)} %constant_dynamic-update-slice_fusion.own_ref), channel_id=1, source_target_pairs={{0,4},{4,0},{8,12},{12,8},{16,20},{20,16},{24,28},{28,24},{32,36},... | collective-permute-start | bytes 1179656 | tf_op jit(solution)/shard_map/ppermute | solution.py:52
  32.4 1.2 %collective-permute-start.9 = (bf16[32,2048]{1,0:T(8,128)(2,1)S(1)}, bf16[32,2048]{1,0:T(8,128)(2,1)S(1)}, u32[]{:S(2)}, u32[]{:S(2)}) collective-permute-start(bf16[32,2048]{1,0:T(8,128)(2,1)S(1)} %collective-permute-done.6), channel_id=1, source_target_pairs={{0,32},{4,228},{8,40},{12,236},{16,48},{20,244},{24,56},{28,252},{... | collective-permute-start | bytes 393224 | tf_op jit(solution)/shard_map/ppermute | solution.py:52
  34.3 5.3 %collective-permute-done.9.far_ref = bf16[32,2048]{1,0:T(8,128)(2,1)S(1)} collective-permute-done((bf16[32,2048]{1,0:T(8,128)(2,1)S(1)}, bf16[32,2048]{1,0:T(8,128)(2,1)S(1)}, u32[]{:S(2)}, u32[]{:S(2)}) %collective-permute-start.9) | collective-permute-done | bytes 131104 | tf_op jit(solution)/shard_map/ppermute | solution.py:52
  39.7 2.6 %collective-permute-start.13 = (bf16[128,3072]{1,0:T(8,128)(2,1)S(1)}, bf16[128,3072]{1,0:T(8,128)(2,1)S(1)}, u32[]{:S(2)}, u32[]{:S(2)}) collective-permute-start(bf16[128,3072]{1,0:T(8,128)(2,1)S(1)} %collective-permute-done.11.refs_1_), channel_id=1, source_target_pairs={{0,4},{4,0},{8,12},{12,8},{16,20},{20,16},{24,28},{28,24},{32,36},... | collective-permute-start | bytes 2359304 | tf_op jit(solution)/shard_map/ppermute | solution.py:52
  43.0 2.4 %collective-permute-start.14 = (bf16[256,256]{1,0:T(8,128)(2,1)S(1)}, bf16[256,256]{1,0:T(8,128)(2,1)S(1)}, u32[]{:S(2)}, u32[]{:S(2)}) collective-permute-start(bf16[256,256]{1,0:T(8,128)(2,1)S(1)} %constant_dynamic-update-slice_fusion.3.refs_0_), channel_id=1, source_target_pairs={{0,8},{4,28},{8,16},{12,4},{16,24},{20,12},{24,0},{28,20},{32,40},... | collective-permute-start | bytes 393224 | tf_op jit(solution)/shard_map/ppermute | solution.py:52
  45.7 4.6 %collective-permute-done.15 = bf16[256,128]{1,0:T(8,128)(2,1)S(1)} collective-permute-done((bf16[256,128]{1,0:T(8,128)(2,1)S(1)}, bf16[256,128]{1,0:T(8,128)(2,1)S(1)}, u32[]{:S(2)}, u32[]{:S(2)}) %collective-permute-start.15) | collective-permute-done | bytes 65568 | tf_op jit(solution)/shard_map/ppermute | solution.py:52
  51.3 1.8 %collective-permute-start.19 = (bf16[256,2048]{1,0:T(8,128)(2,1)S(1)}, bf16[256,2048]{1,0:T(8,128)(2,1)S(1)}, u32[]{:S(2)}, u32[]{:S(2)}) collective-permute-start(bf16[256,2048]{1,0:T(8,128)(2,1)S(1)} %assemble.1.refs_0_), channel_id=1, source_target_pairs={{0,8},{4,28},{8,16},{12,4},{16,24},{20,12},{24,0},{28,20},{32,40},... | collective-permute-start | bytes 3145736 | tf_op jit(solution)/shard_map/ppermute | solution.py:52
  54.4 1.3 %collective-permute-start.23 = (bf16[128,3072]{1,0:T(8,128)(2,1)}, bf16[128,3072]{1,0:T(8,128)(2,1)}, u32[]{:S(2)}, u32[]{:S(2)}) collective-permute-start(bf16[128,3072]{1,0:T(8,128)(2,1)} %collective-permute-done.12.refs_2_), channel_id=1, source_target_pairs={{0,4},{4,0},{8,12},{12,8},{16,20},{20,16},{24,28},{28,24},{32,36},... | collective-permute-start | bytes 2359304 | tf_op jit(solution)/shard_map/ppermute | solution.py:52
  55.7 2.8 %collective-permute-start.22 = (bf16[256,256]{1,0:T(8,128)(2,1)S(1)}, bf16[256,256]{1,0:T(8,128)(2,1)}, u32[]{:S(2)}, u32[]{:S(2)}) collective-permute-start(bf16[256,256]{1,0:T(8,128)(2,1)S(1)} %broadcast_select_fusion.4), channel_id=1, source_target_pairs={{0,2},{1,3},{2,0},{3,1},{4,6},{5,7},{6,4},{7,5},{8,10},{9,11},{10,... | collective-permute-start | bytes 393224 | tf_op jit(solution)/shard_map/ppermute | solution.py:48
  60.3 2.2 %collective-permute-done.22 = bf16[256,256]{1,0:T(8,128)(2,1)} collective-permute-done((bf16[256,256]{1,0:T(8,128)(2,1)S(1)}, bf16[256,256]{1,0:T(8,128)(2,1)}, u32[]{:S(2)}, u32[]{:S(2)}) %collective-permute-start.22) | collective-permute-done | bytes 131104 | tf_op jit(solution)/shard_map/ppermute | solution.py:48
  62.5 1.2 %collective-permute-start.20 = (bf16[256,256]{1,0:T(8,128)(2,1)S(1)}, bf16[256,256]{1,0:T(8,128)(2,1)S(1)}, u32[]{:S(2)}, u32[]{:S(2)}) collective-permute-start(bf16[256,256]{1,0:T(8,128)(2,1)S(1)} %broadcast_select_fusion.4), channel_id=1, source_target_pairs={{0,1},{1,0},{2,3},{3,2},{4,5},{5,4},{6,7},{7,6},{8,9},{9,8},{10,11... | collective-permute-start | bytes 393224 | tf_op jit(solution)/shard_map/ppermute | solution.py:48
  63.7 1.2 %select_select_fusion = (bf16[512,256]{1,0:T(8,128)(2,1)S(1)}, bf16[512,256]{1,0:T(8,128)(2,1)S(1)}) fusion(bf16[512,256]{1,0:T(8,128)(2,1)S(1)} %slice.63, bf16[512,256]{1,0:T(8,128)(2,1)} %copy-done.13, bf16[512,256]{1,0:T(8,128)(2,1)} %copy-done.12, bf16[512,256]{1,0:T(8,128)(2,1)} %copy-done.14, pred[]{:T(512)S(6)} %eq.29, pred[]{:T(512)S(6)} %eq.14, ...), kind=kLoop, calls=%fused_computation.8 | loop fusion | flops 786432 | bytes 1572868 | tf_op jit(solution)/shard_map/jit(_where)/select_n | solution.py:389
  64.9 1.3 %collective-permute-done.21 = bf16[256,256]{1,0:T(8,128)(2,1)S(1)} collective-permute-done((bf16[256,256]{1,0:T(8,128)(2,1)S(1)}, bf16[256,256]{1,0:T(8,128)(2,1)S(1)}, u32[]{:S(2)}, u32[]{:S(2)}) %collective-permute-start.21) | collective-permute-done | bytes 131104 | tf_op jit(solution)/shard_map/ppermute | solution.py:48
  67.9 3.2 %select.7 = (bf16[256,3072]{1,0:T(8,128)(2,1)S(1)}, bf16[256,3072]{1,0:T(8,128)(2,1)S(1)}) custom-call(bf16[512,512]{1,0:T(8,128)(2,1)S(1)} %copy-done, bf16[128,3072]{1,0:T(8,128)(2,1)S(1)} %copy-done.3, bf16[128,3072]{1,0:T(8,128)(2,1)S(1)} %copy-done.5, bf16[128,3072]{1,0:T(8,128)(2,1)} %collective-permute-done.12.refs_2_, ...), custom_call_target="tpu_custom_call" | custom-call | flops 1006632960 | bytes 1048576 | tf_op jit(solution)/shard_map/select/pallas_call | solution.py:306
  71.1 1.7 %collective-permute-start.26 = (bf16[256,512]{1,0:T(8,128)(2,1)S(1)}, bf16[256,512]{1,0:T(8,128)(2,1)S(1)}, u32[]{:S(2)}, u32[]{:S(2)}) collective-permute-start(bf16[256,512]{1,0:T(8,128)(2,1)S(1)} %pad_maximum_fusion.2), channel_id=1, source_target_pairs={{0,4},{4,0},{8,12},{12,8},{16,20},{20,16},{24,28},{28,24},{32,36},... | collective-permute-start | bytes 786440 | tf_op jit(solution)/shard_map/ppermute | solution.py:52
  72.7 1.2 %slice_select_fusion.1 = bf16[128,1536]{1,0:T(8,128)(2,1)S(1)} fusion(bf16[128,3072]{1,0:T(8,128)(2,1)} %collective-permute-done.18.refs_0_, pred[]{:T(512)S(6)} %eq.12), kind=kLoop, calls=%fused_computation.4 | loop fusion | flops 196608 | bytes 1179649 | tf_op jit(solution)/shard_map/jit(_where)/select_n | solution.py:394
  75.0 2.2 %collective-permute-start.24 = (bf16[256,1024]{1,0:T(8,128)(2,1)S(1)}, bf16[256,1024]{1,0:T(8,128)(2,1)S(1)}, u32[]{:S(2)}, u32[]{:S(2)}) collective-permute-start(bf16[256,1024]{1,0:T(8,128)(2,1)S(1)} %slice_select_fusion), channel_id=1, source_target_pairs={{0,8},{4,28},{8,16},{12,4},{16,24},{20,12},{24,0},{28,20},{32,40},... | collective-permute-start | bytes 1572872 | tf_op jit(solution)/shard_map/ppermute | solution.py:52
  77.3 4.5 %factor.1 = (bf16[512,256]{1,0:T(8,128)(2,1)S(1)}, bf16[512,256]{1,0:T(8,128)(2,1)S(1)}, bf16[256,256]{1,0:T(8,128)(2,1)S(1)}, bf16[512,256]{1,0:T(8,128)(2,1)S(1)}) custom-call(s32[2]{0:T(128)S(1)} %copy-done.9, s32[2,256]{1,0:T(2,128)S(1)} %copy-done.11, bf16[512,256]{1,0:T(8,128)(2,1)S(1)} %get-tuple-element.106.s0_ref, ...), custom_call_target="tpu_custom_call" | custom-call | flops 6442450944 | bytes 4194304 | tf_op jit(solution)/shard_map/factor/pallas_call | solution.py:244
  81.8 2.2 %select.8 = (bf16[256,3072]{1,0:T(8,128)(2,1)S(1)}, bf16[256,3072]{1,0:T(8,128)(2,1)S(1)}) custom-call(bf16[512,512]{1,0:T(8,128)(2,1)S(1)} %copy-done, bf16[128,3072]{1,0:T(8,128)(2,1)} %collective-permute-done.18.refs_0_, bf16[128,3072]{1,0:T(8,128)(2,1)S(1)} %collective-permute-done.27.refs_1_, bf16[256,3072]{1,0:T(8,128)(2,1)S(1)} %get-tuple-element.86.refs_2_, ...), custom_call_target="tpu_custom_call" | custom-call | flops 402653184 | bytes 1048576 | tf_op jit(solution)/shard_map/select/pallas_call | solution.py:306
  84.0 2.2 %collective-permute-start.29 = (bf16[256,1024]{1,0:T(8,128)(2,1)S(1)}, bf16[256,1024]{1,0:T(8,128)(2,1)S(1)}, u32[]{:S(2)}, u32[]{:S(2)}) collective-permute-start(bf16[256,1024]{1,0:T(8,128)(2,1)S(1)} %collective-permute-done.24.z_mine), channel_id=1, source_target_pairs={{0,4},{4,0},{8,12},{12,8},{16,20},{20,16},{24,28},{28,24},{32,36},... | collective-permute-start | bytes 1572872 | tf_op jit(solution)/shard_map/ppermute | solution.py:52
  86.2 1.3 %select.9 = (bf16[256,2048]{1,0:T(8,128)(2,1)S(1)}, bf16[256,2048]{1,0:T(8,128)(2,1)S(1)}) custom-call(bf16[512,512]{1,0:T(8,128)(2,1)S(1)} %copy-done.1, bf16[256,2048]{1,0:T(8,128)(2,1)S(1)} %assemble.1.refs_0_, bf16[256,2048]{1,0:T(8,128)(2,1)S(1)} %collective-permute-done.19.refs_1_, bf16[256,2048]{1,0:T(8,128)(2,1)S(1)} %collective-permute-done.28.refs_2_), custom_call_target="tpu_custom_call" | custom-call | flops 805306368 | bytes 1048576 | tf_op jit(solution)/shard_map/select/pallas_call | solution.py:306
  88.3 7.4 %update.1 = bf16[512,5120]{1,0:T(8,128)(2,1)} custom-call(s32[2]{0:T(128)S(1)} %copy-done.9, bf16[512,512]{1,0:T(8,128)(2,1)S(1)} %copy-done.1, bf16[512,512]{1,0:T(8,128)(2,1)S(1)} %copy-done, bf16[256,2048]{1,0:T(8,128)(2,1)S(1)} %get-tuple-element.92.uz0, bf16[256,2048]{1,0:T(8,128)(2,1)S(1)} %get-tuple-element.93.uz1, ...), custom_call_target="tpu_custom_call" | custom-call | flops 4026531840 | bytes 10485760 | tf_op jit(solution)/shard_map/update/pallas_call | solution.py:364
  (103 shorter events, 13.3 us)
Async XLA Ops:
  4.2 4.6 %collective-permute-start = (bf16[32,5120]{1,0:T(8,128)(2,1)S(1)}, bf16[32,5120]{1,0:T(8,128)(2,1)S(1)}, u32[]{:S(2)}, u32[]{:S(2)}) collective-permute-start(bf16[32,5120]{1,0:T(8,128)(2,1)S(1)} %pick.1), channel_id=1, source_target_pairs={{0,4},{4,0},{8,12},{12,8},{16,20},{20,16},{24,28},{28,24},{32,36},... | collective-permute-start | bytes 983048 | tf_op jit(solution)/shard_map/ppermute | solution.py:52
  8.9 9.8 %collective-permute-start.2 = (bf16[32,3072]{1,0:T(8,128)(2,1)S(1)}, bf16[32,3072]{1,0:T(8,128)(2,1)S(1)}, u32[]{:S(2)}, u32[]{:S(2)}) collective-permute-start(bf16[32,3072]{1,0:T(8,128)(2,1)S(1)} %slice.82), channel_id=1, source_target_pairs={{0,8},{4,28},{8,16},{12,4},{16,24},{20,12},{24,0},{28,20},{32,40},... | collective-permute-start | bytes 589832 | tf_op jit(solution)/shard_map/ppermute | solution.py:52
  10.0 8.7 %collective-permute-start.1 = (bf16[32,2048]{1,0:T(8,128)(2,1)S(1)}, bf16[32,2048]{1,0:T(8,128)(2,1)S(1)}, u32[]{:S(2)}, u32[]{:S(2)}) collective-permute-start(bf16[32,2048]{1,0:T(8,128)(2,1)S(1)} %slice.81.near_ref), channel_id=1, source_target_pairs={{0,32},{4,228},{8,40},{12,236},{16,48},{20,244},{24,56},{28,252},{... | collective-permute-start | bytes 393224 | tf_op jit(solution)/shard_map/ppermute | solution.py:52
  18.6 5.4 %collective-permute-start.5 = (bf16[32,3072]{1,0:T(8,128)(2,1)S(1)}, bf16[32,3072]{1,0:T(8,128)(2,1)S(1)}, u32[]{:S(2)}, u32[]{:S(2)}) collective-permute-start(bf16[32,3072]{1,0:T(8,128)(2,1)S(1)} %collective-permute-done.2), channel_id=1, source_target_pairs={{0,4},{4,0},{8,12},{12,8},{16,20},{20,16},{24,28},{28,24},{32,36},... | collective-permute-start | bytes 589832 | tf_op jit(solution)/shard_map/ppermute | solution.py:52
  18.7 5.3 %collective-permute-start.4 = (bf16[32,3072]{1,0:T(8,128)(2,1)S(1)}, bf16[32,3072]{1,0:T(8,128)(2,1)S(1)}, u32[]{:S(2)}, u32[]{:S(2)}) collective-permute-start(bf16[32,3072]{1,0:T(8,128)(2,1)S(1)} %collective-permute-done.2), channel_id=1, source_target_pairs={{0,8},{4,28},{8,16},{12,4},{16,24},{20,12},{24,0},{28,20},{32,40},... | collective-permute-start | bytes 589832 | tf_op jit(solution)/shard_map/ppermute | solution.py:52
  19.4 4.6 %collective-permute-start.3 = (bf16[32,2048]{1,0:T(8,128)(2,1)S(1)}, bf16[32,2048]{1,0:T(8,128)(2,1)S(1)}, u32[]{:S(2)}, u32[]{:S(2)}) collective-permute-start(bf16[32,2048]{1,0:T(8,128)(2,1)S(1)} %collective-permute-done.1), channel_id=1, source_target_pairs={{0,32},{4,228},{8,40},{12,236},{16,48},{20,244},{24,56},{28,252},{... | collective-permute-start | bytes 393224 | tf_op jit(solution)/shard_map/ppermute | solution.py:52
  21.6 7.8 %collective-permute-start.8 = (bf16[512,256]{1,0:T(8,128)(2,1)S(1)}, bf16[512,256]{1,0:T(8,128)(2,1)S(1)}, u32[]{:S(2)}, u32[]{:S(2)}) collective-permute-start(bf16[512,256]{1,0:T(8,128)(2,1)S(1)} %slice.63), channel_id=1, source_target_pairs={{0,3},{1,2},{2,1},{3,0},{4,7},{5,6},{6,5},{7,4},{8,11},{9,10},{10,... | collective-permute-start | bytes 786440 | tf_op jit(solution)/shard_map/ppermute | solution.py:48
  24.0 7.1 %collective-permute-start.7 = (bf16[512,256]{1,0:T(8,128)(2,1)S(1)}, bf16[512,256]{1,0:T(8,128)(2,1)S(1)}, u32[]{:S(2)}, u32[]{:S(2)}) collective-permute-start(bf16[512,256]{1,0:T(8,128)(2,1)S(1)} %slice.63), channel_id=1, source_target_pairs={{0,1},{1,0},{2,3},{3,2},{4,5},{5,4},{6,7},{7,6},{8,9},{9,8},{10,11... | collective-permute-start | bytes 786440 | tf_op jit(solution)/shard_map/ppermute | solution.py:48
  24.1 7.1 %collective-permute-start.6 = (bf16[32,2048]{1,0:T(8,128)(2,1)S(1)}, bf16[32,2048]{1,0:T(8,128)(2,1)S(1)}, u32[]{:S(2)}, u32[]{:S(2)}) collective-permute-start(bf16[32,2048]{1,0:T(8,128)(2,1)S(1)} %collective-permute-done.3), channel_id=1, source_target_pairs={{0,32},{4,228},{8,40},{12,236},{16,48},{20,244},{24,56},{28,252},{... | collective-permute-start | bytes 393224 | tf_op jit(solution)/shard_map/ppermute | solution.py:52
  26.9 23.7 %copy-start.9 = (s32[2]{0:T(128)S(1)}, s32[2]{0:T(128)}, u32[]{:S(2)}) copy-start(s32[2]{0:T(128)} %copy-done.8) | copy-start | bytes 28
  27.0 12.6 %collective-permute-start.11 = (bf16[128,3072]{1,0:T(8,128)(2,1)S(1)}, bf16[128,3072]{1,0:T(8,128)(2,1)S(1)}, u32[]{:S(2)}, u32[]{:S(2)}) collective-permute-start(bf16[128,3072]{1,0:T(8,128)(2,1)S(1)} %pad_maximum_fusion.refs_0_), channel_id=1, source_target_pairs={{0,32},{4,228},{8,40},{12,236},{16,48},{20,244},{24,56},{28,252},{... | collective-permute-start | bytes 2359304 | tf_op jit(solution)/shard_map/ppermute | solution.py:52
  31.2 8.4 %collective-permute-start.10 = (bf16[96,2048]{1,0:T(8,128)(2,1)S(1)}, bf16[96,2048]{1,0:T(8,128)(2,1)S(1)}, u32[]{:S(2)}, u32[]{:S(2)}) collective-permute-start(bf16[96,2048]{1,0:T(8,128)(2,1)S(1)} %constant_dynamic-update-slice_fusion.own_ref), channel_id=1, source_target_pairs={{0,4},{4,0},{8,12},{12,8},{16,20},{20,16},{24,28},{28,24},{32,36},... | collective-permute-start | bytes 1179656 | tf_op jit(solution)/shard_map/ppermute | solution.py:52
  32.4 7.2 %collective-permute-start.9 = (bf16[32,2048]{1,0:T(8,128)(2,1)S(1)}, bf16[32,2048]{1,0:T(8,128)(2,1)S(1)}, u32[]{:S(2)}, u32[]{:S(2)}) collective-permute-start(bf16[32,2048]{1,0:T(8,128)(2,1)S(1)} %collective-permute-done.6), channel_id=1, source_target_pairs={{0,32},{4,228},{8,40},{12,236},{16,48},{20,244},{24,56},{28,252},{... | collective-permute-start | bytes 393224 | tf_op jit(solution)/shard_map/ppermute | solution.py:52
  33.6 12.1 %collective-permute-start.16 = (bf16[512,256]{1,0:T(8,128)(2,1)S(1)}, bf16[512,256]{1,0:T(8,128)(2,1)S(1)}, u32[]{:S(2)}, u32[]{:S(2)}) collective-permute-start(bf16[512,256]{1,0:T(8,128)(2,1)S(1)} %collective-permute-done.8), channel_id=1, source_target_pairs={{0,1},{1,0},{2,3},{3,2},{4,5},{5,4},{6,7},{7,6},{8,9},{9,8},{10,11... | collective-permute-start | bytes 786440 | tf_op jit(solution)/shard_map/ppermute | solution.py:48
  39.7 13.8 %collective-permute-start.13 = (bf16[128,3072]{1,0:T(8,128)(2,1)S(1)}, bf16[128,3072]{1,0:T(8,128)(2,1)S(1)}, u32[]{:S(2)}, u32[]{:S(2)}) collective-permute-start(bf16[128,3072]{1,0:T(8,128)(2,1)S(1)} %collective-permute-done.11.refs_1_), channel_id=1, source_target_pairs={{0,4},{4,0},{8,12},{12,8},{16,20},{20,16},{24,28},{28,24},{32,36},... | collective-permute-start | bytes 2359304 | tf_op jit(solution)/shard_map/ppermute | solution.py:52
  42.2 12.1 %collective-permute-start.12 = (bf16[128,3072]{1,0:T(8,128)(2,1)S(1)}, bf16[128,3072]{1,0:T(8,128)(2,1)}, u32[]{:S(2)}, u32[]{:S(2)}) collective-permute-start(bf16[128,3072]{1,0:T(8,128)(2,1)S(1)} %collective-permute-done.11.refs_1_), channel_id=1, source_target_pairs={{0,32},{4,228},{8,40},{12,236},{16,48},{20,244},{24,56},{28,252},{... | collective-permute-start | bytes 2359304 | tf_op jit(solution)/shard_map/ppermute | solution.py:52
  43.0 7.3 %collective-permute-start.14 = (bf16[256,256]{1,0:T(8,128)(2,1)S(1)}, bf16[256,256]{1,0:T(8,128)(2,1)S(1)}, u32[]{:S(2)}, u32[]{:S(2)}) collective-permute-start(bf16[256,256]{1,0:T(8,128)(2,1)S(1)} %constant_dynamic-update-slice_fusion.3.refs_0_), channel_id=1, source_target_pairs={{0,8},{4,28},{8,16},{12,4},{16,24},{20,12},{24,0},{28,20},{32,40},... | collective-permute-start | bytes 393224 | tf_op jit(solution)/shard_map/ppermute | solution.py:52
  45.4 5.0 %collective-permute-start.15 = (bf16[256,128]{1,0:T(8,128)(2,1)S(1)}, bf16[256,128]{1,0:T(8,128)(2,1)S(1)}, u32[]{:S(2)}, u32[]{:S(2)}) collective-permute-start(bf16[256,128]{1,0:T(8,128)(2,1)S(1)} %slice_select_fusion.2), channel_id=1, source_target_pairs={{0,16},{4,20},{8,24},{12,28},{16,0},{20,4},{24,8},{28,12},{32,48},... | collective-permute-start | bytes 196616 | tf_op jit(solution)/shard_map/ppermute | solution.py:52
  50.4 2.7 %collective-permute-start.17 = (bf16[256,384]{1,0:T(8,128)(2,1)S(1)}, bf16[256,384]{1,0:T(8,128)(2,1)S(1)}, u32[]{:S(2)}, u32[]{:S(2)}) collective-permute-start(bf16[256,384]{1,0:T(8,128)(2,1)S(1)} %pad_maximum_fusion.3), channel_id=1, source_target_pairs={{0,4},{4,0},{8,12},{12,8},{16,20},{20,16},{24,28},{28,24},{32,36},... | collective-permute-start | bytes 589832 | tf_op jit(solution)/shard_map/ppermute | solution.py:52
  51.3 19.8 %collective-permute-start.19 = (bf16[256,2048]{1,0:T(8,128)(2,1)S(1)}, bf16[256,2048]{1,0:T(8,128)(2,1)S(1)}, u32[]{:S(2)}, u32[]{:S(2)}) collective-permute-start(bf16[256,2048]{1,0:T(8,128)(2,1)S(1)} %assemble.1.refs_0_), channel_id=1, source_target_pairs={{0,8},{4,28},{8,16},{12,4},{16,24},{20,12},{24,0},{28,20},{32,40},... | collective-permute-start | bytes 3145736 | tf_op jit(solution)/shard_map/ppermute | solution.py:52
  54.4 13.4 %collective-permute-start.23 = (bf16[128,3072]{1,0:T(8,128)(2,1)}, bf16[128,3072]{1,0:T(8,128)(2,1)}, u32[]{:S(2)}, u32[]{:S(2)}) collective-permute-start(bf16[128,3072]{1,0:T(8,128)(2,1)} %collective-permute-done.12.refs_2_), channel_id=1, source_target_pairs={{0,4},{4,0},{8,12},{12,8},{16,20},{20,16},{24,28},{28,24},{32,36},... | collective-permute-start | bytes 2359304 | tf_op jit(solution)/shard_map/ppermute | solution.py:52
  55.7 6.8 %collective-permute-start.22 = (bf16[256,256]{1,0:T(8,128)(2,1)S(1)}, bf16[256,256]{1,0:T(8,128)(2,1)}, u32[]{:S(2)}, u32[]{:S(2)}) collective-permute-start(bf16[256,256]{1,0:T(8,128)(2,1)S(1)} %broadcast_select_fusion.4), channel_id=1, source_target_pairs={{0,2},{1,3},{2,0},{3,1},{4,6},{5,7},{6,4},{7,5},{8,10},{9,11},{10,... | collective-permute-start | bytes 393224 | tf_op jit(solution)/shard_map/ppermute | solution.py:48
  58.5 12.6 %collective-permute-start.18 = (bf16[128,3072]{1,0:T(8,128)(2,1)}, bf16[128,3072]{1,0:T(8,128)(2,1)}, u32[]{:S(2)}, u32[]{:S(2)}) collective-permute-start(bf16[128,3072]{1,0:T(8,128)(2,1)} %collective-permute-done.12.refs_2_), channel_id=1, source_target_pairs={{0,32},{4,228},{8,40},{12,236},{16,48},{20,244},{24,56},{28,252},{... | collective-permute-start | bytes 2359304 | tf_op jit(solution)/shard_map/ppermute | solution.py:52
  59.5 6.7 %collective-permute-start.21 = (bf16[256,256]{1,0:T(8,128)(2,1)S(1)}, bf16[256,256]{1,0:T(8,128)(2,1)S(1)}, u32[]{:S(2)}, u32[]{:S(2)}) collective-permute-start(bf16[256,256]{1,0:T(8,128)(2,1)S(1)} %broadcast_select_fusion.4), channel_id=1, source_target_pairs={{0,3},{1,2},{2,1},{3,0},{4,7},{5,6},{6,5},{7,4},{8,11},{9,10},{10,... | collective-permute-start | bytes 393224 | tf_op jit(solution)/shard_map/ppermute | solution.py:48
  62.5 4.3 %collective-permute-start.20 = (bf16[256,256]{1,0:T(8,128)(2,1)S(1)}, bf16[256,256]{1,0:T(8,128)(2,1)S(1)}, u32[]{:S(2)}, u32[]{:S(2)}) collective-permute-start(bf16[256,256]{1,0:T(8,128)(2,1)S(1)} %broadcast_select_fusion.4), channel_id=1, source_target_pairs={{0,1},{1,0},{2,3},{3,2},{4,5},{5,4},{6,7},{7,6},{8,9},{9,8},{10,11... | collective-permute-start | bytes 393224 | tf_op jit(solution)/shard_map/ppermute | solution.py:48
  71.1 6.1 %collective-permute-start.26 = (bf16[256,512]{1,0:T(8,128)(2,1)S(1)}, bf16[256,512]{1,0:T(8,128)(2,1)S(1)}, u32[]{:S(2)}, u32[]{:S(2)}) collective-permute-start(bf16[256,512]{1,0:T(8,128)(2,1)S(1)} %pad_maximum_fusion.2), channel_id=1, source_target_pairs={{0,4},{4,0},{8,12},{12,8},{16,20},{20,16},{24,28},{28,24},{32,36},... | collective-permute-start | bytes 786440 | tf_op jit(solution)/shard_map/ppermute | solution.py:52
  73.9 7.9 %collective-permute-start.27 = (bf16[128,3072]{1,0:T(8,128)(2,1)}, bf16[128,3072]{1,0:T(8,128)(2,1)S(1)}, u32[]{:S(2)}, u32[]{:S(2)}) collective-permute-start(bf16[128,3072]{1,0:T(8,128)(2,1)} %collective-permute-done.18.refs_0_), channel_id=1, source_target_pairs={{0,4},{4,0},{8,12},{12,8},{16,20},{20,16},{24,28},{28,24},{32,36},... | collective-permute-start | bytes 2359304 | tf_op jit(solution)/shard_map/ppermute | solution.py:52
  74.0 9.9 %collective-permute-start.25 = (bf16[128,1536]{1,0:T(8,128)(2,1)S(1)}, bf16[128,1536]{1,0:T(8,128)(2,1)S(1)}, u32[]{:S(2)}, u32[]{:S(2)}) collective-permute-start(bf16[128,1536]{1,0:T(8,128)(2,1)S(1)} %slice_select_fusion.1), channel_id=1, source_target_pairs={{0,32},{4,228},{8,40},{12,236},{16,48},{20,244},{24,56},{28,252},{... | collective-permute-start | bytes 1179656 | tf_op jit(solution)/shard_map/ppermute | solution.py:52
  74.9 11.3 %collective-permute-start.28 = (bf16[256,2048]{1,0:T(8,128)(2,1)S(1)}, bf16[256,2048]{1,0:T(8,128)(2,1)S(1)}, u32[]{:S(2)}, u32[]{:S(2)}) collective-permute-start(bf16[256,2048]{1,0:T(8,128)(2,1)S(1)} %collective-permute-done.19.refs_1_), channel_id=1, source_target_pairs={{0,4},{4,0},{8,12},{12,8},{16,20},{20,16},{24,28},{28,24},{32,36},... | collective-permute-start | bytes 3145736 | tf_op jit(solution)/shard_map/ppermute | solution.py:52
  75.0 9.0 %collective-permute-start.24 = (bf16[256,1024]{1,0:T(8,128)(2,1)S(1)}, bf16[256,1024]{1,0:T(8,128)(2,1)S(1)}, u32[]{:S(2)}, u32[]{:S(2)}) collective-permute-start(bf16[256,1024]{1,0:T(8,128)(2,1)S(1)} %slice_select_fusion), channel_id=1, source_target_pairs={{0,8},{4,28},{8,16},{12,4},{16,24},{20,12},{24,0},{28,20},{32,40},... | collective-permute-start | bytes 1572872 | tf_op jit(solution)/shard_map/ppermute | solution.py:52
  84.0 4.3 %collective-permute-start.29 = (bf16[256,1024]{1,0:T(8,128)(2,1)S(1)}, bf16[256,1024]{1,0:T(8,128)(2,1)S(1)}, u32[]{:S(2)}, u32[]{:S(2)}) collective-permute-start(bf16[256,1024]{1,0:T(8,128)(2,1)S(1)} %collective-permute-done.24.z_mine), channel_id=1, source_target_pairs={{0,4},{4,0},{8,12},{12,8},{16,20},{20,16},{24,28},{28,24},{32,36},... | collective-permute-start | bytes 1572872 | tf_op jit(solution)/shard_map/ppermute | solution.py:52
  86.2 2.1 %collective-permute-start.30 = (bf16[128,1536]{1,0:T(8,128)(2,1)S(1)}, bf16[128,1536]{1,0:T(8,128)(2,1)S(1)}, u32[]{:S(2)}, u32[]{:S(2)}) collective-permute-start(bf16[128,1536]{1,0:T(8,128)(2,1)S(1)} %collective-permute-done.25.y_mine), channel_id=1, source_target_pairs={{0,4},{4,0},{8,12},{12,8},{16,20},{20,16},{24,28},{28,24},{32,36},... | collective-permute-start | bytes 1179656 | tf_op jit(solution)/shard_map/ppermute | solution.py:52
  (16 other events, 148.6 us)

commit v5 on v3

--- a/solution.py
+++ b/solution.py
@@ -282,25 +282,28 @@
     return 640 if width % 1280 == 0 else 512
 
 
-def select_kernel(spans, hot_ref, *refs):
-    blocks, (u0_ref, u1_ref) = refs[:-2], refs[-2:]
-    width = u0_ref.shape[1]
+def select_kernel(gap, gap_rows, hot_ref, *refs):
+    blocks, outs = refs[:-2], refs[-2:]
+    width = outs[0].shape[1]
     step = step_of(width)
     for at in range(0, width, step):
         cols = slice(at, at + step)
         parts = [block[:, cols] for block in blocks]
-        for which, out in ((0, u0_ref), (1, u1_ref)):
-            rows = slice(which * NB, (which + 1) * NB)
-            hot = jnp.concatenate([hot_ref[rows, a:b] for a, b in spans], axis=1)
-            out[:, cols] = dot(hot, list_rows(parts, which)).astype(BF16)
-
-
-def select(hot, blocks, spans):
+        for which, out in enumerate(outs):
+            rows = list_rows(parts[:gap], which)
+            if gap_rows:
+                none = jnp.zeros((gap_rows, step), BF16)
+                rows = jnp.concatenate([rows, none, list_rows(parts[gap:], which)], axis=0)
+            hot = hot_ref[which * NB : (which + 1) * NB, :]
+            out[:, cols] = dot(hot, rows).astype(BF16)
+
+
+def select(hot, blocks, gap=None, gap_rows=0):
     width = blocks[0].shape[1]
     shape = jax.ShapeDtypeStruct((NB, width), BF16)
-    slots = sum(b - a for a, b in spans)
-    return pl.pallas_call(
-        functools.partial(select_kernel, spans),
+    slots = ZN * YN * SLOTS - gap_rows
+    return pl.pallas_call(
+        functools.partial(select_kernel, gap, gap_rows),
         in_specs=[VMEM] * (1 + len(blocks)),
         out_specs=[VMEM, VMEM],
         out_shape=[shape, shape],
@@ -419,7 +422,7 @@
     w1, w2 = w[:, :NB], w[:, NB:]
     opposite = jnp.concatenate([jnp.where(even, v2, w2), jnp.where(even, w2, v2)], axis=1)
     k = ZN * SLOTS
-    entries = select(hot_z, [v0, v1, opposite, w1], [(i * k, (i + 1) * k) for i in range(4)])
+    entries = select(hot_z, [v0, v1, opposite, w1])
     y2, o1, *entries = both(send(y1, ALONG_Z), send(y1, PAIR), *entries)
     pan0, pan1 = panels(panel, near, far, across)
 
@@ -434,11 +437,10 @@
     left0, left1, lower, fin = factor(ids, pivots, uppers, pan0, pan1)
     p1, o3 = send(z1, PAIR), send(y3, PAIR)
     n = YN * SLOTS
-    spans = [(i * n, (i + 1) * n) for i in (0, 1, 2, 3, 5, 6, 7)]
-    uy = select(hot_y, [yf, y1, y2, y3, o3, o2, o1], spans)
+    uy = select(hot_y, [yf, y1, y2, y3, o3, o2, o1], 4, n)
     z2, y4, left0, *uy = both(send(half(z1), ALONG_Y), send(half(y3), ALONG_Z), left0, *uy)
     p2, o4 = send(z2, PAIR), send(y4, PAIR)
-    uz = select(after(hot_z, z2), [zf, z1, p1], [(0, k), (k, 2 * k), (3 * k, 4 * k)])
+    uz = select(after(hot_z, z2), [zf, z1, p1], 2, k)
     spans = ((2 * k, 3 * k), (4 * n, 5 * n))
     z_parts, y_parts = (*uz, z2, p2), (*uy, y4, o4)
     return update(

time: 95 us -> 95 us (level)
  no operation moved by 1% of the time
where the time goes in v5:
time: 95 us; the launch traced here: 94.7 us
  starting transfers between devices  42.4 us (45%)
  Pallas kernels  22.9 us (24%)
  waiting for transfers between devices  21.5 us (23%)
  other arithmetic  4.55 us (5%)
  local copies, waits for them, and re-layouts  2.7 us (3%)
    ppermute x25, starting transfers between devices, send(): return lax.ppermute(array, 'prow', pairs)  33.9 us
    ppermute x25, waiting for transfers between devices, send(): return lax.ppermute(array, 'prow', pairs)  12 us
    ppermute x6, waiting for transfers between devices, over(): return lax.ppermute(array, 'pcol', pairs)  9.45 us
    ppermute x6, starting transfers between devices, over(): return lax.ppermute(array, 'pcol', pairs)  8.44 us
    pallas_call x1, Pallas kernels, update(): pl.pallas_call(functools.partial(update_kernel, [slice(*span) for span in...  7.36 us
    pallas_call x3, Pallas kernels, select(): pl.pallas_call(functools.partial(select_kernel, gap, gap_rows), in_specs=...  5.01 us
    pallas_call x1, Pallas kernels, factor(): pl.pallas_call(factor_kernel, in_specs=[SMEM] + [VMEM] * 5, out_specs=[VM...  4.46 us
    pallas_call x1, Pallas kernels, pick(): pl.pallas_call(functools.partial(pick_kernel, chunk), in_specs=[SMEM, VME...  3.4 us
  transfers between devices with their start and end apart: 31, of which 9 were waited for; matrix products, arithmetic and copies ran while one was open for 6% of the time, Pallas kernels for 13%

profile of v5, /device:TPU:1, one launch (start us, length us, event | category | flops | bytes accessed | tf_op | source)
XLA Modules:
  0.0 94.7 jit_solution(10987750047361772143)
XLA Ops:
  0.8 3.4 %pick.1 = bf16[32,5120]{1,0:T(8,128)(2,1)S(1)} custom-call(s32[2]{0:T(128)S(1)} %pad_add_fusion.ids, s32[2,256]{1,0:T(2,128)S(1)} %copy-done.8, bf16[512,5120]{1,0:T(8,128)(2,1)} %a_ref.1), custom_call_target="tpu_custom_call" | custom-call | flops 167772160 | bytes 10485760 | tf_op jit(solution)/shard_map/pick/pallas_call | solution.py:165
  4.2 3.3 %collective-permute-start = (bf16[32,5120]{1,0:T(8,128)(2,1)S(1)}, bf16[32,5120]{1,0:T(8,128)(2,1)S(1)}, u32[]{:S(2)}, u32[]{:S(2)}) collective-permute-start(bf16[32,5120]{1,0:T(8,128)(2,1)S(1)} %pick.1), channel_id=1, source_target_pairs={{0,4},{4,0},{8,12},{12,8},{16,20},{20,16},{24,28},{28,24},{32,36},... | collective-permute-start | bytes 983048 | tf_op jit(solution)/shard_map/ppermute | solution.py:52
  7.5 1.3 %collective-permute-done = bf16[32,5120]{1,0:T(8,128)(2,1)S(1)} collective-permute-done((bf16[32,5120]{1,0:T(8,128)(2,1)S(1)}, bf16[32,5120]{1,0:T(8,128)(2,1)S(1)}, u32[]{:S(2)}, u32[]{:S(2)}) %collective-permute-start) | collective-permute-done | bytes 327712 | tf_op jit(solution)/shard_map/ppermute | solution.py:52
  8.9 1.1 %collective-permute-start.2 = (bf16[32,3072]{1,0:T(8,128)(2,1)S(1)}, bf16[32,3072]{1,0:T(8,128)(2,1)S(1)}, u32[]{:S(2)}, u32[]{:S(2)}) collective-permute-start(bf16[32,3072]{1,0:T(8,128)(2,1)S(1)} %slice.82), channel_id=1, source_target_pairs={{0,8},{4,28},{8,16},{12,4},{16,24},{20,12},{24,0},{28,20},{32,40},... | collective-permute-start | bytes 589832 | tf_op jit(solution)/shard_map/ppermute | solution.py:52
  10.0 5.7 %collective-permute-start.1 = (bf16[32,2048]{1,0:T(8,128)(2,1)S(1)}, bf16[32,2048]{1,0:T(8,128)(2,1)S(1)}, u32[]{:S(2)}, u32[]{:S(2)}) collective-permute-start(bf16[32,2048]{1,0:T(8,128)(2,1)S(1)} %slice.81.near_ref), channel_id=1, source_target_pairs={{0,32},{4,228},{8,40},{12,236},{16,48},{20,244},{24,56},{28,252},{... | collective-permute-start | bytes 393224 | tf_op jit(solution)/shard_map/ppermute | solution.py:52
  16.6 2.1 %maps.1 = (bf16[512,512]{1,0:T(8,128)(2,1)}, bf16[512,512]{1,0:T(8,128)(2,1)}) custom-call(s32[2]{0:T(128)} %copy-done.6, s32[2,256]{1,0:T(2,128)} %piv_ref.5), custom_call_target="tpu_custom_call" | custom-call | flops 1073741824 | bytes 4194304 | tf_op jit(solution)/shard_map/maps/pallas_call | solution.py:193
  19.4 2.1 %collective-permute-start.3 = (bf16[32,2048]{1,0:T(8,128)(2,1)S(1)}, bf16[32,2048]{1,0:T(8,128)(2,1)S(1)}, u32[]{:S(2)}, u32[]{:S(2)}) collective-permute-start(bf16[32,2048]{1,0:T(8,128)(2,1)S(1)} %collective-permute-done.1), channel_id=1, source_target_pairs={{0,32},{4,228},{8,40},{12,236},{16,48},{20,244},{24,56},{28,252},{... | collective-permute-start | bytes 393224 | tf_op jit(solution)/shard_map/ppermute | solution.py:52
  21.6 2.5 %collective-permute-start.8 = (bf16[512,256]{1,0:T(8,128)(2,1)S(1)}, bf16[512,256]{1,0:T(8,128)(2,1)S(1)}, u32[]{:S(2)}, u32[]{:S(2)}) collective-permute-start(bf16[512,256]{1,0:T(8,128)(2,1)S(1)} %slice.63), channel_id=1, source_target_pairs={{0,3},{1,2},{2,1},{3,0},{4,7},{5,6},{6,5},{7,4},{8,11},{9,10},{10,... | collective-permute-start | bytes 786440 | tf_op jit(solution)/shard_map/ppermute | solution.py:48
  24.1 2.8 %collective-permute-start.6 = (bf16[32,2048]{1,0:T(8,128)(2,1)S(1)}, bf16[32,2048]{1,0:T(8,128)(2,1)S(1)}, u32[]{:S(2)}, u32[]{:S(2)}) collective-permute-start(bf16[32,2048]{1,0:T(8,128)(2,1)S(1)} %collective-permute-done.3), channel_id=1, source_target_pairs={{0,32},{4,228},{8,40},{12,236},{16,48},{20,244},{24,56},{28,252},{... | collective-permute-start | bytes 393224 | tf_op jit(solution)/shard_map/ppermute | solution.py:52
  27.1 2.2 %collective-permute-done.8 = bf16[512,256]{1,0:T(8,128)(2,1)S(1)} collective-permute-done((bf16[512,256]{1,0:T(8,128)(2,1)S(1)}, bf16[512,256]{1,0:T(8,128)(2,1)S(1)}, u32[]{:S(2)}, u32[]{:S(2)}) %collective-permute-start.8) | collective-permute-done | bytes 262176 | tf_op jit(solution)/shard_map/ppermute | solution.py:48
  29.3 1.8 %collective-permute-done.7 = bf16[512,256]{1,0:T(8,128)(2,1)S(1)} collective-permute-done((bf16[512,256]{1,0:T(8,128)(2,1)S(1)}, bf16[512,256]{1,0:T(8,128)(2,1)S(1)}, u32[]{:S(2)}, u32[]{:S(2)}) %collective-permute-start.7) | collective-permute-done | bytes 262176 | tf_op jit(solution)/shard_map/ppermute | solution.py:48
  31.2 1.2 %collective-permute-start.10 = (bf16[96,2048]{1,0:T(8,128)(2,1)S(1)}, bf16[96,2048]{1,0:T(8,128)(2,1)S(1)}, u32[]{:S(2)}, u32[]{:S(2)}) collective-permute-start(bf16[96,2048]{1,0:T(8,128)(2,1)S(1)} %constant_dynamic-update-slice_fusion.own_ref), channel_id=1, source_target_pairs={{0,4},{4,0},{8,12},{12,8},{16,20},{20,16},{24,28},{28,24},{32,36},... | collective-permute-start | bytes 1179656 | tf_op jit(solution)/shard_map/ppermute | solution.py:52
  32.4 1.2 %collective-permute-start.9 = (bf16[32,2048]{1,0:T(8,128)(2,1)S(1)}, bf16[32,2048]{1,0:T(8,128)(2,1)S(1)}, u32[]{:S(2)}, u32[]{:S(2)}) collective-permute-start(bf16[32,2048]{1,0:T(8,128)(2,1)S(1)} %collective-permute-done.6), channel_id=1, source_target_pairs={{0,32},{4,228},{8,40},{12,236},{16,48},{20,244},{24,56},{28,252},{... | collective-permute-start | bytes 393224 | tf_op jit(solution)/shard_map/ppermute | solution.py:52
  34.3 5.3 %collective-permute-done.9.far_ref = bf16[32,2048]{1,0:T(8,128)(2,1)S(1)} collective-permute-done((bf16[32,2048]{1,0:T(8,128)(2,1)S(1)}, bf16[32,2048]{1,0:T(8,128)(2,1)S(1)}, u32[]{:S(2)}, u32[]{:S(2)}) %collective-permute-start.9) | collective-permute-done | bytes 131104 | tf_op jit(solution)/shard_map/ppermute | solution.py:52
  39.6 2.6 %collective-permute-start.13 = (bf16[128,3072]{1,0:T(8,128)(2,1)S(1)}, bf16[128,3072]{1,0:T(8,128)(2,1)S(1)}, u32[]{:S(2)}, u32[]{:S(2)}) collective-permute-start(bf16[128,3072]{1,0:T(8,128)(2,1)S(1)} %collective-permute-done.11.refs_1_), channel_id=1, source_target_pairs={{0,4},{4,0},{8,12},{12,8},{16,20},{20,16},{24,28},{28,24},{32,36},... | collective-permute-start | bytes 2359304 | tf_op jit(solution)/shard_map/ppermute | solution.py:52
  43.0 2.4 %collective-permute-start.14 = (bf16[256,256]{1,0:T(8,128)(2,1)S(1)}, bf16[256,256]{1,0:T(8,128)(2,1)S(1)}, u32[]{:S(2)}, u32[]{:S(2)}) collective-permute-start(bf16[256,256]{1,0:T(8,128)(2,1)S(1)} %constant_dynamic-update-slice_fusion.3.refs_0_), channel_id=1, source_target_pairs={{0,8},{4,28},{8,16},{12,4},{16,24},{20,12},{24,0},{28,20},{32,40},... | collective-permute-start | bytes 393224 | tf_op jit(solution)/shard_map/ppermute | solution.py:52
  45.7 4.7 %collective-permute-done.15 = bf16[256,128]{1,0:T(8,128)(2,1)S(1)} collective-permute-done((bf16[256,128]{1,0:T(8,128)(2,1)S(1)}, bf16[256,128]{1,0:T(8,128)(2,1)S(1)}, u32[]{:S(2)}, u32[]{:S(2)}) %collective-permute-start.15) | collective-permute-done | bytes 65568 | tf_op jit(solution)/shard_map/ppermute | solution.py:52
  51.3 1.8 %collective-permute-start.19 = (bf16[256,2048]{1,0:T(8,128)(2,1)S(1)}, bf16[256,2048]{1,0:T(8,128)(2,1)S(1)}, u32[]{:S(2)}, u32[]{:S(2)}) collective-permute-start(bf16[256,2048]{1,0:T(8,128)(2,1)S(1)} %assemble.1.refs_0_), channel_id=1, source_target_pairs={{0,8},{4,28},{8,16},{12,4},{16,24},{20,12},{24,0},{28,20},{32,40},... | collective-permute-start | bytes 3145736 | tf_op jit(solution)/shard_map/ppermute | solution.py:52
  54.4 1.3 %collective-permute-start.20 = (bf16[128,3072]{1,0:T(8,128)(2,1)}, bf16[128,3072]{1,0:T(8,128)(2,1)}, u32[]{:S(2)}, u32[]{:S(2)}) collective-permute-start(bf16[128,3072]{1,0:T(8,128)(2,1)} %collective-permute-done.12.refs_2_), channel_id=1, source_target_pairs={{0,4},{4,0},{8,12},{12,8},{16,20},{20,16},{24,28},{28,24},{32,36},... | collective-permute-start | bytes 2359304 | tf_op jit(solution)/shard_map/ppermute | solution.py:52
  57.3 2.7 %collective-permute-start.23 = (bf16[256,256]{1,0:T(8,128)(2,1)}, bf16[256,256]{1,0:T(8,128)(2,1)S(1)}, u32[]{:S(2)}, u32[]{:S(2)}) collective-permute-start(bf16[256,256]{1,0:T(8,128)(2,1)} %broadcast_select_fusion.4), channel_id=1, source_target_pairs={{0,2},{1,3},{2,0},{3,1},{4,6},{5,7},{6,4},{7,5},{8,10},{9,11},{10,... | collective-permute-start | bytes 393224 | tf_op jit(solution)/shard_map/ppermute | solution.py:48
  60.9 2.9 %collective-permute-done.23 = bf16[256,256]{1,0:T(8,128)(2,1)S(1)} collective-permute-done((bf16[256,256]{1,0:T(8,128)(2,1)}, bf16[256,256]{1,0:T(8,128)(2,1)S(1)}, u32[]{:S(2)}, u32[]{:S(2)}) %collective-permute-start.23) | collective-permute-done | bytes 131104 | tf_op jit(solution)/shard_map/ppermute | solution.py:48
  63.8 1.6 %collective-permute-start.21 = (bf16[256,256]{1,0:T(8,128)(2,1)}, bf16[256,256]{1,0:T(8,128)(2,1)S(1)}, u32[]{:S(2)}, u32[]{:S(2)}) collective-permute-start(bf16[256,256]{1,0:T(8,128)(2,1)} %broadcast_select_fusion.4), channel_id=1, source_target_pairs={{0,1},{1,0},{2,3},{3,2},{4,5},{5,4},{6,7},{7,6},{8,9},{9,8},{10,11... | collective-permute-start | bytes 393224 | tf_op jit(solution)/shard_map/ppermute | solution.py:48
  65.4 1.2 %select_select_fusion = (bf16[512,256]{1,0:T(8,128)(2,1)S(1)}, bf16[512,256]{1,0:T(8,128)(2,1)S(1)}) fusion(bf16[512,256]{1,0:T(8,128)(2,1)} %copy-done.10, bf16[512,256]{1,0:T(8,128)(2,1)} %copy-done.12, bf16[512,256]{1,0:T(8,128)(2,1)} %copy-done.11, bf16[512,256]{1,0:T(8,128)(2,1)} %copy-done.13, pred[]{:T(512)S(6)} %eq.29, pred[]{:T(512)S(6)} %eq.14, ...), kind=kLoop, calls=%fused_computation.8 | loop fusion | flops 786432 | bytes 1572868 | tf_op jit(solution)/shard_map/jit(_where)/select_n | solution.py:388
  67.0 2.2 %collective-permute-done.21 = bf16[256,256]{1,0:T(8,128)(2,1)S(1)} collective-permute-done((bf16[256,256]{1,0:T(8,128)(2,1)}, bf16[256,256]{1,0:T(8,128)(2,1)S(1)}, u32[]{:S(2)}, u32[]{:S(2)}) %collective-permute-start.21) | collective-permute-done | bytes 131104 | tf_op jit(solution)/shard_map/ppermute | solution.py:48
  69.2 1.0 %select_select_fusion.3 = (bf16[256,256]{1,0:T(8,128)(2,1)S(1)}, bf16[256,256]{1,0:T(8,128)(2,1)S(1)}) fusion(bf16[256,256]{1,0:T(8,128)(2,1)} %broadcast_select_fusion.4, bf16[256,256]{1,0:T(8,128)(2,1)S(1)} %collective-permute-done.21, bf16[256,256]{1,0:T(8,128)(2,1)S(1)} %collective-permute-done.22, bf16[256,256]{1,0:T(8,128)(2,1)} %copy-done.14, ...), kind=kLoop, calls=%fused_computation.17 | loop fusion | flops 393216 | bytes 786436 | tf_op jit(solution)/shard_map/jit(_where)/select_n | solution.py:387
  71.3 1.2 %slice_select_fusion.1 = bf16[128,1536]{1,0:T(8,128)(2,1)S(1)} fusion(bf16[128,3072]{1,0:T(8,128)(2,1)} %collective-permute-done.18.refs_3_, pred[]{:T(512)S(6)} %eq.12), kind=kLoop, calls=%fused_computation.4 | loop fusion | flops 196608 | bytes 1179649 | tf_op jit(solution)/shard_map/jit(_where)/select_n | solution.py:393
  72.5 1.2 %collective-permute-start.25 = (bf16[128,1536]{1,0:T(8,128)(2,1)S(1)}, bf16[128,1536]{1,0:T(8,128)(2,1)S(1)}, u32[]{:S(2)}, u32[]{:S(2)}) collective-permute-start(bf16[128,1536]{1,0:T(8,128)(2,1)S(1)} %slice_select_fusion.1), channel_id=1, source_target_pairs={{0,32},{4,228},{8,40},{12,236},{16,48},{20,244},{24,56},{28,252},{... | collective-permute-start | bytes 1179656 | tf_op jit(solution)/shard_map/ppermute | solution.py:52
  73.9 2.5 %collective-permute-start.24 = (bf16[256,1024]{1,0:T(8,128)(2,1)S(1)}, bf16[256,1024]{1,0:T(8,128)(2,1)S(1)}, u32[]{:S(2)}, u32[]{:S(2)}) collective-permute-start(bf16[256,1024]{1,0:T(8,128)(2,1)S(1)} %slice_select_fusion), channel_id=1, source_target_pairs={{0,8},{4,28},{8,16},{12,4},{16,24},{20,12},{24,0},{28,20},{32,40},... | collective-permute-start | bytes 1572872 | tf_op jit(solution)/shard_map/ppermute | solution.py:52
  76.6 4.5 %factor.1 = (bf16[512,256]{1,0:T(8,128)(2,1)S(1)}, bf16[512,256]{1,0:T(8,128)(2,1)S(1)}, bf16[256,256]{1,0:T(8,128)(2,1)S(1)}, bf16[512,256]{1,0:T(8,128)(2,1)S(1)}) custom-call(s32[2]{0:T(128)S(1)} %copy-done.7, s32[2,256]{1,0:T(2,128)S(1)} %copy-done.9, bf16[512,256]{1,0:T(8,128)(2,1)S(1)} %get-tuple-element.100.s0_ref, ...), custom_call_target="tpu_custom_call" | custom-call | flops 6442450944 | bytes 4194304 | tf_op jit(solution)/shard_map/factor/pallas_call | solution.py:244
  81.1 3.5 %select.6 = (bf16[256,3072]{1,0:T(8,128)(2,1)S(1)}, bf16[256,3072]{1,0:T(8,128)(2,1)S(1)}) custom-call(bf16[512,512]{1,0:T(8,128)(2,1)S(1)} %copy-done.1, bf16[128,3072]{1,0:T(8,128)(2,1)S(1)} %pad_maximum_fusion.refs_0_, bf16[128,3072]{1,0:T(8,128)(2,1)S(1)} %copy-done.3, bf16[128,3072]{1,0:T(8,128)(2,1)} %collective-permute-done.12.refs_2_, ...), custom_call_target="tpu_custom_call" | custom-call | flops 1409286144 | bytes 1048576 | tf_op jit(solution)/shard_map/select/pallas_call | solution.py:305
  85.2 1.3 %select.7 = (bf16[256,2048]{1,0:T(8,128)(2,1)S(1)}, bf16[256,2048]{1,0:T(8,128)(2,1)S(1)}) custom-call(bf16[512,512]{1,0:T(8,128)(2,1)S(1)} %copy-done, bf16[256,2048]{1,0:T(8,128)(2,1)S(1)} %assemble.1.refs_0_, bf16[256,2048]{1,0:T(8,128)(2,1)S(1)} %collective-permute-done.19.refs_1_, bf16[256,2048]{1,0:T(8,128)(2,1)S(1)} %collective-permute-done.28.refs_2_), custom_call_target="tpu_custom_call" | custom-call | flops 805306368 | bytes 1048576 | tf_op jit(solution)/shard_map/select/pallas_call | solution.py:305
  87.2 7.4 %update.1 = bf16[512,5120]{1,0:T(8,128)(2,1)} custom-call(s32[2]{0:T(128)S(1)} %copy-done.7, bf16[512,512]{1,0:T(8,128)(2,1)S(1)} %copy-done, bf16[512,512]{1,0:T(8,128)(2,1)S(1)} %copy-done.1, bf16[256,2048]{1,0:T(8,128)(2,1)S(1)} %get-tuple-element.86.uz0, bf16[256,2048]{1,0:T(8,128)(2,1)S(1)} %get-tuple-element.87.uz1, ...), custom_call_target="tpu_custom_call" | custom-call | flops 4026531840 | bytes 10485760 | tf_op jit(solution)/shard_map/update/pallas_call | solution.py:363
  (102 shorter events, 12.2 us)
Async XLA Ops:
  4.2 4.6 %collective-permute-start = (bf16[32,5120]{1,0:T(8,128)(2,1)S(1)}, bf16[32,5120]{1,0:T(8,128)(2,1)S(1)}, u32[]{:S(2)}, u32[]{:S(2)}) collective-permute-start(bf16[32,5120]{1,0:T(8,128)(2,1)S(1)} %pick.1), channel_id=1, source_target_pairs={{0,4},{4,0},{8,12},{12,8},{16,20},{20,16},{24,28},{28,24},{32,36},... | collective-permute-start | bytes 983048 | tf_op jit(solution)/shard_map/ppermute | solution.py:52
  8.9 9.8 %collective-permute-start.2 = (bf16[32,3072]{1,0:T(8,128)(2,1)S(1)}, bf16[32,3072]{1,0:T(8,128)(2,1)S(1)}, u32[]{:S(2)}, u32[]{:S(2)}) collective-permute-start(bf16[32,3072]{1,0:T(8,128)(2,1)S(1)} %slice.82), channel_id=1, source_target_pairs={{0,8},{4,28},{8,16},{12,4},{16,24},{20,12},{24,0},{28,20},{32,40},... | collective-permute-start | bytes 589832 | tf_op jit(solution)/shard_map/ppermute | solution.py:52
  10.0 8.7 %collective-permute-start.1 = (bf16[32,2048]{1,0:T(8,128)(2,1)S(1)}, bf16[32,2048]{1,0:T(8,128)(2,1)S(1)}, u32[]{:S(2)}, u32[]{:S(2)}) collective-permute-start(bf16[32,2048]{1,0:T(8,128)(2,1)S(1)} %slice.81.near_ref), channel_id=1, source_target_pairs={{0,32},{4,228},{8,40},{12,236},{16,48},{20,244},{24,56},{28,252},{... | collective-permute-start | bytes 393224 | tf_op jit(solution)/shard_map/ppermute | solution.py:52
  18.7 5.4 %collective-permute-start.5 = (bf16[32,3072]{1,0:T(8,128)(2,1)S(1)}, bf16[32,3072]{1,0:T(8,128)(2,1)S(1)}, u32[]{:S(2)}, u32[]{:S(2)}) collective-permute-start(bf16[32,3072]{1,0:T(8,128)(2,1)S(1)} %collective-permute-done.2), channel_id=1, source_target_pairs={{0,4},{4,0},{8,12},{12,8},{16,20},{20,16},{24,28},{28,24},{32,36},... | collective-permute-start | bytes 589832 | tf_op jit(solution)/shard_map/ppermute | solution.py:52
  18.8 5.3 %collective-permute-start.4 = (bf16[32,3072]{1,0:T(8,128)(2,1)S(1)}, bf16[32,3072]{1,0:T(8,128)(2,1)S(1)}, u32[]{:S(2)}, u32[]{:S(2)}) collective-permute-start(bf16[32,3072]{1,0:T(8,128)(2,1)S(1)} %collective-permute-done.2), channel_id=1, source_target_pairs={{0,8},{4,28},{8,16},{12,4},{16,24},{20,12},{24,0},{28,20},{32,40},... | collective-permute-start | bytes 589832 | tf_op jit(solution)/shard_map/ppermute | solution.py:52
  19.4 4.6 %collective-permute-start.3 = (bf16[32,2048]{1,0:T(8,128)(2,1)S(1)}, bf16[32,2048]{1,0:T(8,128)(2,1)S(1)}, u32[]{:S(2)}, u32[]{:S(2)}) collective-permute-start(bf16[32,2048]{1,0:T(8,128)(2,1)S(1)} %collective-permute-done.1), channel_id=1, source_target_pairs={{0,32},{4,228},{8,40},{12,236},{16,48},{20,244},{24,56},{28,252},{... | collective-permute-start | bytes 393224 | tf_op jit(solution)/shard_map/ppermute | solution.py:52
  21.6 7.8 %collective-permute-start.8 = (bf16[512,256]{1,0:T(8,128)(2,1)S(1)}, bf16[512,256]{1,0:T(8,128)(2,1)S(1)}, u32[]{:S(2)}, u32[]{:S(2)}) collective-permute-start(bf16[512,256]{1,0:T(8,128)(2,1)S(1)} %slice.63), channel_id=1, source_target_pairs={{0,3},{1,2},{2,1},{3,0},{4,7},{5,6},{6,5},{7,4},{8,11},{9,10},{10,... | collective-permute-start | bytes 786440 | tf_op jit(solution)/shard_map/ppermute | solution.py:48
  24.0 7.1 %collective-permute-start.7 = (bf16[512,256]{1,0:T(8,128)(2,1)S(1)}, bf16[512,256]{1,0:T(8,128)(2,1)S(1)}, u32[]{:S(2)}, u32[]{:S(2)}) collective-permute-start(bf16[512,256]{1,0:T(8,128)(2,1)S(1)} %slice.63), channel_id=1, source_target_pairs={{0,1},{1,0},{2,3},{3,2},{4,5},{5,4},{6,7},{7,6},{8,9},{9,8},{10,11... | collective-permute-start | bytes 786440 | tf_op jit(solution)/shard_map/ppermute | solution.py:48
  24.1 7.1 %collective-permute-start.6 = (bf16[32,2048]{1,0:T(8,128)(2,1)S(1)}, bf16[32,2048]{1,0:T(8,128)(2,1)S(1)}, u32[]{:S(2)}, u32[]{:S(2)}) collective-permute-start(bf16[32,2048]{1,0:T(8,128)(2,1)S(1)} %collective-permute-done.3), channel_id=1, source_target_pairs={{0,32},{4,228},{8,40},{12,236},{16,48},{20,244},{24,56},{28,252},{... | collective-permute-start | bytes 393224 | tf_op jit(solution)/shard_map/ppermute | solution.py:52
  26.9 23.8 %copy-start.7 = (s32[2]{0:T(128)S(1)}, s32[2]{0:T(128)}, u32[]{:S(2)}) copy-start(s32[2]{0:T(128)} %copy-done.6) | copy-start | bytes 28
  27.0 12.6 %collective-permute-start.11 = (bf16[128,3072]{1,0:T(8,128)(2,1)S(1)}, bf16[128,3072]{1,0:T(8,128)(2,1)S(1)}, u32[]{:S(2)}, u32[]{:S(2)}) collective-permute-start(bf16[128,3072]{1,0:T(8,128)(2,1)S(1)} %pad_maximum_fusion.refs_0_), channel_id=1, source_target_pairs={{0,32},{4,228},{8,40},{12,236},{16,48},{20,244},{24,56},{28,252},{... | collective-permute-start | bytes 2359304 | tf_op jit(solution)/shard_map/ppermute | solution.py:52
  31.2 8.4 %collective-permute-start.10 = (bf16[96,2048]{1,0:T(8,128)(2,1)S(1)}, bf16[96,2048]{1,0:T(8,128)(2,1)S(1)}, u32[]{:S(2)}, u32[]{:S(2)}) collective-permute-start(bf16[96,2048]{1,0:T(8,128)(2,1)S(1)} %constant_dynamic-update-slice_fusion.own_ref), channel_id=1, source_target_pairs={{0,4},{4,0},{8,12},{12,8},{16,20},{20,16},{24,28},{28,24},{32,36},... | collective-permute-start | bytes 1179656 | tf_op jit(solution)/shard_map/ppermute | solution.py:52
  32.4 7.2 %collective-permute-start.9 = (bf16[32,2048]{1,0:T(8,128)(2,1)S(1)}, bf16[32,2048]{1,0:T(8,128)(2,1)S(1)}, u32[]{:S(2)}, u32[]{:S(2)}) collective-permute-start(bf16[32,2048]{1,0:T(8,128)(2,1)S(1)} %collective-permute-done.6), channel_id=1, source_target_pairs={{0,32},{4,228},{8,40},{12,236},{16,48},{20,244},{24,56},{28,252},{... | collective-permute-start | bytes 393224 | tf_op jit(solution)/shard_map/ppermute | solution.py:52
  33.6 12.1 %collective-permute-start.16 = (bf16[512,256]{1,0:T(8,128)(2,1)S(1)}, bf16[512,256]{1,0:T(8,128)(2,1)S(1)}, u32[]{:S(2)}, u32[]{:S(2)}) collective-permute-start(bf16[512,256]{1,0:T(8,128)(2,1)S(1)} %collective-permute-done.8), channel_id=1, source_target_pairs={{0,1},{1,0},{2,3},{3,2},{4,5},{5,4},{6,7},{7,6},{8,9},{9,8},{10,11... | collective-permute-start | bytes 786440 | tf_op jit(solution)/shard_map/ppermute | solution.py:48
  39.6 13.8 %collective-permute-start.13 = (bf16[128,3072]{1,0:T(8,128)(2,1)S(1)}, bf16[128,3072]{1,0:T(8,128)(2,1)S(1)}, u32[]{:S(2)}, u32[]{:S(2)}) collective-permute-start(bf16[128,3072]{1,0:T(8,128)(2,1)S(1)} %collective-permute-done.11.refs_1_), channel_id=1, source_target_pairs={{0,4},{4,0},{8,12},{12,8},{16,20},{20,16},{24,28},{28,24},{32,36},... | collective-permute-start | bytes 2359304 | tf_op jit(solution)/shard_map/ppermute | solution.py:52
  42.3 12.1 %collective-permute-start.12 = (bf16[128,3072]{1,0:T(8,128)(2,1)S(1)}, bf16[128,3072]{1,0:T(8,128)(2,1)}, u32[]{:S(2)}, u32[]{:S(2)}) collective-permute-start(bf16[128,3072]{1,0:T(8,128)(2,1)S(1)} %collective-permute-done.11.refs_1_), channel_id=1, source_target_pairs={{0,32},{4,228},{8,40},{12,236},{16,48},{20,244},{24,56},{28,252},{... | collective-permute-start | bytes 2359304 | tf_op jit(solution)/shard_map/ppermute | solution.py:52
  43.0 7.4 %collective-permute-start.14 = (bf16[256,256]{1,0:T(8,128)(2,1)S(1)}, bf16[256,256]{1,0:T(8,128)(2,1)S(1)}, u32[]{:S(2)}, u32[]{:S(2)}) collective-permute-start(bf16[256,256]{1,0:T(8,128)(2,1)S(1)} %constant_dynamic-update-slice_fusion.3.refs_0_), channel_id=1, source_target_pairs={{0,8},{4,28},{8,16},{12,4},{16,24},{20,12},{24,0},{28,20},{32,40},... | collective-permute-start | bytes 393224 | tf_op jit(solution)/shard_map/ppermute | solution.py:52
  45.4 5.0 %collective-permute-start.15 = (bf16[256,128]{1,0:T(8,128)(2,1)S(1)}, bf16[256,128]{1,0:T(8,128)(2,1)S(1)}, u32[]{:S(2)}, u32[]{:S(2)}) collective-permute-start(bf16[256,128]{1,0:T(8,128)(2,1)S(1)} %slice_select_fusion.2), channel_id=1, source_target_pairs={{0,16},{4,20},{8,24},{12,28},{16,0},{20,4},{24,8},{28,12},{32,48},... | collective-permute-start | bytes 196616 | tf_op jit(solution)/shard_map/ppermute | solution.py:52
  50.4 2.7 %collective-permute-start.17 = (bf16[256,384]{1,0:T(8,128)(2,1)S(1)}, bf16[256,384]{1,0:T(8,128)(2,1)S(1)}, u32[]{:S(2)}, u32[]{:S(2)}) collective-permute-start(bf16[256,384]{1,0:T(8,128)(2,1)S(1)} %pad_maximum_fusion.3), channel_id=1, source_target_pairs={{0,4},{4,0},{8,12},{12,8},{16,20},{20,16},{24,28},{28,24},{32,36},... | collective-permute-start | bytes 589832 | tf_op jit(solution)/shard_map/ppermute | solution.py:52
  51.3 18.9 %collective-permute-start.19 = (bf16[256,2048]{1,0:T(8,128)(2,1)S(1)}, bf16[256,2048]{1,0:T(8,128)(2,1)S(1)}, u32[]{:S(2)}, u32[]{:S(2)}) collective-permute-start(bf16[256,2048]{1,0:T(8,128)(2,1)S(1)} %assemble.1.refs_0_), channel_id=1, source_target_pairs={{0,8},{4,28},{8,16},{12,4},{16,24},{20,12},{24,0},{28,20},{32,40},... | collective-permute-start | bytes 3145736 | tf_op jit(solution)/shard_map/ppermute | solution.py:52
  54.4 15.9 %collective-permute-start.20 = (bf16[128,3072]{1,0:T(8,128)(2,1)}, bf16[128,3072]{1,0:T(8,128)(2,1)}, u32[]{:S(2)}, u32[]{:S(2)}) collective-permute-start(bf16[128,3072]{1,0:T(8,128)(2,1)} %collective-permute-done.12.refs_2_), channel_id=1, source_target_pairs={{0,4},{4,0},{8,12},{12,8},{16,20},{20,16},{24,28},{28,24},{32,36},... | collective-permute-start | bytes 2359304 | tf_op jit(solution)/shard_map/ppermute | solution.py:52
  55.7 14.6 %collective-permute-start.18 = (bf16[128,3072]{1,0:T(8,128)(2,1)}, bf16[128,3072]{1,0:T(8,128)(2,1)}, u32[]{:S(2)}, u32[]{:S(2)}) collective-permute-start(bf16[128,3072]{1,0:T(8,128)(2,1)} %collective-permute-done.12.refs_2_), channel_id=1, source_target_pairs={{0,32},{4,228},{8,40},{12,236},{16,48},{20,244},{24,56},{28,252},{... | collective-permute-start | bytes 2359304 | tf_op jit(solution)/shard_map/ppermute | solution.py:52
  57.3 6.5 %collective-permute-start.23 = (bf16[256,256]{1,0:T(8,128)(2,1)}, bf16[256,256]{1,0:T(8,128)(2,1)S(1)}, u32[]{:S(2)}, u32[]{:S(2)}) collective-permute-start(bf16[256,256]{1,0:T(8,128)(2,1)} %broadcast_select_fusion.4), channel_id=1, source_target_pairs={{0,2},{1,3},{2,0},{3,1},{4,6},{5,7},{6,4},{7,5},{8,10},{9,11},{10,... | collective-permute-start | bytes 393224 | tf_op jit(solution)/shard_map/ppermute | solution.py:48
  60.1 6.9 %collective-permute-start.22 = (bf16[256,256]{1,0:T(8,128)(2,1)}, bf16[256,256]{1,0:T(8,128)(2,1)S(1)}, u32[]{:S(2)}, u32[]{:S(2)}) collective-permute-start(bf16[256,256]{1,0:T(8,128)(2,1)} %broadcast_select_fusion.4), channel_id=1, source_target_pairs={{0,3},{1,2},{2,1},{3,0},{4,7},{5,6},{6,5},{7,4},{8,11},{9,10},{10,... | collective-permute-start | bytes 393224 | tf_op jit(solution)/shard_map/ppermute | solution.py:48
  63.8 5.4 %collective-permute-start.21 = (bf16[256,256]{1,0:T(8,128)(2,1)}, bf16[256,256]{1,0:T(8,128)(2,1)S(1)}, u32[]{:S(2)}, u32[]{:S(2)}) collective-permute-start(bf16[256,256]{1,0:T(8,128)(2,1)} %broadcast_select_fusion.4), channel_id=1, source_target_pairs={{0,1},{1,0},{2,3},{3,2},{4,5},{5,4},{6,7},{7,6},{8,9},{9,8},{10,11... | collective-permute-start | bytes 393224 | tf_op jit(solution)/shard_map/ppermute | solution.py:48
  70.3 6.1 %collective-permute-start.26 = (bf16[256,512]{1,0:T(8,128)(2,1)S(1)}, bf16[256,512]{1,0:T(8,128)(2,1)S(1)}, u32[]{:S(2)}, u32[]{:S(2)}) collective-permute-start(bf16[256,512]{1,0:T(8,128)(2,1)S(1)} %pad_maximum_fusion.2), channel_id=1, source_target_pairs={{0,4},{4,0},{8,12},{12,8},{16,20},{20,16},{24,28},{28,24},{32,36},... | collective-permute-start | bytes 786440 | tf_op jit(solution)/shard_map/ppermute | solution.py:52
  72.4 8.6 %collective-permute-start.27 = (bf16[128,3072]{1,0:T(8,128)(2,1)}, bf16[128,3072]{1,0:T(8,128)(2,1)S(1)}, u32[]{:S(2)}, u32[]{:S(2)}) collective-permute-start(bf16[128,3072]{1,0:T(8,128)(2,1)} %collective-permute-done.18.refs_3_), channel_id=1, source_target_pairs={{0,4},{4,0},{8,12},{12,8},{16,20},{20,16},{24,28},{28,24},{32,36},... | collective-permute-start | bytes 2359304 | tf_op jit(solution)/shard_map/ppermute | solution.py:52
  72.5 12.0 %collective-permute-start.25 = (bf16[128,1536]{1,0:T(8,128)(2,1)S(1)}, bf16[128,1536]{1,0:T(8,128)(2,1)S(1)}, u32[]{:S(2)}, u32[]{:S(2)}) collective-permute-start(bf16[128,1536]{1,0:T(8,128)(2,1)S(1)} %slice_select_fusion.1), channel_id=1, source_target_pairs={{0,32},{4,228},{8,40},{12,236},{16,48},{20,244},{24,56},{28,252},{... | collective-permute-start | bytes 1179656 | tf_op jit(solution)/shard_map/ppermute | solution.py:52
  73.8 11.4 %collective-permute-start.28 = (bf16[256,2048]{1,0:T(8,128)(2,1)S(1)}, bf16[256,2048]{1,0:T(8,128)(2,1)S(1)}, u32[]{:S(2)}, u32[]{:S(2)}) collective-permute-start(bf16[256,2048]{1,0:T(8,128)(2,1)S(1)} %collective-permute-done.19.refs_1_), channel_id=1, source_target_pairs={{0,4},{4,0},{8,12},{12,8},{16,20},{20,16},{24,28},{28,24},{32,36},... | collective-permute-start | bytes 3145736 | tf_op jit(solution)/shard_map/ppermute | solution.py:52
  73.9 10.6 %collective-permute-start.24 = (bf16[256,1024]{1,0:T(8,128)(2,1)S(1)}, bf16[256,1024]{1,0:T(8,128)(2,1)S(1)}, u32[]{:S(2)}, u32[]{:S(2)}) collective-permute-start(bf16[256,1024]{1,0:T(8,128)(2,1)S(1)} %slice_select_fusion), channel_id=1, source_target_pairs={{0,8},{4,28},{8,16},{12,4},{16,24},{20,12},{24,0},{28,20},{32,40},... | collective-permute-start | bytes 1572872 | tf_op jit(solution)/shard_map/ppermute | solution.py:52
  84.6 2.6 %collective-permute-start.29 = (bf16[256,1024]{1,0:T(8,128)(2,1)S(1)}, bf16[256,1024]{1,0:T(8,128)(2,1)S(1)}, u32[]{:S(2)}, u32[]{:S(2)}) collective-permute-start(bf16[256,1024]{1,0:T(8,128)(2,1)S(1)} %collective-permute-done.24.z_mine), channel_id=1, source_target_pairs={{0,4},{4,0},{8,12},{12,8},{16,20},{20,16},{24,28},{28,24},{32,36},... | collective-permute-start | bytes 1572872 | tf_op jit(solution)/shard_map/ppermute | solution.py:52
  85.0 2.1 %collective-permute-start.30 = (bf16[128,1536]{1,0:T(8,128)(2,1)S(1)}, bf16[128,1536]{1,0:T(8,128)(2,1)S(1)}, u32[]{:S(2)}, u32[]{:S(2)}) collective-permute-start(bf16[128,1536]{1,0:T(8,128)(2,1)S(1)} %collective-permute-done.25.y_mine), channel_id=1, source_target_pairs={{0,4},{4,0},{8,12},{12,8},{16,20},{20,16},{24,28},{28,24},{32,36},... | collective-permute-start | bytes 1179656 | tf_op jit(solution)/shard_map/ppermute | solution.py:52
  (16 other events, 110.9 us)
